TPU v7x, 32 devices: a whole 2x2x4 slice. The times are simulated.
32 devices in a mesh: dp: 4 (over z), seq: 4 (over y, x), tensor: 2 (over core).
Axes of the slice: x: 2, y: 2, z: 4, core: 2. Of those that a mesh axis runs over, the one named last changes fastest.
Arguments:
- tokens: bfloat16 [2, 4, 1024, 1536], P(None, 'dp', 'seq'), may hold values from -6 to 6
- cotangent: bfloat16 [2, 4, 1024, 1536], P(None, 'dp', 'seq'), may hold values from -6 to 6
- norm_gain: float32 [2, 1536], replicated, may hold values from 0.1 to 1.9
- inner_weight: bfloat16 [2, 1536, 2, 3072], P(None, ('dp', 'seq'), None, 'tensor'), may hold values from -0.15625 to 0.15625
- rate_weight: bfloat16 [2, 1536, 48], P(None, ('dp', 'seq'), 'tensor'), may hold values from -0.15625 to 0.15625
- state_weight: bfloat16 [2, 1536, 256], P(None, ('dp', 'seq', 'tensor')), may hold values from -0.15625 to 0.15625
- conv_inner: float32 [2, 4, 3072], P(None, None, 'tensor'), may hold values from -3 to 3
- bias_inner: float32 [2, 3072], P(None, 'tensor'), may hold values from -0.5 to 0.5
- conv_state: float32 [2, 4, 256], replicated, may hold values from -3 to 3
- bias_state: float32 [2, 256], replicated, may hold values from -0.5 to 0.5
- rate_bias: float32 [2, 48], P(None, 'tensor'), may hold values from -8 to -3
- decay_log: float32 [2, 48], P(None, 'tensor'), may hold values from -1.5 to 0.5
- skip_gain: float32 [2, 48], P(None, 'tensor'), may hold values from 0.5 to 1.5
- gate_gain: float32 [2, 3072], P(None, 'tensor'), may hold values from 0.1 to 1.9
- out_weight: bfloat16 [2, 3072, 1536], P(None, 'tensor', ('dp', 'seq')), may hold values from -0.109375 to 0.109375
Outputs:
- output: float32 [2, 4, 1024, 1536], P(None, 'dp', 'seq')
- input_grad: float32 [2, 4, 1024, 1536], P(None, 'dp', 'seq')
- grad_norm_gain: float32 [2, 1536], replicated
- grad_inner_weight: float32 [2, 1536, 2, 3072], P(None, ('dp', 'seq'), None, 'tensor')
- grad_rate_weight: float32 [2, 1536, 48], P(None, ('dp', 'seq'), 'tensor')
- grad_state_weight: float32 [2, 1536, 256], P(None, ('dp', 'seq', 'tensor'))
- grad_conv_inner: float32 [2, 4, 3072], P(None, None, 'tensor')
- grad_bias_inner: float32 [2, 3072], P(None, 'tensor')
- grad_conv_state: float32 [2, 4, 256], replicated
- grad_bias_state: float32 [2, 256], replicated
- grad_rate_bias: float32 [2, 48], P(None, 'tensor')
- grad_decay_log: float32 [2, 48], P(None, 'tensor')
- grad_skip_gain: float32 [2, 48], P(None, 'tensor')
- grad_gate_gain: float32 [2, 3072], P(None, 'tensor')
- grad_out_weight: float32 [2, 3072, 1536], P(None, 'tensor', ('dp', 'seq'))
All inputs are finite; a program needn't handle non-finite values.
Results may differ from a plain program's by a relative error of at most 0.019.
Values may be sent and summed in bfloat16 or wider, within the bound.
No kernel may reach another device: no remote copies, remote signals or barrier semaphores. Data moves between devices by JAX's collectives and lax.ppermute only.
A program may use at most 512 MiB of HBM per device.

v0:
```python
import jax
import jax.numpy as jnp
from jax import lax
from jax.sharding import PartitionSpec as P

DI = 3072
STRETCH = 128


EPSILON = 1e-05
HIGHEST = lax.Precision.HIGHEST


def shifted(value, axis, steps):
    count = lax.axis_size(axis)
    leading, last = (max(0, -steps), min(count, count - steps))
    return lax.ppermute(value, axis, [(source, source + steps) for source in range(leading, last)])


def carried_in(array, axis, combine, identity):
    length, place = (lax.axis_size(axis), lax.axis_index(axis))
    everything = jax.tree.map(
        lambda part, kind: lax.all_gather(part.astype(kind), axis),
        array,
        (jnp.bfloat16, jnp.bfloat16),
    )
    start = jax.tree.map(
        lambda part, zero: jnp.broadcast_to(jnp.asarray(zero, part.dtype), part.shape),
        array,
        identity,
    )

    def turn(k, before):
        reached = k < place
        new = combine(
            before, jax.tree.map(lambda part, own: part[k].astype(own.dtype), everything, array)
        )
        return jax.tree.map(lambda a, b: jnp.where(reached, a, b), new, before)

    return lax.fori_loop(0, length, turn, start)


def carried_in_2(array, axis, join, neutral):
    count = lax.axis_size(axis)
    place = lax.axis_index(axis)
    ahead = count - 1 - place
    gathered = jax.tree.map(
        lambda a, kind: lax.all_gather(a.astype(kind), axis),
        array,
        jax.tree.map(lambda a: jnp.bfloat16 if a.dtype == jnp.float32 else a.dtype, array),
    )
    state = jax.tree.map(lambda a, e: jnp.zeros_like(a) + jnp.asarray(e, a.dtype), array, neutral)

    def one(turn, state):
        source = count - 1 - turn
        return join(
            state,
            jax.tree.map(
                lambda a, own: lax.dynamic_index_in_dim(a, source, 0, False).astype(own.dtype),
                gathered,
                array,
            ),
        )

    return lax.fori_loop(0, ahead, one, state)


def product(left_side, right_side):
    return jnp.dot(left_side, right_side, precision=HIGHEST, preferred_element_type=jnp.float32)


def conv_silu(padded, weight, conv_bias):
    conv_width = weight.shape[0]
    out_rows = padded.shape[0] - conv_width + 1
    summed = conv_bias[None, :] + weight[0][None, :] * padded[0:out_rows]
    for offset in range(1, conv_width):
        summed = summed + weight[offset][None, :] * padded[offset : offset + out_rows]
    return jax.nn.silu(summed)


def block_step(carry_state, pieces):
    inputs, keys_b, queries_c, step_rates, decays = pieces
    running = jnp.cumsum(decays, axis=0)
    block_len = inputs.shape[0]
    causal = jnp.arange(block_len)[:, None] >= jnp.arange(block_len)[None, :]
    spread = running.T[:, :, None] - running.T[:, None, :]
    weights = jnp.exp(jnp.where(causal[None, :, :], spread, -jnp.inf))
    scores = product(queries_c, keys_b.T)
    mixing = scores[None, :, :] * weights * step_rates.T[:, None, :]
    inside = jnp.einsum("hts,shp->thp", mixing, inputs, precision=HIGHEST)
    carried = (
        jnp.einsum("tn,hpn->thp", queries_c, carry_state, precision=HIGHEST)
        * jnp.exp(running)[:, :, None]
    )
    tail_weight = jnp.exp(running[-1][None, :] - running) * step_rates
    update = jnp.einsum("shp,sn->hpn", tail_weight[:, :, None] * inputs, keys_b, precision=HIGHEST)
    return (jnp.exp(running[-1])[:, None, None] * carry_state + update, inside + carried)


def state_step(carry_state, pieces):
    inputs, keys_b, step_rates, decays = pieces
    running = jnp.cumsum(decays, axis=0)
    tail_weight = jnp.exp(running[-1][None, :] - running) * step_rates
    update = jnp.einsum("shp,sn->hpn", tail_weight[:, :, None] * inputs, keys_b, precision=HIGHEST)
    return (jnp.exp(running[-1])[:, None, None] * carry_state + update, None)


def to_blocks(values):
    return values.reshape((values.shape[0] // STRETCH, STRETCH) + values.shape[1:])


def span_summary(inputs, keys_b, step_rates, decays):
    zero_state = jnp.zeros((inputs.shape[1], inputs.shape[2], keys_b.shape[1]), jnp.float32)
    end_state, _ = lax.scan(
        state_step,
        zero_state,
        (to_blocks(inputs), to_blocks(keys_b), to_blocks(step_rates), to_blocks(decays)),
    )
    return (jnp.exp(jnp.sum(decays, axis=0)), end_state)


def span_output(inputs, keys_b, queries_c, step_rates, decays, entry_state, skip_gain):
    _, block_out = lax.scan(
        block_step,
        entry_state,
        (
            to_blocks(inputs),
            to_blocks(keys_b),
            to_blocks(queries_c),
            to_blocks(step_rates),
            to_blocks(decays),
        ),
    )
    mixed_out = block_out.reshape(inputs.shape) + skip_gain[None, :, None] * inputs
    return mixed_out.reshape(inputs.shape[0], -1)


def rate_piece(rate_raw, rate_bias, decay_log):
    step_rates = jax.nn.softplus(rate_raw + rate_bias[None, :])
    return (step_rates, -jnp.exp(decay_log)[None, :] * step_rates)


def norm_piece(hidden, norm_gain):
    row_scale = lax.rsqrt(jnp.mean(hidden * hidden, axis=1, keepdims=True) + EPSILON)
    return hidden * row_scale * norm_gain[None, :]


def chain_combine(earlier, following):
    return (earlier[0] * following[0], following[1] + following[0][:, None, None] * earlier[1])


def gather_layer(inner_weight, rate_weight, state_weight, out_weight, layer_index):
    inner_full, rate_full, out_full = (
        lax.all_gather(inner_weight[layer_index], ("dp", "seq"), axis=0, tiled=True),
        lax.all_gather(rate_weight[layer_index], ("dp", "seq"), axis=0, tiled=True),
        lax.all_gather(out_weight[layer_index], ("dp", "seq"), axis=1, tiled=True),
    )
    state_full = lax.all_gather(
        state_weight[layer_index], ("dp", "seq", "tensor"), axis=0, tiled=True
    )
    return (inner_full.reshape(inner_full.shape[0], -1), rate_full, state_full, out_full)


def forward_layer(hidden, weights, small_params, layer_index):
    inner_full, rate_full, state_full, out_full = weights
    (
        norm_gain,
        conv_inner,
        bias_inner,
        conv_state,
        bias_state,
        rate_bias,
        decay_log,
        skip_gain,
        gate_gain,
    ) = small_params
    seq_rows = hidden.shape[0]
    normed_full, norm_pull = jax.vjp(norm_piece, hidden, norm_gain[layer_index])
    normed = normed_full.astype(jnp.bfloat16)
    gate_inner = jnp.dot(normed, inner_full, preferred_element_type=jnp.float32)
    rate_raw = jnp.dot(normed, rate_full, preferred_element_type=jnp.float32)
    state_raw = jnp.dot(normed, state_full, preferred_element_type=jnp.float32)
    local_width = gate_inner.shape[1] // 2
    gate_part = gate_inner[:, :local_width]
    conv_input = jnp.concatenate([gate_inner[:, local_width:], state_raw], axis=1).astype(
        jnp.bfloat16
    )
    edge_count = conv_inner.shape[1] - 1
    edge_rows = shifted(conv_input[seq_rows - edge_count :], "seq", 1)
    padded = jnp.concatenate([edge_rows, conv_input], axis=0).astype(jnp.float32)
    conv_weight = jnp.concatenate([conv_inner[layer_index], conv_state[layer_index]], axis=1)
    conv_bias = jnp.concatenate([bias_inner[layer_index], bias_state[layer_index]])
    activated, conv_pull = jax.vjp(conv_silu, padded, conv_weight, conv_bias)
    state_size = state_raw.shape[1] // 2
    head_count = rate_bias.shape[1]
    inputs = activated[:, :local_width].reshape(seq_rows, head_count, local_width // head_count)
    keys_b = activated[:, local_width : local_width + state_size]
    queries_c = activated[:, local_width + state_size :]
    (step_rates, decays), rate_pull = jax.vjp(
        rate_piece, rate_raw, rate_bias[layer_index], decay_log[layer_index]
    )
    (span_decay, span_state), summary_pull = jax.vjp(
        span_summary, inputs, keys_b, step_rates, decays
    )
    identity = (jnp.ones_like(span_decay), jnp.zeros_like(span_state))
    entry_state = carried_in((span_decay, span_state), "seq", chain_combine, identity)[1]
    mixed_out, output_pull = jax.vjp(
        span_output,
        inputs,
        keys_b,
        queries_c,
        step_rates,
        decays,
        entry_state,
        skip_gain[layer_index],
    )
    gate_silu, silu_pull = jax.vjp(jax.nn.silu, gate_part)
    gated_out = mixed_out * gate_silu
    square_sum = lax.psum(jnp.sum(gated_out * gated_out, axis=1), "tensor")
    gate_scale = lax.rsqrt(square_sum / DI + EPSILON)[:, None]
    normed_out = (gated_out * gate_scale * gate_gain[layer_index][None, :]).astype(jnp.bfloat16)
    partial_out = jnp.dot(normed_out, out_full, preferred_element_type=jnp.float32)
    new_hidden = hidden + lax.psum(partial_out, "tensor")
    kept_values = (
        norm_pull,
        normed,
        silu_pull,
        gate_silu,
        mixed_out,
        gated_out,
        gate_scale,
        normed_out,
        conv_pull,
        rate_pull,
        summary_pull,
        output_pull,
        span_decay,
        entry_state,
        identity,
        local_width,
        edge_count,
    )
    return (new_hidden, kept_values)


def backward_layer(grad_hidden, weights, small_params, kept_values, layer_index):
    inner_full, rate_full, state_full, out_full = weights
    gate_gain = small_params[8]
    (
        norm_pull,
        normed,
        silu_pull,
        gate_silu,
        mixed_out,
        gated_out,
        gate_scale,
        normed_out,
        conv_pull,
        rate_pull,
        summary_pull,
        output_pull,
        span_decay,
        entry_state,
        identity,
        local_width,
        edge_count,
    ) = kept_values
    seq_rows = normed.shape[0]
    grad_low = grad_hidden.astype(jnp.bfloat16)
    grad_out_weight = jnp.dot(normed_out.T, grad_low, preferred_element_type=jnp.float32)
    grad_normed_out = jnp.dot(grad_low, out_full.T, preferred_element_type=jnp.float32)
    grad_gate_gain = jnp.sum(grad_normed_out * gated_out * gate_scale, axis=0)
    scaled_grad = grad_normed_out * gate_gain[layer_index][None, :]
    inner_sum = lax.psum(jnp.sum(scaled_grad * gated_out, axis=1), "tensor")
    scale_cube = gate_scale * gate_scale * gate_scale
    grad_gated = gate_scale * scaled_grad - gated_out * scale_cube * (inner_sum[:, None] / DI)
    grad_mixed = grad_gated * gate_silu
    grad_gate = silu_pull(grad_gated * mixed_out)[0]
    grad_inputs, grad_keys, grad_queries, grad_rates, grad_decays, grad_entry, grad_skip_gain = (
        output_pull(grad_mixed)
    )
    end_grads = carried_in_2((span_decay, grad_entry), "seq", chain_combine, identity)[1]
    grad_span_decay = jnp.sum(end_grads * entry_state, axis=(1, 2))
    more_inputs, more_keys, more_rates, more_decays = summary_pull((grad_span_decay, end_grads))
    grad_raw, grad_rate_bias, grad_decay_log = rate_pull(
        (grad_rates + more_rates, grad_decays + more_decays)
    )
    grad_activated = jnp.concatenate(
        [(grad_inputs + more_inputs).reshape(seq_rows, -1), grad_keys + more_keys, grad_queries],
        axis=1,
    )
    grad_padded, grad_conv_weight, grad_conv_bias = conv_pull(grad_activated)
    edge_back = shifted(grad_padded[:edge_count], "seq", -1)
    grad_conv_input = grad_padded[edge_count:]
    grad_conv_input = jnp.concatenate(
        [
            grad_conv_input[: seq_rows - edge_count],
            grad_conv_input[seq_rows - edge_count :] + edge_back,
        ],
        axis=0,
    )
    grad_inner_low = jnp.concatenate([grad_gate, grad_conv_input[:, :local_width]], axis=1).astype(
        jnp.bfloat16
    )
    grad_state_raw = grad_conv_input[:, local_width:]
    grad_rate_low = grad_raw.astype(jnp.bfloat16)
    grad_inner_weight = jnp.dot(normed.T, grad_inner_low, preferred_element_type=jnp.float32)
    grad_rate_weight = jnp.dot(normed.T, grad_rate_low, preferred_element_type=jnp.float32)
    grad_state_weight = product(normed.astype(jnp.float32).T, grad_state_raw)
    grad_normed_part = (
        jnp.dot(grad_inner_low, inner_full.T, preferred_element_type=jnp.float32)
        + jnp.dot(grad_rate_low, rate_full.T, preferred_element_type=jnp.float32)
        + product(grad_state_raw, state_full.astype(jnp.float32).T)
    )
    grad_normed, grad_conv_state, grad_bias_state = (
        lax.psum(grad_normed_part.astype(jnp.bfloat16), "tensor").astype(jnp.float32),
        lax.psum(grad_conv_weight[:, local_width:].astype(jnp.bfloat16), "tensor").astype(
            jnp.float32
        ),
        lax.psum(grad_conv_bias[local_width:].astype(jnp.bfloat16), "tensor").astype(jnp.float32),
    )
    grad_hidden_norm, grad_norm_gain = norm_pull(grad_normed)
    layer_grads = (
        grad_inner_weight.reshape(grad_inner_weight.shape[0], 2, local_width),
        grad_rate_weight,
        grad_state_weight,
        grad_out_weight,
        grad_norm_gain,
        grad_conv_weight[:, :local_width],
        grad_conv_bias[:local_width],
        grad_conv_state,
        grad_bias_state,
        grad_rate_bias,
        grad_decay_log,
        grad_skip_gain,
        grad_gate_gain,
    )
    return (grad_hidden + grad_hidden_norm, layer_grads)


def stack_layers(layer_sums, position):
    return jnp.stack([grads_here[position] for grads_here in layer_sums])


def body(
    tokens,
    cotangent,
    norm_gain,
    inner_weight,
    rate_weight,
    state_weight,
    conv_inner,
    bias_inner,
    conv_state,
    bias_state,
    rate_bias,
    decay_log,
    skip_gain,
    gate_gain,
    out_weight,
):
    small_params = (
        norm_gain,
        conv_inner,
        bias_inner,
        conv_state,
        bias_state,
        rate_bias,
        decay_log,
        skip_gain,
        gate_gain,
    )
    layer_count = norm_gain.shape[0]
    batch_count = tokens.shape[0]
    results = []
    kept_batches = []
    for batch_index in range(batch_count):
        hidden = tokens[batch_index, 0].astype(jnp.float32)
        kept_layers = []
        for layer_index in range(layer_count):
            weights = gather_layer(inner_weight, rate_weight, state_weight, out_weight, layer_index)
            hidden, kept_values = forward_layer(hidden, weights, small_params, layer_index)
            kept_layers.append(kept_values)
        results.append(hidden)
        kept_batches.append(kept_layers)
    layer_sums = [None] * layer_count
    seq_grads = []
    for batch_index in range(batch_count):
        grad_hidden = cotangent[batch_index, 0].astype(jnp.float32)
        for layer_index in reversed(range(layer_count)):
            weights = gather_layer(inner_weight, rate_weight, state_weight, out_weight, layer_index)
            grad_hidden, layer_grads = backward_layer(
                grad_hidden,
                weights,
                small_params,
                kept_batches[batch_index][layer_index],
                layer_index,
            )
            if layer_sums[layer_index] is None:
                layer_sums[layer_index] = layer_grads
            else:
                layer_sums[layer_index] = tuple(
                    (older + newer for older, newer in zip(layer_sums[layer_index], layer_grads))
                )
        seq_grads.append(grad_hidden)
    shard_inner, shard_rate, shard_out = (
        lax.psum_scatter(
            stack_layers(layer_sums, 0), ("dp", "seq"), scatter_dimension=1, tiled=True
        ),
        lax.psum_scatter(
            stack_layers(layer_sums, 1), ("dp", "seq"), scatter_dimension=1, tiled=True
        ),
        lax.psum_scatter(
            stack_layers(layer_sums, 3), ("dp", "seq"), scatter_dimension=2, tiled=True
        ),
    )
    shard_state = lax.psum_scatter(
        stack_layers(layer_sums, 2), ("dp", "seq", "tensor"), scatter_dimension=1, tiled=True
    )
    summed_small = lax.psum(
        (
            stack_layers(layer_sums, 4),
            stack_layers(layer_sums, 5),
            stack_layers(layer_sums, 6),
            stack_layers(layer_sums, 7),
            stack_layers(layer_sums, 8),
            stack_layers(layer_sums, 9),
            stack_layers(layer_sums, 10),
            stack_layers(layer_sums, 11),
            stack_layers(layer_sums, 12),
        ),
        ("dp", "seq"),
    )
    output = jnp.stack(results)[:, None]
    input_grad = jnp.stack(seq_grads)[:, None]
    return (
        output,
        input_grad,
        summed_small[0],
        shard_inner,
        shard_rate,
        shard_state,
        summed_small[1],
        summed_small[2],
        summed_small[3],
        summed_small[4],
        summed_small[5],
        summed_small[6],
        summed_small[7],
        summed_small[8],
        shard_out,
    )


def solution(mesh):
    in_specs = (
        P(None, "dp", "seq", None),
        P(None, "dp", "seq", None),
        P(),
        P(None, ("dp", "seq"), None, "tensor"),
        P(None, ("dp", "seq"), "tensor"),
        P(None, ("dp", "seq", "tensor"), None),
        P(None, None, "tensor"),
        P(None, "tensor"),
        P(),
        P(),
        P(None, "tensor"),
        P(None, "tensor"),
        P(None, "tensor"),
        P(None, "tensor"),
        P(None, "tensor", ("dp", "seq")),
    )
    out_specs = (
        P(None, "dp", "seq", None),
        P(None, "dp", "seq", None),
        P(),
        P(None, ("dp", "seq"), None, "tensor"),
        P(None, ("dp", "seq"), "tensor"),
        P(None, ("dp", "seq", "tensor"), None),
        P(None, None, "tensor"),
        P(None, "tensor"),
        P(),
        P(),
        P(None, "tensor"),
        P(None, "tensor"),
        P(None, "tensor"),
        P(None, "tensor"),
        P(None, "tensor", ("dp", "seq")),
    )
    return jax.shard_map(body, mesh=mesh, in_specs=in_specs, out_specs=out_specs, check_vma=False)
```

profile of v0, /device:TPU:1, one launch (start us, length us, event | category | flops | bytes accessed | tf_op | source)
XLA Modules:
  0.0 3136.7 jit_solution(18337068367693772501)
XLA Ops:
  11.1 43.4 %all-gather = bf16[1,1536,24]{2,0,1:T(2,128)(2,1)S(1)} all-gather(bf16[1,96,24]{2,0,1:T(2,128)(2,1)S(1)} %copy.1161), channel_id=2, replica_groups=mesh['dp'=4,'seq'=4,'tensor'=2] {'dp','seq'}, dimensions={1}, use_global_device_ids=true | all-gather | bytes 78336 | tf_op jit(solution)/shard_map/all_gather | solution.py:155
  65.6 50.4 %all-gather.2 = bf16[1,1536,256]{2,1,0:T(8,128)(2,1)S(1)} all-gather(bf16[1,48,256]{2,1,0:T(8,128)(2,1)S(1)} %get-tuple-element.9088), channel_id=4, replica_groups=mesh['dp'=4,'seq'=4,'tensor'=2] {'dp','seq','tensor'}, dimensions={1}, use_global_device_ids=true | all-gather | bytes 811008 | tf_op jit(solution)/shard_map/all_gather | solution.py:158
  117.3 25.5 all-gather.33.cloned.1.call-done
  285.2 85.5 %while.582 = (s32[]{:T(128)}, f32[24,64,128]{2,1,0:T(8,128)}, f32[2,128,24,64]{1,3,2,0:T(8,128)}, f32[2,24,128,128]{3,2,1,0:T(8,128)}, f32[2,128,128]{1,2,0:T(8,...) while((s32[]{:T(128)}, f32[24,64,128]{2,1,0:T(8,128)}, ...), condition=%wide.region_35.37_spmd.clone.clone, body=%wide.region_33.36_spmd.clone.clone.sunk | while | flops 935866368 | bytes 29146912 | solution.py:123
  405.4 46.1 %while.580 = (s32[]{:T(128)}, f32[24,64,128]{2,1,0:T(8,128)S(1)}, f32[2,128,24,64]{1,3,2,0:T(8,128)}, f32[2,24,128,128]{3,2,1,0:T(8,128)}, f32[2,128,128]{1,2,0:...) while((s32[]{:T(128)}, f32[24,64,128]{2,1,0:T(8,128)S(1)}, ...), condition=%wide.region_9.11_spmd.clone.clone, body=%wide.region_7.10_spmd.clone.clone.sunk | while | flops 935866368 | bytes 43221408 | solution.py:123
  481.5 42.3 %all-gather.6 = bf16[1,1536,24]{2,0,1:T(2,128)(2,1)S(1)} all-gather(bf16[1,96,24]{2,0,1:T(2,128)(2,1)S(1)} %copy.1163), channel_id=8, replica_groups=mesh['dp'=4,'seq'=4,'tensor'=2] {'dp','seq'}, dimensions={1}, use_global_device_ids=true | all-gather | bytes 78336 | tf_op jit(solution)/shard_map/all_gather | solution.py:155
  525.1 48.6 %all-gather.8 = bf16[1,1536,256]{2,1,0:T(8,128)(2,1)S(1)} all-gather(bf16[1,48,256]{2,1,0:T(8,128)(2,1)S(1)} %copy-done.303), channel_id=10, replica_groups=mesh['dp'=4,'seq'=4,'tensor'=2] {'dp','seq','tensor'}, dimensions={1}, use_global_device_ids=true | all-gather | bytes 811008 | tf_op jit(solution)/shard_map/all_gather | solution.py:158
  659.4 27.3 while.586
  698.6 34.1 %while.590 = (s32[]{:T(128)}, f32[24,64,128]{2,1,0:T(8,128)}, f32[2,128,24]{1,2,0:T(8,128)}, f32[2,128,24,1]{1,2,3,0:T(8,128)}, f32[2,128,24,64]{1,3,2,0:T(8,128...) while((s32[]{:T(128)}, f32[24,64,128]{2,1,0:T(8,128)}, ...), condition=%wide.region_43.45_spmd.clone, body=%wide.region_41.44_spmd.clone.sunk | while | flops 303575040 | bytes 10738264 | solution.py:114
  763.1 85.9 %while.581 = (s32[]{:T(128)}, f32[24,64,128]{2,1,0:T(8,128)}, f32[2,128,24,64]{1,3,2,0:T(8,128)}, f32[2,24,128,128]{3,2,1,0:T(8,128)}, f32[2,128,128]{1,2,0:T(8,...) while((s32[]{:T(128)}, f32[24,64,128]{2,1,0:T(8,128)}, ...), condition=%wide.region_22.24_spmd.clone.clone, body=%wide.region_20.23_spmd.clone.clone.sunk | while | flops 935866368 | bytes 29146912 | solution.py:123
  883.9 81.4 %while.583 = (s32[]{:T(128)}, f32[24,64,128]{2,1,0:T(8,128)}, f32[2,128,24,64]{1,3,2,0:T(8,128)}, f32[2,24,128,128]{3,2,1,0:T(8,128)}, f32[2,128,128]{1,2,0:T(8,...) while((s32[]{:T(128)}, f32[24,64,128]{2,1,0:T(8,128)}, ...), condition=%wide.region_48.50_spmd.clone.clone, body=%wide.region_46.49_spmd.clone.clone.sunk | while | flops 935866368 | bytes 59227116 | solution.py:123
  1012.1 62.0 %while.592 = (s32[]{:T(128)}, f32[24,64,128]{2,1,0:T(8,128)}, f32[2,128,24,64]{1,3,2,0:T(8,128)}, f32[2,128,128]{2,1,0:T(8,128)}, f32[2,128,128]{2,1,0:T(8,128)}...) while((s32[]{:T(128)}, f32[24,64,128]{2,1,0:T(8,128)}, ...), condition=%wide.region_64.66_spmd.clone, body=%wide.region_54.65_spmd.clone.sunk | while | flops 1869786112 | bytes 50676312 | solution.py:123
  1093.6 60.4 %while.594 = (s32[]{:T(128)}, f32[24,64,128]{2,1,0:T(8,128)}, f32[2,128,24,64]{1,3,2,0:T(8,128)}, f32[2,128,128]{2,1,0:T(8,128)}, f32[2,128,128]{2,1,0:T(8,128)}...) while((s32[]{:T(128)}, f32[24,64,128]{2,1,0:T(8,128)}, ...), condition=%wide.region_112.114_spmd.clone, body=%wide.region_102.113_spmd.clone.sunk | while | flops 1869786112 | bytes 50676312 | solution.py:123
  1180.7 30.1 while.573
  1326.2 24.4 all-reduce.76.cloned.1.call-done
  1386.6 60.5 %while.593 = (s32[]{:T(128)}, f32[24,64,128]{2,1,0:T(8,128)}, f32[2,128,24,64]{1,3,2,0:T(8,128)}, f32[2,128,128]{2,1,0:T(8,128)}, f32[2,128,128]{2,1,0:T(8,128)}...) while((s32[]{:T(128)}, f32[24,64,128]{2,1,0:T(8,128)}, ...), condition=%wide.region_88.90_spmd.clone, body=%wide.region_78.89_spmd.clone.sunk | while | flops 1869786112 | bytes 50151996 | solution.py:123
  1465.5 78.3 %while.595 = (s32[]{:T(128)}, f32[24,64,128]{2,1,0:T(8,128)}, f32[2,128,24,64]{1,3,2,0:T(8,128)}, f32[2,128,128]{2,1,0:T(8,128)}, f32[2,128,128]{2,1,0:T(8,128)}...) while((s32[]{:T(128)}, f32[24,64,128]{2,1,0:T(8,128)}, ...), condition=%wide.region_136.138_spmd.clone, body=%wide.region_126.137_spmd.clone.sunk | while | flops 1869786112 | bytes 44651704 | solution.py:123
  1570.4 28.9 while.575
  1713.1 28.5 copy.1024
  1834.0 28.1 pad_maximum_fusion
  1901.4 445.7 %all-reduce.72.cloned.1.call-done = f32[2,1536,1536]{1,0,2:T(2,128)} async-done(((f32[2,1536,1536]{1,0,2:T(2,128)}), f32[2,1536,1536]{1,0,2:T(2,128)}) %all-reduce.72.cloned.1.call-update) | async-done | bytes 18874384
  2349.7 546.2 %reduce-scatter.6.cloned.1.call-done = f32[2,96,2,1536]{3,1,2,0:T(8,128)} async-done(((f32[2,1536,2,1536]{3,1,2,0:T(8,128)}), f32[2,96,2,1536]{3,1,2,0:T(8,128)}) %reduce-scatter.6.cloned.1.call-update) | async-done | bytes 2359312 | tf_op jit(solution)/shard_map/reduce_scatter | solution.py:407
  2900.7 109.4 %all-reduce.74.cloned.1.call-done = (f32[2,1536]{1,0:T(2,128)}, f32[2,4,1536]{2,1,0:T(4,128)}, f32[2,1536]{1,0:T(2,128)}, f32[2,4,256]{2,1,0:T(4,128)}, f32[2,25...) async-done(((f32[2,1536]{1,0:T(2,128)}, f32[2,4,1536]{2,1,0:T(4,128)}, f32[2,1536]{1,0:T(2,128)}, ...) | async-done | bytes 96848 | tf_op jit(solution)/shard_map/psum | solution.py:420
  3010.1 107.8 %reduce-scatter.8.cloned.1.call-done = f32[2,48,256]{2,1,0:T(8,128)} async-done(((f32[2,1536,256]{2,1,0:T(8,128)}), f32[2,48,256]{2,1,0:T(8,128)}) %reduce-scatter.8.cloned.1.call-update) | async-done | bytes 98320 | tf_op jit(solution)/shard_map/reduce_scatter | solution.py:417
  (2613 shorter events, 1737.3 us)
Async XLA Ops:
  7.2 135.6 %all-gather.33.cloned.1.call-start = ((), (), s32[]{:S(2)}) async-start(), calls=%async_computation.5 | async-start | bytes 10027008 | tf_op jit(solution)/shard_map/all_gather | solution.py:154
  10.3 246.5 %all-gather.45.cloned.1.call-start = ((), (), s32[]{:S(2)}) async-start(), calls=%async_computation.11 | async-start | bytes 1966080 | tf_op jit(solution)/shard_map/all_gather | solution.py:23
  204.9 173.3 %all-gather.35.cloned.1.call-start = ((), (), s32[]{:S(2)}) async-start(), calls=%async_computation.6 | async-start | bytes 1966080 | tf_op jit(solution)/shard_map/all_gather | solution.py:23
  241.4 231.6 %all-gather.37.cloned.1.call-start = ((), (), s32[]{:S(2)}) async-start(), calls=%async_computation.7 | async-start | bytes 5013504 | tf_op jit(solution)/shard_map/all_gather | solution.py:156
  243.3 330.4 %all-gather.43.cloned.1.call-start = ((), (), s32[]{:S(2)}) async-start(), calls=%async_computation.10 | async-start | bytes 5013504 | tf_op jit(solution)/shard_map/all_gather | solution.py:156
  243.9 336.0 %all-gather.39.cloned.1.call-start = ((), (), s32[]{:S(2)}) async-start(), calls=%async_computation.8 | async-start | bytes 10027008 | tf_op jit(solution)/shard_map/all_gather | solution.py:154
  244.5 359.4 %all-reduce.78.cloned.1.call-start = ((), (), s32[]{:S(2)}) async-start(), calls=%async_computation.21 | async-start | bytes 6291456 | tf_op jit(solution)/shard_map/psum | solution.py:223
  480.8 254.1 %all-gather.41.cloned.1.call-start = ((), (), s32[]{:S(2)}) async-start(), calls=%async_computation.9 | async-start | bytes 1966080 | tf_op jit(solution)/shard_map/all_gather | solution.py:23
  622.9 19.9 collective-permute-start.1
  627.8 15.1 collective-permute-start.3
  687.6 168.2 %all-gather.47.cloned.1.call-start = ((), (), s32[]{:S(2)}) async-start(), calls=%async_computation.12 | async-start | bytes 1966080 | tf_op jit(solution)/shard_map/all_gather | solution.py:23
  734.7 435.8 %all-gather.49.cloned.1.call-start = ((), (), s32[]{:S(2)}) async-start(), calls=%async_computation.13 | async-start | bytes 1966080 | tf_op jit(solution)/shard_map/all_gather | solution.py:48
  1076.8 141.0 %all-gather.53.cloned.1.call-start = ((), (), s32[]{:S(2)}) async-start(), calls=%async_computation.15 | async-start | bytes 1966080 | tf_op jit(solution)/shard_map/all_gather | solution.py:48
  1170.4 152.8 %all-reduce.82.cloned.1.call-start = ((), (), s32[]{:S(2)}) async-start(), calls=%async_computation.23 | async-start | bytes 3145728 | tf_op jit(solution)/shard_map/psum | solution.py:316
  1299.3 51.3 %all-reduce.76.cloned.1.call-start = ((), (), s32[]{:S(2)}) async-start(), calls=%async_computation.20 | async-start | bytes 6291456 | tf_op jit(solution)/shard_map/psum | solution.py:223
  1310.5 249.6 %all-gather.51.cloned.1.call-start = ((), (), s32[]{:S(2)}) async-start(), calls=%async_computation.14 | async-start | bytes 1966080 | tf_op jit(solution)/shard_map/all_gather | solution.py:48
  1449.3 156.8 %all-gather.55.cloned.1.call-start = ((), (), s32[]{:S(2)}) async-start(), calls=%async_computation.16 | async-start | bytes 1966080 | tf_op jit(solution)/shard_map/all_gather | solution.py:48
  1560.0 322.1 %all-reduce.80.cloned.1.call-start = ((), (), s32[]{:S(2)}) async-start(), calls=%async_computation.22 | async-start | bytes 3145728 | tf_op jit(solution)/shard_map/psum | solution.py:316
  1658.9 8.5 collective-permute-start.5
  1686.1 209.1 %reduce-scatter.10.cloned.1.call-start = ((), (), s32[]{:S(2)}) async-start(), calls=%async_computation.17 | async-start | bytes 835584
  1698.2 648.9 %all-reduce.72.cloned.1.call-start = ((), (), s32[]{:S(2)}) async-start(), calls=%async_computation.18 | async-start | bytes 37748736
  1741.6 1154.2 %reduce-scatter.6.cloned.1.call-start = ((), (), s32[]{:S(2)}) async-start(), calls=%async_computation.3 | async-start | bytes 40108032 | tf_op jit(solution)/shard_map/reduce_scatter | solution.py:407
  1862.2 1147.8 %all-reduce.74.cloned.1.call-start = ((), (), s32[]{:S(2)}) async-start(), calls=%async_computation.19 | async-start | bytes 198656 | tf_op jit(solution)/shard_map/psum | solution.py:420
  1885.6 1232.3 %reduce-scatter.8.cloned.1.call-start = ((), (), s32[]{:S(2)}) async-start(), calls=%async_computation.4 | async-start | bytes 3244032 | tf_op jit(solution)/shard_map/reduce_scatter | solution.py:417
  (622 other events, 4340.2 us)
Sparse Core Ops, SparseCore 0:
  11.4 131.3 all-gather.32
  205.0 33.7 all-gather.44
  241.5 33.8 all-gather.34
  278.0 79.6 all-gather.36
  360.3 79.3 all-gather.42
  442.3 137.5 all-gather.38
  582.9 20.9 all-reduce.77
  687.7 33.0 all-gather.40
  734.8 33.0 all-gather.46
  1076.9 30.6 all-gather.48
  1170.5 30.6 all-gather.52
  1299.4 23.7 all-reduce.81
  1326.1 24.4 all-reduce.75
  1449.4 31.7 all-gather.50
  1560.2 31.7 all-gather.54
  1686.2 23.9 all-reduce.79
  1714.8 121.5 reduce-scatter.9
  1842.6 504.4 all-reduce.71
  2354.1 541.6 reduce-scatter.5
  2904.4 105.6 all-reduce.73
  3016.1 101.7 reduce-scatter.7
where the time goes:
time: 3160 us; the launch traced here: 3140 us
  waiting for transfers between devices  1280 us (41%)
  local copies, waits for them, and re-layouts  739 us (23%)
  matrix products  436 us (14%)
  other arithmetic  416 us (13%)
  blocking collectives  223 us (7%)
    reduce_scatter x1, waiting for transfers between devices, body(): lax.psum_scatter(stack_layers(layer_sums, 0), ('dp', 'seq'), scatter_dime...  546 us
    unnamed x23, waiting for transfers between devices  447 us
    dynamic_update_slice x136, local copies, waits for them, and re-layouts, span_summary(): lax.scan(state_step, zero_state, (to_blocks(inputs), to_blocks(keys_b), t...  123 us
    unnamed x737, local copies, waits for them, and re-layouts  121 us
    another operation x128, local copies, waits for them, and re-layouts  116 us
    psum x1, waiting for transfers between devices, body(): lax.psum((stack_layers(layer_sums, 4), stack_layers(layer_sums, 5), stack...  109 us
    reduce_scatter x1, waiting for transfers between devices, body(): lax.psum_scatter(stack_layers(layer_sums, 2), ('dp', 'seq', 'tensor'), sc...  108 us
    dot_general x24, matrix products, block_step(): inside = jnp.einsum('hts,shp->thp', mixing, inputs, precision=HIGHEST)  102 us
  transfers between devices with their start and end apart: 29, of which 10 were waited for; matrix products, arithmetic and copies ran while one was open for 31% of the time, Pallas kernels for 0%

commit v1 on v0

--- a/solution.py
+++ b/solution.py
@@ -1,6 +1,8 @@
 import jax
 import jax.numpy as jnp
 from jax import lax
+from jax.experimental import pallas as pl
+from jax.experimental.pallas import tpu as pltpu
 from jax.sharding import PartitionSpec as P
 
 DI = 3072
@@ -342,7 +344,7 @@
     return jnp.stack([grads_here[position] for grads_here in layer_sums])
 
 
-def body(
+def span_body(
     tokens,
     cotangent,
     norm_gain,
@@ -452,6 +454,830 @@
     )
 
 
+GROUP = ("seq", "tensor")
+LANES = 128
+ROWS = 8
+BF16, F32 = jnp.bfloat16, jnp.float32
+
+
+def hop(value, first, second):
+    pairs = [
+        (place * 2 + core, (place ^ (second if core else first)) * 2 + core)
+        for place in range(4)
+        for core in range(2)
+    ]
+    return lax.ppermute(value, GROUP, pairs)
+
+
+def swap(value):
+    return lax.ppermute(value, "tensor", [(0, 1), (1, 0)])
+
+
+def places():
+    place, core = lax.axis_index("seq"), lax.axis_index("tensor")
+    return place, core, place ^ (1 + core), place ^ (2 - core), place ^ 3
+
+
+def put(buffer, block, *index):
+    spots = index + (0,) * (buffer.ndim - len(index))
+    return lax.dynamic_update_slice(buffer, block.reshape((1,) * len(index) + block.shape), spots)
+
+
+def pick(array, index, axis=0):
+    return lax.dynamic_index_in_dim(array, index, axis, False)
+
+
+def group_gather(block):
+    place, core, near, far, across = places()
+    from_near, from_far = hop(block, 1, 2), hop(block, 2, 1)
+    from_across = hop(from_near, 2, 1)
+    out = jnp.zeros((4, 2) + block.shape, block.dtype)
+    for piece, own, other in (
+        (block, place, place),
+        (from_near, near, far),
+        (from_far, far, near),
+        (from_across, across, across),
+    ):
+        out = put(out, piece, own, core)
+        out = put(out, swap(piece), other, 1 - core)
+    return out
+
+
+def group_scatter(parts):
+    place, core, near, far, across = places()
+    arrived = swap(pick(parts, 1 - core, 1))
+    own = pick(parts, core, 1)
+
+    def both(index):
+        return pick(own, index).astype(F32) + pick(arrived, index).astype(F32)
+
+    side = both(near) + hop(both(across).astype(BF16), 2, 1).astype(F32)
+    here = both(place) + hop(both(far).astype(BF16), 2, 1).astype(F32)
+    return here + hop(side.astype(BF16), 1, 2).astype(F32)
+
+
+def group_sum(value):
+    for first, second in ((1, 2), (2, 1)):
+        value = value + hop(value, first, second)
+    return value + swap(value)
+
+
+def line_shift(value, axis, step):
+    count = lax.axis_size(axis)
+    return lax.ppermute(value, axis, [(i, (i + step) % count) for i in range(count)])
+
+
+def line_gather(block):
+    count, place = lax.axis_size("dp"), lax.axis_index("dp")
+    out = put(jnp.zeros((count,) + block.shape, block.dtype), block, place)
+    for step in range(1, count):
+        out = put(out, line_shift(block, "dp", step), (place - step) % count)
+    return out
+
+
+def line_scatter(parts):
+    count, place = lax.axis_size("dp"), lax.axis_index("dp")
+    total = pick(parts, place)
+    for step in range(1, count):
+        sent = pick(parts, (place + step) % count).astype(BF16)
+        total = total + line_shift(sent, "dp", step).astype(F32)
+    return total
+
+
+def seq_trade(parts):
+    place = lax.axis_index("seq")
+    out = put(jnp.zeros_like(parts), pick(parts, place), place)
+    for turn in (1, 2, 3):
+        got = lax.ppermute(pick(parts, place ^ turn), "seq", [(i, i ^ turn) for i in range(4)])
+        out = put(out, got, place ^ turn)
+    return out
+
+
+def mesh_sum(value):
+    for turn in (1, 2):
+        value = value + lax.ppermute(value, "seq", [(i, i ^ turn) for i in range(4)])
+    count = lax.axis_size("dp")
+    if count & (count - 1):
+        return lax.psum(value, "dp")
+    turn = 1
+    while turn < count:
+        value = value + lax.ppermute(value, "dp", [(i, i ^ turn) for i in range(count)])
+        turn *= 2
+    return value
+
+
+def dot(left, right, left_dim=1, right_dim=0):
+    return lax.dot_general(
+        left, right, (((left_dim,), (right_dim,)), ((), ())), preferred_element_type=F32
+    )
+
+
+def split(value, count):
+    pieces = []
+    for _ in range(count):
+        piece = value.astype(BF16)
+        pieces.append(piece)
+        value = value - piece.astype(F32)
+    return pieces
+
+
+def exact_left(value, ones, count, right_dim=0):
+    rows = value.shape[0]
+    stacked = dot(jnp.concatenate(split(value, count), axis=0), ones, 1, right_dim)
+    total = stacked[:rows]
+    for index in range(1, count):
+        total = total + stacked[index * rows : (index + 1) * rows]
+    return total
+
+
+def head_sums(picker, value):
+    high, low_part = split(value, 2)
+    return dot(picker, high, 1, 1) + dot(picker, low_part, 1, 1)
+
+
+def front(raw, window, taps, heads, spread, upper, width, state, extra):
+    length = raw.shape[0]
+    summed = taps[4:5, :] + taps[0:1, :] * window[5 : 5 + length, :]
+    for tap in range(1, 4):
+        summed = summed + taps[tap : tap + 1, :] * window[5 + tap : 5 + tap + length, :]
+    sig = jax.nn.sigmoid(summed)
+    activated = summed * sig
+    rates = jnp.transpose(raw[:, 2 * width + 2 * state :])[:ROWS] + heads[0:ROWS, :]
+    steps = jnp.maximum(rates, 0.0) + jnp.log1p(jnp.exp(-jnp.abs(rates)))
+    decays = -jnp.exp(heads[ROWS : 2 * ROWS, :]) * steps
+    running = exact_left(decays, upper, 3)
+    ending = running[:, length - 1 : length]
+    grown = jnp.exp(running)
+    tail = jnp.exp(ending - running)
+    rows = [steps, running, grown, tail] + extra
+    rows.append(jnp.zeros((length - ROWS * len(rows), length), F32))
+    columns = jnp.transpose(jnp.concatenate(rows, axis=0))
+    high, low_part = split(columns, 2)
+    wide = dot(high, spread) + dot(low_part, spread)
+    whole_decay = jnp.exp(jnp.broadcast_to(ending, (ROWS, LANES)))
+    inputs = activated[:, :width]
+    return dict(
+        summed=summed,
+        sig=sig,
+        inputs=inputs,
+        keys=activated[:, width : width + state].astype(BF16),
+        queries=activated[:, width + state :].astype(BF16),
+        rates=rates,
+        decays=decays,
+        running=running,
+        columns=columns,
+        steps_wide=wide[:, :width],
+        grown_wide=wide[:, width : 2 * width],
+        tail_wide=wide[:, 2 * width : 3 * width],
+        whole_decay=whole_decay,
+    )
+
+
+def per_row(whole_decay, head_count, head_size):
+    return jnp.concatenate(
+        [
+            jnp.broadcast_to(whole_decay[h : h + 1, :], (head_size, LANES))
+            for h in range(head_count)
+        ],
+        axis=0,
+    )
+
+
+def decay_matrix(parts, h, causal):
+    length = causal.shape[0]
+    column = parts["columns"][:, ROWS + h : ROWS + h + 1]
+    row = parts["running"][h : h + 1, :]
+    gap = jnp.broadcast_to(column, (length, length)) - row
+    return jnp.exp(jnp.where(causal, gap, -1e30))
+
+
+def causal_mask(length):
+    return lax.broadcasted_iota(jnp.int32, (length, length), 0) >= lax.broadcasted_iota(
+        jnp.int32, (length, length), 1
+    )
+
+
+def forward_kernel(
+    head_size,
+    raw_ref,
+    taps_ref,
+    chans_ref,
+    heads_ref,
+    spread_ref,
+    upper_ref,
+    value_ref,
+    square_ref,
+    mixed_ref,
+    state_ref,
+    carry,
+    window,
+):
+    length, width, state = raw_ref.shape[0], chans_ref.shape[1], carry.shape[1]
+    conv_width = width + 2 * state
+    head_count = width // head_size
+    pair = LANES // head_size
+
+    @pl.when(pl.program_id(0) == 0)
+    def _():
+        carry[...] = jnp.zeros_like(carry)
+        window[0:ROWS, :] = jnp.zeros((ROWS, conv_width), F32)
+
+    raw = raw_ref[...]
+    window[ROWS : ROWS + length, :] = raw[:, width : width + conv_width].astype(BF16).astype(F32)
+    parts = front(
+        raw,
+        window,
+        taps_ref[...],
+        heads_ref[...],
+        spread_ref[...],
+        upper_ref[...],
+        width,
+        state,
+        [],
+    )
+    window[0:ROWS, :] = window[length : length + ROWS, :]
+    inputs, keys, queries = parts["inputs"], parts["keys"], parts["queries"]
+    before = carry[...]
+    state_ref[...] = before
+    stepped = inputs * parts["steps_wide"]
+    stepped_low = stepped.astype(BF16)
+    scores = dot(queries, keys, 1, 1)
+    causal = causal_mask(length)
+    lane = lax.broadcasted_iota(jnp.int32, (length, LANES), 1) // head_size
+    columns = []
+    for block in range(head_count // pair):
+        source = stepped_low[:, block * LANES : (block + 1) * LANES]
+        joined = None
+        for k in range(pair):
+            mixing = (scores * decay_matrix(parts, block * pair + k, causal)).astype(BF16)
+            got = dot(mixing, source)
+            joined = got if joined is None else jnp.where(lane == k, got, joined)
+        columns.append(joined)
+    carried = dot(queries, before.astype(BF16), 1, 1)
+    mixed = (
+        jnp.concatenate(columns, axis=1)
+        + carried * parts["grown_wide"]
+        + chans_ref[0:1, :] * inputs
+    )
+    update = dot((stepped * parts["tail_wide"]).astype(BF16), keys, 0, 0)
+    carry[...] = per_row(parts["whole_decay"], head_count, head_size) * before + update
+    gate = raw[:, :width]
+    gated = mixed * (gate * jax.nn.sigmoid(gate))
+    mixed_ref[...] = mixed
+    value_ref[...] = (gated * chans_ref[1:2, :]).astype(BF16)
+    squares = jnp.sum(gated * gated, axis=1, keepdims=True)
+    square_ref[...] = jnp.transpose(jnp.broadcast_to(squares, (length, length)))[:ROWS]
+
+
+def backward_kernel(
+    head_size,
+    inner_count,
+    grad_ref,
+    raw_ref,
+    past_ref,
+    mixed_ref,
+    state_ref,
+    token_ref,
+    taps_ref,
+    chans_ref,
+    heads_ref,
+    spread_ref,
+    upper_ref,
+    picker_ref,
+    back_ref,
+    normed_ref,
+    taps_out,
+    chans_out,
+    heads_out,
+    carry,
+    window,
+    later,
+):
+    length, width, state = raw_ref.shape[0], chans_ref.shape[1], carry.shape[1]
+    conv_width = width + 2 * state
+    head_count = width // head_size
+    pair = LANES // head_size
+    step, count = pl.program_id(0), pl.num_programs(0)
+
+    @pl.when(step == 0)
+    def _():
+        carry[...] = jnp.zeros_like(carry)
+        later[length : length + ROWS, :] = jnp.zeros((ROWS, conv_width), F32)
+        taps_out[...] = jnp.zeros_like(taps_out)
+        chans_out[...] = jnp.zeros_like(chans_out)
+        heads_out[...] = jnp.zeros_like(heads_out)
+
+    raw = raw_ref[...]
+    past = past_ref[:, width : width + conv_width].astype(BF16).astype(F32)
+    window[0:ROWS, :] = jnp.where(step == count - 1, 0.0, past)
+    window[ROWS : ROWS + length, :] = raw[:, width : width + conv_width].astype(BF16).astype(F32)
+    taps, heads, picker = taps_ref[...], heads_ref[...], picker_ref[...]
+    parts = front(
+        raw, window, taps, heads, spread_ref[...], upper_ref[...], width, state, [token_ref[...]]
+    )
+    inputs, keys, queries = parts["inputs"], parts["keys"], parts["queries"]
+    skip, gain = chans_ref[0:1, :], chans_ref[1:2, :]
+    scale = parts["columns"][:, 4 * ROWS : 4 * ROWS + 1]
+    inner = parts["columns"][:, 4 * ROWS + 1 : 4 * ROWS + 2]
+
+    gate, mixed = raw[:, :width], mixed_ref[...]
+    gate_sig = jax.nn.sigmoid(gate)
+    gate_silu = gate * gate_sig
+    gated = mixed * gate_silu
+    grad = grad_ref[...]
+    scaled_gated = gated * scale
+    normed_ref[...] = (scaled_gated * gain).astype(BF16)
+    gain_term = jnp.sum(grad * scaled_gated, axis=0, keepdims=True)
+    grad_gated = scale * (grad * gain) - gated * (scale * scale * scale * inner / inner_count)
+    grad_mixed = grad_gated * gate_silu
+    back_ref[:, :width] = (
+        grad_gated * mixed * (gate_sig + gate_silu * (1.0 - gate_sig))
+    ).astype(BF16)
+    skip_term = jnp.sum(grad_mixed * inputs, axis=0, keepdims=True)
+    chans_out[0:1, :] += skip_term
+    chans_out[1:2, :] += gain_term
+
+    stepped = inputs * parts["steps_wide"]
+    stepped_low, grad_low = stepped.astype(BF16), grad_mixed.astype(BF16)
+    scores = dot(queries, keys, 1, 1)
+    causal = causal_mask(length)
+    lane = lax.broadcasted_iota(jnp.int32, (length, LANES), 1)
+    head_lane = lane // head_size
+    grad_scores = jnp.zeros((length, length), F32)
+    row_sums = jnp.zeros((length, length), F32)
+    column_sums, columns = [], []
+    for block in range(head_count // pair):
+        cut = slice(block * LANES, (block + 1) * LANES)
+        source, target = stepped_low[:, cut], grad_low[:, cut]
+        joined = None
+        for k in range(pair):
+            h = block * pair + k
+            spread_h = decay_matrix(parts, h, causal)
+            own_target = jnp.where(head_lane == k, target, jnp.zeros_like(target))
+            pulled = dot(own_target, source, 1, 1) * spread_h
+            grad_scores = grad_scores + pulled
+            moved = pulled * scores
+            row_sums = jnp.where(lane == h, jnp.sum(moved, axis=1, keepdims=True), row_sums)
+            column_sums.append(jnp.sum(moved, axis=0, keepdims=True))
+            got = dot((scores * spread_h).astype(BF16), target, 0, 0)
+            joined = got if joined is None else jnp.where(head_lane == k, got, joined)
+        columns.append(joined)
+    before, after = state_ref[...], carry[...]
+    before_low, after_low = before.astype(BF16), after.astype(BF16)
+    tail_wide, grown_wide = parts["tail_wide"], parts["grown_wide"]
+    through = tail_wide * dot(keys, after_low, 1, 1)
+    grad_stepped = jnp.concatenate(columns, axis=1) + through
+    ended = stepped * through
+    carried = dot(queries, before_low, 1, 1) * grown_wide
+    whole_rows = per_row(parts["whole_decay"], head_count, head_size)
+    kept = whole_rows * after
+    held = jnp.sum(kept * before, axis=1, keepdims=True)
+    spare = jnp.zeros((ROWS - head_count, 1), F32)
+    held_heads = jnp.concatenate(
+        [
+            jnp.sum(held[h * head_size : (h + 1) * head_size], axis=0, keepdims=True)
+            for h in range(head_count)
+        ]
+        + [spare],
+        axis=0,
+    )
+    ended_heads = head_sums(picker, ended)
+    grad_running = (
+        jnp.transpose(row_sums)[:ROWS]
+        - jnp.concatenate(column_sums + [jnp.zeros((ROWS - head_count, length), F32)], axis=0)
+        + head_sums(picker, grad_mixed * carried)
+        - ended_heads
+    )
+    last = jnp.sum(ended_heads, axis=1, keepdims=True) + held_heads
+    row_lane = lax.broadcasted_iota(jnp.int32, (ROWS, length), 1)
+    grad_running = grad_running + jnp.where(row_lane == length - 1, last, 0.0)
+    grad_decays = exact_left(grad_running, upper_ref[...], 3, 1)
+    grad_steps = head_sums(picker, inputs * grad_stepped)
+    grad_rates = (
+        grad_steps - jnp.exp(heads[ROWS : 2 * ROWS, :]) * grad_decays
+    ) * jax.nn.sigmoid(parts["rates"])
+    row_head = lax.broadcasted_iota(jnp.int32, (ROWS, length), 0)
+    grad_rates = jnp.where(row_head < head_count, grad_rates, 0.0)
+    heads_out[0:ROWS, :] += grad_rates
+    heads_out[ROWS : 2 * ROWS, :] += grad_decays * parts["decays"]
+    back_ref[:, 2 * width + 2 * state :] = jnp.transpose(
+        jnp.concatenate([grad_rates, jnp.zeros((LANES - ROWS, length), F32)], axis=0)
+    ).astype(BF16)
+
+    grad_inputs = parts["steps_wide"] * grad_stepped + skip * grad_mixed
+    grown_low = (grown_wide * grad_mixed).astype(BF16)
+    scores_low = grad_scores.astype(BF16)
+    grad_queries = dot(scores_low, keys) + dot(grown_low, before_low)
+    grad_keys = dot(scores_low, queries, 0, 0) + dot(
+        (stepped * tail_wide).astype(BF16), after_low
+    )
+    carry[...] = kept + dot(grown_low, queries, 0, 0)
+
+    sig, summed = parts["sig"], parts["summed"]
+    grad_v = jnp.concatenate([grad_inputs, grad_keys, grad_queries], axis=1) * (
+        sig + summed * sig * (1.0 - sig)
+    )
+    later[0:length, :] = grad_v
+    grad_conv = taps[3:4, :] * grad_v
+    taps_out[4:5, :] += jnp.sum(grad_v, axis=0, keepdims=True)
+    for tap in range(4):
+        if tap < 3:
+            grad_conv = grad_conv + taps[tap : tap + 1, :] * later[3 - tap : 3 - tap + length, :]
+        taps_out[tap : tap + 1, :] += jnp.sum(
+            grad_v * window[5 + tap : 5 + tap + length, :], axis=0, keepdims=True
+        )
+    later[length : length + ROWS, :] = grad_v[0:ROWS]
+    back_ref[:, width : width + conv_width] = grad_conv.astype(BF16)
+
+
+def tables(width, head_size):
+    channel_head = jnp.arange(width)[None, :] // head_size
+    rows = jnp.arange(LANES)[:, None]
+    spread = jnp.concatenate(
+        [rows == channel_head + ROWS * kind for kind in (0, 2, 3)], axis=1
+    ).astype(BF16)
+    upper = (rows <= jnp.arange(LANES)[None, :]).astype(BF16)
+    picker = (jnp.arange(ROWS)[:, None] == channel_head).astype(BF16)
+    return spread, upper, picker
+
+
+def fixed(shape):
+    return pl.BlockSpec(shape, lambda i: (0,) * len(shape))
+
+
+def mix_forward(raw, small, tabs, head_size, width, state):
+    taps, chans, heads = small
+    spread, upper, _ = tabs
+    tokens, columns = raw.shape
+    count = tokens // STRETCH
+    return pl.pallas_call(
+        lambda *refs: forward_kernel(head_size, *refs),
+        grid=(count,),
+        in_specs=[
+            pl.BlockSpec((STRETCH, columns), lambda i: (i, 0)),
+            fixed(taps.shape),
+            fixed(chans.shape),
+            fixed(heads.shape),
+            fixed(spread.shape),
+            fixed(upper.shape),
+        ],
+        out_specs=[
+            pl.BlockSpec((STRETCH, width), lambda i: (i, 0)),
+            pl.BlockSpec((ROWS, LANES), lambda i: (i, 0)),
+            pl.BlockSpec((STRETCH, width), lambda i: (i, 0)),
+            pl.BlockSpec((None, width, state), lambda i: (i, 0, 0)),
+        ],
+        out_shape=[
+            jax.ShapeDtypeStruct((tokens, width), BF16),
+            jax.ShapeDtypeStruct((count * ROWS, LANES), F32),
+            jax.ShapeDtypeStruct((tokens, width), F32),
+            jax.ShapeDtypeStruct((count, width, state), F32),
+        ],
+        scratch_shapes=[
+            pltpu.VMEM((width, state), F32),
+            pltpu.VMEM((STRETCH + ROWS, width + 2 * state), F32),
+        ],
+        compiler_params=pltpu.CompilerParams(
+            dimension_semantics=("arbitrary",), vmem_limit_bytes=40 * 2**20
+        ),
+        cost_estimate=pl.CostEstimate(
+            flops=15_000_000_000, bytes_accessed=10_000_000, transcendentals=0
+        ),
+    )(raw, taps, chans, heads, spread, upper)
+
+
+def mix_backward(grad, raw, mixed, states, token_rows, small, tabs, head_size, inner_count):
+    taps, chans, heads = small
+    spread, upper, picker = tabs
+    tokens, columns = raw.shape
+    width, state = states.shape[1:]
+    count = tokens // STRETCH
+    per = STRETCH // ROWS
+
+    def back(i):
+        return (count - 1 - i, 0)
+
+    return pl.pallas_call(
+        lambda *refs: backward_kernel(head_size, inner_count, *refs),
+        grid=(count,),
+        in_specs=[
+            pl.BlockSpec((STRETCH, width), back),
+            pl.BlockSpec((STRETCH, columns), back),
+            pl.BlockSpec((ROWS, columns), lambda i: (jnp.maximum((count - 1 - i) * per - 1, 0), 0)),
+            pl.BlockSpec((STRETCH, width), back),
+            pl.BlockSpec((None, width, state), lambda i: (count - 1 - i, 0, 0)),
+            pl.BlockSpec((ROWS, LANES), back),
+            fixed(taps.shape),
+            fixed(chans.shape),
+            fixed(heads.shape),
+            fixed(spread.shape),
+            fixed(upper.shape),
+            fixed(picker.shape),
+        ],
+        out_specs=[
+            pl.BlockSpec((STRETCH, columns), back),
+            pl.BlockSpec((STRETCH, width), back),
+            fixed(taps.shape),
+            fixed(chans.shape),
+            fixed(heads.shape),
+        ],
+        out_shape=[
+            jax.ShapeDtypeStruct((tokens, columns), BF16),
+            jax.ShapeDtypeStruct((tokens, width), BF16),
+            jax.ShapeDtypeStruct(taps.shape, F32),
+            jax.ShapeDtypeStruct(chans.shape, F32),
+            jax.ShapeDtypeStruct(heads.shape, F32),
+        ],
+        scratch_shapes=[
+            pltpu.VMEM((width, state), F32),
+            pltpu.VMEM((STRETCH + ROWS, width + 2 * state), F32),
+            pltpu.VMEM((STRETCH + ROWS, width + 2 * state), F32),
+        ],
+        compiler_params=pltpu.CompilerParams(
+            dimension_semantics=("arbitrary",), vmem_limit_bytes=40 * 2**20
+        ),
+        cost_estimate=pl.CostEstimate(
+            flops=30_000_000_000, bytes_accessed=16_000_000, transcendentals=0
+        ),
+    )(grad, raw, raw, mixed, states, token_rows, taps, chans, heads, spread, upper, picker)
+
+
+def norm_scale(hidden):
+    return lax.rsqrt(jnp.mean(hidden * hidden, axis=1, keepdims=True) + EPSILON)
+
+
+def head_body(
+    tokens,
+    cotangent,
+    norm_gain,
+    inner_weight,
+    rate_weight,
+    state_weight,
+    conv_inner,
+    bias_inner,
+    conv_state,
+    bias_state,
+    rate_bias,
+    decay_log,
+    skip_gain,
+    gate_gain,
+    out_weight,
+):
+    layers, batches = norm_gain.shape[0], tokens.shape[0]
+    model = tokens.shape[3]
+    place, core = lax.axis_index("seq"), lax.axis_index("tensor")
+    line = lax.axis_size("dp")
+    share, half_width = inner_weight.shape[1], inner_weight.shape[3]
+    inner_count = half_width * 2
+    width = half_width // 4
+    head_count = rate_bias.shape[1] // 4
+    head_size = width // head_count
+    state_share, state = state_weight.shape[1], state_weight.shape[2] // 2
+    own_rows = tokens.shape[2] // 2
+    length = own_rows * 8
+    conv_width = width + 2 * state
+    columns = 2 * width + 2 * state + LANES
+    tabs = tables(width, head_size)
+
+    def out_share(layer):
+        turned = out_weight[layer].T.reshape(share, 4, width)
+        return turned.transpose(1, 0, 2)
+
+    def inner_share(layer):
+        cut = inner_weight[layer].reshape(share, 2, 4, width)
+        return cut.transpose(2, 0, 1, 3).reshape(4, share, 2 * width)
+
+    def whole(parts):
+        traded = seq_trade(parts)
+        return line_gather(traded.reshape(4 * share, -1)).reshape(line * 4 * share, -1)
+
+    heads_here = rate_weight.shape[2]
+    rate_flat = rate_weight.reshape(layers, state_share, -1)
+    rate_flat = jnp.pad(rate_flat, ((0, 0), (0, 0), (0, LANES - rate_flat.shape[2])))
+    small_share = jnp.concatenate([state_weight, rate_flat], axis=2)
+    small_line = line_gather(small_share.reshape(layers * state_share, -1))
+    small_all = group_gather(small_line.reshape(line * layers * state_share, -1))
+    small_all = small_all.reshape(4, 2, line, layers, state_share, -1)
+    state_full = small_all[..., : 2 * state].transpose(3, 2, 0, 1, 4, 5).reshape(layers, model, -1)
+    rate_half = pick(small_all, core, 1)[..., 2 * state : 2 * state + 2 * heads_here]
+    rate_half = rate_half.reshape(4, line, layers, share, heads_here)
+    rate_own = lax.dynamic_slice_in_dim(rate_half, place * head_count, head_count, 4)
+    rate_own = rate_own.transpose(2, 1, 0, 3, 4).reshape(layers, model, head_count)
+    rate_own = jnp.pad(rate_own, ((0, 0), (0, 0), (0, LANES - head_count)))
+
+    in_weights, out_weights = [], []
+    for layer in range(layers):
+        inner_full = whole(inner_share(layer))
+        in_weights.append(
+            jnp.concatenate([inner_full, state_full[layer], rate_own[layer]], axis=1)
+        )
+        out_weights.append(whole(out_share(layer)))
+
+    def quarter(array, count):
+        return lax.dynamic_slice_in_dim(array, place * count, count, array.ndim - 1)
+
+    smalls = []
+    for layer in range(layers):
+        taps = jnp.concatenate([quarter(conv_inner[layer], width), conv_state[layer]], axis=1)
+        bias = jnp.concatenate([quarter(bias_inner[layer], width), bias_state[layer]])
+        taps = jnp.concatenate([taps, bias[None], jnp.zeros((3, conv_width), F32)], axis=0)
+        skip = jnp.repeat(quarter(skip_gain[layer], head_count), head_size)
+        chans = jnp.stack([skip, quarter(gate_gain[layer], width)])
+        chans = jnp.concatenate([chans, jnp.zeros((ROWS - 2, width), F32)], axis=0)
+        heads = jnp.stack([quarter(rate_bias[layer], head_count), quarter(decay_log[layer], head_count)])
+        heads = jnp.pad(heads, ((0, 0), (0, ROWS - head_count))).reshape(2 * ROWS, 1)
+        smalls.append((taps, chans, jnp.broadcast_to(heads, (2 * ROWS, LANES))))
+
+    def own(array):
+        return lax.dynamic_slice_in_dim(array, core * own_rows, own_rows, 0)
+
+    results, kept = [], [[None] * layers for _ in range(batches)]
+    hiddens = [own(tokens[batch, 0]).astype(F32) for batch in range(batches)]
+    for layer in range(layers):
+        for batch in range(batches):
+            hidden = hiddens[batch]
+            row_scale = norm_scale(hidden)
+            normed_own = (hidden * row_scale * norm_gain[layer][None, :]).astype(BF16)
+            normed = group_gather(normed_own).reshape(length, model)
+            raw = dot(normed, in_weights[layer])
+            value, squares, mixed, states = mix_forward(
+                raw, smalls[layer], tabs, head_size, width, state
+            )
+            partial = dot(value, out_weights[layer], 1, 1).astype(BF16)
+            summed = group_scatter(partial.reshape(4, 2, own_rows, model))
+            squares = group_sum(squares.reshape(-1, ROWS, LANES)[:, 0])
+            scales = lax.rsqrt(squares / inner_count + EPSILON)
+            own_scale = pick(scales.reshape(8, own_rows), place * 2 + core)[:, None]
+            kept[batch][layer] = (hidden, row_scale, normed, raw, mixed, states, summed, scales)
+            hiddens[batch] = hidden + own_scale * summed
+    results = hiddens
+
+    grads = [own(cotangent[batch, 0]).astype(F32) for batch in range(batches)]
+    big, small_sums = [None] * layers, [None] * layers
+    for layer in reversed(range(layers)):
+        sums = None
+        for batch in range(batches):
+            hidden, row_scale, normed, raw, mixed, states, summed, scales = kept[batch][layer]
+            grad_hidden = grads[batch]
+            grad_low = grad_hidden.astype(BF16)
+            inner_own = jnp.sum(grad_low.astype(F32) * summed, axis=1)
+            inner = jnp.zeros((8, own_rows), F32)
+            inner = put(inner, inner_own, place * 2 + core)
+            inner = group_sum(inner).reshape(-1, LANES)
+            token_rows = jnp.stack([scales, inner], axis=1)
+            token_rows = jnp.pad(token_rows, ((0, 0), (0, ROWS - 2), (0, 0)))
+            grad_all = group_gather(grad_low).reshape(length, model)
+            grad_value = dot(grad_all, out_weights[layer])
+            back, normed_out, taps_grad, chans_grad, heads_grad = mix_backward(
+                grad_value,
+                raw,
+                mixed,
+                states,
+                token_rows.reshape(-1, LANES),
+                smalls[layer],
+                tabs,
+                head_size,
+                inner_count,
+            )
+            partial = dot(back, in_weights[layer], 1, 1).astype(BF16)
+            grad_normed = group_scatter(partial.reshape(4, 2, own_rows, model))
+            gain_term = jnp.sum(grad_normed * hidden * row_scale, axis=0)
+            weighted = grad_normed * norm_gain[layer][None, :]
+            mean = jnp.mean(weighted * hidden, axis=1, keepdims=True)
+            grads[batch] = (
+                grad_hidden
+                + row_scale * weighted
+                - hidden * (row_scale * row_scale * row_scale) * mean
+            )
+            out_term = dot(grad_all, normed_out, 0, 0)
+            in_term = dot(normed, back, 0, 0)
+            new = (in_term, out_term, taps_grad, chans_grad, heads_grad, gain_term)
+            sums = new if sums is None else tuple(a + b for a, b in zip(sums, new))
+        big[layer] = sums[:2]
+        small_sums[layer] = sums[2:]
+
+    def traded(total, cut):
+        return seq_trade(total[:, :cut].reshape(4, share, cut).astype(BF16)).astype(F32)
+
+    inner_grads, rate_grads, state_grads, out_grads = [], [], [], []
+    for layer in range(layers):
+        in_sum, out_sum = big[layer]
+        out_total = line_scatter(out_sum.reshape(line, 4 * share, width))
+        out_here = traded(out_total, width)
+        out_grads.append(out_here.transpose(1, 0, 2).reshape(share, half_width).T)
+        states_part = in_sum[:, 2 * width : 2 * width + 2 * state]
+        states_part = states_part.reshape(line * 4, 2, state_share, 2 * state)
+        sent = swap(pick(states_part, 1 - core, 1).astype(BF16))
+        states_part = pick(states_part, core, 1) + sent.astype(F32)
+        states_part = states_part.reshape(line, 4 * share, state)
+        in_part = in_sum.reshape(line, 4 * share, columns)
+        packed = jnp.concatenate(
+            [in_part[..., : 2 * width], states_part, in_part[..., 2 * width + 2 * state :]], axis=2
+        )
+        total = line_scatter(packed)
+        here = traded(total, total.shape[1])
+        inner_here = here[..., : 2 * width].reshape(4, share, 2, width)
+        inner_grads.append(inner_here.transpose(1, 2, 0, 3).reshape(share, 2, half_width))
+        state_grads.append(
+            jnp.sum(here[..., 2 * width : 2 * width + state], axis=0).reshape(state_share, 2 * state)
+        )
+        rate_here = here[..., 2 * width + state : 2 * width + state + head_count]
+        rate_grads.append(rate_here.transpose(1, 0, 2).reshape(share, heads_here))
+
+    def slot(array, count):
+        shape = array.shape[:-1] + (4 * count,)
+        spots = (0,) * (array.ndim - 1) + (place * count,)
+        return lax.dynamic_update_slice(jnp.zeros(shape, F32), array, spots)
+
+    pieces = []
+    for layer in range(layers):
+        taps_grad, chans_grad, heads_grad, gain_term = small_sums[layer]
+        both = jnp.concatenate([gain_term, taps_grad[:5, width:].reshape(-1)])
+        both = both + swap(both)
+        head_rows = jnp.stack(
+            [
+                jnp.sum(heads_grad[:ROWS], axis=1)[:head_count],
+                jnp.sum(heads_grad[ROWS:], axis=1)[:head_count],
+                jnp.sum(chans_grad[0].reshape(head_count, head_size), axis=1),
+            ]
+        )
+        pieces += [
+            both,
+            slot(taps_grad[:5, :width], width).reshape(-1),
+            slot(chans_grad[1], width),
+            slot(head_rows, head_count).reshape(-1),
+        ]
+    flat = jnp.concatenate(pieces)
+    spill = -flat.shape[0] % (ROWS * LANES)
+    flat = mesh_sum(jnp.pad(flat, (0, spill)).reshape(-1, LANES)).reshape(-1)
+    taken, small_out = 0, []
+    for layer in range(layers):
+        found = []
+        for shape in (
+            (model,),
+            (5, 2 * state),
+            (5, half_width),
+            (half_width,),
+            (3, 4 * head_count),
+        ):
+            size = 1
+            for extent in shape:
+                size *= extent
+            found.append(flat[taken : taken + size].reshape(shape))
+            taken += size
+        small_out.append(found)
+
+    def spread_out(batched):
+        both = []
+        for value in batched:
+            other = swap(value)
+            first = jnp.where(core == 0, value, other)
+            second = jnp.where(core == 0, other, value)
+            both.append(jnp.concatenate([first, second], axis=0))
+        return jnp.stack(both)[:, None]
+
+    def stacked(position, cut=lambda value: value):
+        return jnp.stack([cut(found[position]) for found in small_out])
+
+    return (
+        spread_out(results),
+        spread_out(grads),
+        stacked(0),
+        jnp.stack(inner_grads),
+        jnp.stack(rate_grads),
+        jnp.stack(state_grads),
+        stacked(2, lambda value: value[:4]),
+        stacked(2, lambda value: value[4]),
+        stacked(1, lambda value: value[:4]),
+        stacked(1, lambda value: value[4]),
+        stacked(4, lambda value: value[0]),
+        stacked(4, lambda value: value[1]),
+        stacked(4, lambda value: value[2]),
+        stacked(3),
+        jnp.stack(out_grads),
+    )
+
+
+def by_heads(mesh, tokens, inner_weight, rate_bias, conv_state, state_weight):
+    place_count, core_count, line = mesh.shape["seq"], mesh.shape["tensor"], mesh.shape["dp"]
+    if place_count != 4 or core_count != 2:
+        return False
+    heads, inner = rate_bias.shape[1], inner_weight.shape[3]
+    rows = tokens.shape[2] // 8
+    return (
+        tokens.shape[1] == line
+        and tokens.shape[2] % 8 == 0
+        and rows == STRETCH
+        and heads % 8 == 0
+        and heads // 8 <= ROWS
+        and (inner // 8) % LANES == 0
+        and LANES % (inner // heads) == 0
+        and conv_state.shape[1] == 4
+        and state_weight.shape[2] == 2 * LANES
+        and inner_weight.shape[1] % (line * 4 * 32) == 0
+    )
+
+
 def solution(mesh):
     in_specs = (
         P(None, "dp", "seq", None),
@@ -487,4 +1313,11 @@
         P(None, "tensor"),
         P(None, "tensor", ("dp", "seq")),
     )
-    return jax.shard_map(body, mesh=mesh, in_specs=in_specs, out_specs=out_specs, check_vma=False)
+    def run(*arrays):
+        by_name = (arrays[0], arrays[3], arrays[10], arrays[8], arrays[5])
+        chosen = head_body if by_heads(mesh, *by_name) else span_body
+        return jax.shard_map(
+            chosen, mesh=mesh, in_specs=in_specs, out_specs=out_specs, check_vma=False
+        )(*arrays)
+
+    return run

time: 3160 us -> 1110 us (0.35)
  waiting for transfers between devices: 1280 us -> 360 us
  local copies, waits for them, and re-layouts: 739 us -> 158 us
  matrix products: 436 us -> 99.2 us
  other arithmetic: 416 us -> 84.5 us
  starting transfers between devices: 19.2 us -> 269 us
  blocking collectives: 223 us -> 0 us
  Pallas kernels: 0 us -> 121 us
    reduce_scatter x2 -> x0, waiting for transfers between devices: 654 us -> none  [the longest x1 546 us: body(): lax.psum_scatter(stack_layers(layer_sums, 0), ('dp', 'seq'), scatter_dime...]
    unnamed x23 -> x0, waiting for transfers between devices: 447 us -> none
    ppermute x8 -> x182, waiting for transfers between devices: 0.42 us -> 360 us  [the longest x27 155 us: line_shift(): lax.ppermute(value, axis, [(i, (i + step) % count) for i in range(count)])]
    dot_general x168 -> x24, matrix products: 436 us -> 99.2 us  [dot(): lax.dot_general(left, right, (((left_dim,), (right_dim,)), ((), ())), pre...]
    ppermute x8 -> x182, starting transfers between devices: 17.9 us -> 269 us  [the longest x27 88.4 us: line_shift(): lax.ppermute(value, axis, [(i, (i + step) % count) for i in range(count)])]
    all_gather x4 -> x0, blocking collectives: 185 us -> none  [the longest x2 99 us: gather_layer(): lax.all_gather(state_weight[layer_index], ('dp', 'seq', 'tensor'), axis=0...]
    psum x5 -> x0, waiting for transfers between devices: 150 us -> none  [the longest x1 109 us: body(): lax.psum((stack_layers(layer_sums, 4), stack_layers(layer_sums, 5), stack...]
    another operation x149 -> x59, local copies, waits for them, and re-layouts: 160 us -> 23.7 us  [the longest x35 10.1 us: run(): jax.shard_map(chosen, mesh=mesh, in_specs=in_specs, out_specs=out_specs,...]
  transfers between devices with their start and end apart: 29 -> 182, of which waited for: 10 -> 82; matrix products, arithmetic and copies ran while one was open for 31% -> 19% of each run, Pallas kernels for 0% -> 0%
where the time goes in v1:
time: 1110 us; the launch traced here: 1100 us
  waiting for transfers between devices  360 us (32%)
  starting transfers between devices  269 us (24%)
  local copies, waits for them, and re-layouts  158 us (14%)
  Pallas kernels  121 us (11%)
  matrix products  99.2 us (9%)
  other arithmetic  84.5 us (8%)
    ppermute x27, waiting for transfers between devices, line_shift(): lax.ppermute(value, axis, [(i, (i + step) % count) for i in range(count)])  155 us
    ppermute x67, waiting for transfers between devices, hop(): return lax.ppermute(value, GROUP, pairs)  145 us
    dot_general x24, matrix products, dot(): lax.dot_general(left, right, (((left_dim,), (right_dim,)), ((), ())), pre...  99.2 us
    ppermute x27, starting transfers between devices, line_shift(): lax.ppermute(value, axis, [(i, (i + step) % count) for i in range(count)])  88.4 us
    pallas_call x4, Pallas kernels, mix_backward(): pl.pallas_call(lambda *refs: backward_kernel(head_size, inner_count, *ref...  81.7 us
    ppermute x60, starting transfers between devices, swap(): return lax.ppermute(value, 'tensor', [(0, 1), (1, 0)])  72.9 us
    ppermute x67, starting transfers between devices, hop(): return lax.ppermute(value, GROUP, pairs)  63.6 us
    pallas_call x4, Pallas kernels, mix_forward(): pl.pallas_call(lambda *refs: forward_kernel(head_size, *refs), grid=(coun...  39.2 us
  transfers between devices with their start and end apart: 182, of which 82 were waited for; matrix products, arithmetic and copies ran while one was open for 19% of the time, Pallas kernels for 0%

profile of v1, /device:TPU:1, one launch (start us, length us, event | category | flops | bytes accessed | tf_op | source)
XLA Modules:
  0.0 1096.3 jit_solution(11390491267422507346)
XLA Ops:
  68.9 27.6 %collective-permute-done.56 = bf16[384,384]{1,0:T(8,128)(2,1)S(1)} collective-permute-done((bf16[384,384]{1,0:T(8,128)(2,1)S(1)}, bf16[384,384]{1,0:T(8,128)(2,1)S(1)}, u32[]{:S(2)}, u32[]{:S(2)}) %collective-permute-start.56) | collective-permute-done | bytes 294944 | tf_op jit(solution)/shard_map/ppermute | solution.py:527
  136.7 20.8 %collective-permute-done.11 = bf16[384,768]{1,0:T(8,128)(2,1)S(1)} collective-permute-done((bf16[384,768]{1,0:T(8,128)(2,1)S(1)}, bf16[384,768]{1,0:T(8,128)(2,1)S(1)}, u32[]{:S(2)}, u32[]{:S(2)}) %collective-permute-start.11) | collective-permute-done | bytes 589856 | tf_op jit(solution)/shard_map/ppermute | solution.py:527
  180.3 9.7 shard_map.262
  212.2 11.8 %collective-permute-start.46 = (bf16[384,768]{1,0:T(8,128)(2,1)}, bf16[384,768]{1,0:T(8,128)(2,1)S(1)}, u32[]{:S(2)}, u32[]{:S(2)}) collective-permute-start(bf16[384,768]{1,0:T(8,128)(2,1)} %bitcast.1002), channel_id=1, source_target_pairs={{0,8},{8,16},{16,24},{24,0},{1,9},{9,17},{17,25},{25,1},{2,10},{10... | collective-permute-start | bytes 1769480 | tf_op jit(solution)/shard_map/ppermute | solution.py:527
  255.7 7.1 collective-permute-done.47
  280.2 6.8 fusion.135.refs_0_.refs_1_.refs_2_
  287.1 9.8 shard_map.263
  314.6 7.1 collective-permute-done.59
  357.8 20.3 %shard_map.266 = (bf16[1024,1152]{1,0:T(8,128)(2,1)S(1)}, bf16[1024,384]{1,0:T(8,128)(2,1)S(1)}, f32[8,640]{1,0:T(8,128)S(1)}, f32[8,384]{1,0:T(8,128)S(1)}, f32[16,128]{1,0:T(8,128)S(1)}) custom-call(f32[1024,384]{1,0:T(8,128)S(1)} %fusion.158.refs_0_, f32[1024,1152]{1,0:T(8,128)S(1)} %bitcast.933, f32[1024,1152]{1,0:T(8,128)S(1)} %bitcast.933, ...), custom_call_target="tpu_custom_call" | custom-call | flops 30000001024 | bytes 16000000 | tf_op jit(solution)/shard_map/pallas_call | solution.py:960
  378.1 7.1 convolution_convert_fusion.7
  437.0 20.7 %shard_map.267 = (bf16[1024,1152]{1,0:T(8,128)(2,1)S(1)}, bf16[1024,384]{1,0:T(8,128)(2,1)S(1)}, f32[8,640]{1,0:T(8,128)S(1)}, f32[8,384]{1,0:T(8,128)S(1)}, f32[16,128]{1,0:T(8,128)S(1)}) custom-call(f32[1024,384]{1,0:T(8,128)S(1)} %fusion.159.refs_0_, f32[1024,1152]{1,0:T(8,128)S(1)} %bitcast.929, f32[1024,1152]{1,0:T(8,128)S(1)} %bitcast.929, ...), custom_call_target="tpu_custom_call" | custom-call | flops 30000001024 | bytes 16000000 | tf_op jit(solution)/shard_map/pallas_call | solution.py:960
  510.0 9.9 shard_map.264
  534.9 6.9 collective-permute-done.70
  576.7 9.8 shard_map.265
  657.9 20.3 %shard_map.268 = (bf16[1024,1152]{1,0:T(8,128)(2,1)S(1)}, bf16[1024,384]{1,0:T(8,128)(2,1)S(1)}, f32[8,640]{1,0:T(8,128)S(1)}, f32[8,384]{1,0:T(8,128)S(1)}, f32[16,128]{1,0:T(8,128)S(1)}) custom-call(f32[1024,384]{1,0:T(8,128)S(1)} %fusion.160.refs_0_, f32[1024,1152]{1,0:T(8,128)S(1)} %bitcast.931, f32[1024,1152]{1,0:T(8,128)S(1)} %bitcast.931, ...), custom_call_target="tpu_custom_call" | custom-call | flops 30000001024 | bytes 16000000 | tf_op jit(solution)/shard_map/pallas_call | solution.py:960
  709.0 20.3 %collective-permute-start.176 = (bf16[384,384]{1,0:T(8,128)(2,1)}, bf16[384,384]{1,0:T(8,128)(2,1)}, u32[]{:S(2)}, u32[]{:S(2)}) collective-permute-start(bf16[384,384]{1,0:T(8,128)(2,1)} %get-tuple-element.154), channel_id=1, source_target_pairs={{0,8},{8,16},{16,24},{24,0},{1,9},{9,17},{17,25},{25,1},{2,10},{10... | collective-permute-start | bytes 884744 | tf_op jit(solution)/shard_map/ppermute | solution.py:527
  749.2 10.1 collective-permute-start.166
  770.2 32.5 %collective-permute-done.165 = bf16[384,1024]{1,0:T(8,128)(2,1)} collective-permute-done((bf16[384,1024]{1,0:T(8,128)(2,1)}, bf16[384,1024]{1,0:T(8,128)(2,1)}, u32[]{:S(2)}, u32[]{:S(2)}) %collective-permute-start.165) | collective-permute-done | bytes 786464 | tf_op jit(solution)/shard_map/ppermute | solution.py:527
  873.6 20.4 %shard_map.269 = (bf16[1024,1152]{1,0:T(8,128)(2,1)S(1)}, bf16[1024,384]{1,0:T(8,128)(2,1)S(1)}, f32[8,640]{1,0:T(8,128)S(1)}, f32[8,384]{1,0:T(8,128)S(1)}, f32[16,128]{1,0:T(8,128)S(1)}) custom-call(f32[1024,384]{1,0:T(8,128)S(1)} %fusion.161.refs_0_, f32[1024,1152]{1,0:T(8,128)S(1)} %bitcast.927, f32[1024,1152]{1,0:T(8,128)S(1)} %bitcast.927, ...), custom_call_target="tpu_custom_call" | custom-call | flops 30000001024 | bytes 16000000 | tf_op jit(solution)/shard_map/pallas_call | solution.py:960
  910.5 20.1 %collective-permute-start.170 = (bf16[384,384]{1,0:T(8,128)(2,1)}, bf16[384,384]{1,0:T(8,128)(2,1)}, u32[]{:S(2)}, u32[]{:S(2)}) collective-permute-start(bf16[384,384]{1,0:T(8,128)(2,1)} %get-tuple-element.151), channel_id=1, source_target_pairs={{0,8},{8,16},{16,24},{24,0},{1,9},{9,17},{17,25},{25,1},{2,10},{10... | collective-permute-start | bytes 884744 | tf_op jit(solution)/shard_map/ppermute | solution.py:527
  936.6 10.5 convolution_add_fusion.1
  978.6 8.9 collective-permute-done.157
  987.5 35.0 %collective-permute-done.158 = bf16[384,1024]{1,0:T(8,128)(2,1)S(1)} collective-permute-done((bf16[384,1024]{1,0:T(8,128)(2,1)S(1)}, bf16[384,1024]{1,0:T(8,128)(2,1)S(1)}, u32[]{:S(2)}, u32[]{:S(2)}) %collective-permute-start.158) | collective-permute-done | bytes 786464 | tf_op jit(solution)/shard_map/ppermute | solution.py:527
  1061.9 17.2 %collective-permute-start.154 = (f32[192,128]{1,0:T(8,128)S(1)}, f32[192,128]{1,0:T(8,128)S(1)}, u32[]{:S(2)}, u32[]{:S(2)}) collective-permute-start(f32[192,128]{1,0:T(8,128)S(1)} %fusion.206), channel_id=1, source_target_pairs={{0,8},{8,0},{16,24},{24,16},{1,9},{9,1},{17,25},{25,17},{2,10},{10... | collective-permute-start | bytes 294920 | tf_op jit(solution)/shard_map/ppermute | solution.py:564
  (1171 shorter events, 720.6 us)
Async XLA Ops:
  3.1 48.4 %collective-permute-start.13 = (bf16[96,384]{1,0:T(8,128)(2,1)}, bf16[96,384]{1,0:T(8,128)(2,1)}, u32[]{:S(2)}, u32[]{:S(2)}) collective-permute-start(bf16[96,384]{1,0:T(8,128)(2,1)} %bitcast.23), channel_id=1, source_target_pairs={{0,8},{8,16},{16,24},{24,0},{1,9},{9,17},{17,25},{25,1},{2,10},{10... | collective-permute-start | bytes 221192 | tf_op jit(solution)/shard_map/ppermute | solution.py:527
  5.2 47.5 %collective-permute-start.14 = (bf16[96,384]{1,0:T(8,128)(2,1)}, bf16[96,384]{1,0:T(8,128)(2,1)}, u32[]{:S(2)}, u32[]{:S(2)}) collective-permute-start(bf16[96,384]{1,0:T(8,128)(2,1)} %bitcast.23), channel_id=1, source_target_pairs={{0,16},{8,24},{16,0},{24,8},{1,17},{9,25},{17,1},{25,9},{2,18},{10... | collective-permute-start | bytes 221192 | tf_op jit(solution)/shard_map/ppermute | solution.py:527
  7.5 46.4 %collective-permute-start.15 = (bf16[96,384]{1,0:T(8,128)(2,1)}, bf16[96,384]{1,0:T(8,128)(2,1)}, u32[]{:S(2)}, u32[]{:S(2)}) collective-permute-start(bf16[96,384]{1,0:T(8,128)(2,1)} %bitcast.23), channel_id=1, source_target_pairs={{0,24},{8,0},{16,8},{24,16},{1,25},{9,1},{17,9},{25,17},{2,26},{10... | collective-permute-start | bytes 221192 | tf_op jit(solution)/shard_map/ppermute | solution.py:527
  11.9 104.9 %collective-permute-start = (bf16[128,1536]{1,0:T(8,128)(2,1)S(1)}, bf16[128,1536]{1,0:T(8,128)(2,1)}, u32[]{:S(2)}, u32[]{:S(2)}) collective-permute-start(bf16[128,1536]{1,0:T(8,128)(2,1)S(1)} %fusion.24), channel_id=1, source_target_pairs={{0,1},{1,0},{2,3},{3,2},{4,5},{5,4},{6,7},{7,6},{8,9},{9,8},{10,11... | collective-permute-start | bytes 1179656 | tf_op jit(solution)/shard_map/ppermute | solution.py:473
  50.2 70.0 %collective-permute-start.1 = (bf16[128,1536]{1,0:T(8,128)(2,1)S(1)}, bf16[128,1536]{1,0:T(8,128)(2,1)S(1)}, u32[]{:S(2)}, u32[]{:S(2)}) collective-permute-start(bf16[128,1536]{1,0:T(8,128)(2,1)S(1)} %fusion.24), channel_id=1, source_target_pairs={{0,2},{1,5},{2,0},{3,7},{4,6},{5,1},{6,4},{7,3},{8,10},{9,13},{10,... | collective-permute-start | bytes 1179656 | tf_op jit(solution)/shard_map/ppermute | solution.py:469
  61.8 34.7 %collective-permute-start.56 = (bf16[384,384]{1,0:T(8,128)(2,1)S(1)}, bf16[384,384]{1,0:T(8,128)(2,1)S(1)}, u32[]{:S(2)}, u32[]{:S(2)}) collective-permute-start(bf16[384,384]{1,0:T(8,128)(2,1)S(1)} %bitcast.1026), channel_id=1, source_target_pairs={{0,16},{8,24},{16,0},{24,8},{1,17},{9,25},{17,1},{25,9},{2,18},{10... | collective-permute-start | bytes 884744 | tf_op jit(solution)/shard_map/ppermute | solution.py:527
  65.3 32.8 %collective-permute-start.29 = (bf16[384,384]{1,0:T(8,128)(2,1)S(1)}, bf16[384,384]{1,0:T(8,128)(2,1)S(1)}, u32[]{:S(2)}, u32[]{:S(2)}) collective-permute-start(bf16[384,384]{1,0:T(8,128)(2,1)S(1)} %bitcast.1029), channel_id=1, source_target_pairs={{0,8},{8,16},{16,24},{24,0},{1,9},{9,17},{17,25},{25,1},{2,10},{10... | collective-permute-start | bytes 884744 | tf_op jit(solution)/shard_map/ppermute | solution.py:527
  68.8 34.0 %collective-permute-start.30 = (bf16[384,384]{1,0:T(8,128)(2,1)S(1)}, bf16[384,384]{1,0:T(8,128)(2,1)S(1)}, u32[]{:S(2)}, u32[]{:S(2)}) collective-permute-start(bf16[384,384]{1,0:T(8,128)(2,1)S(1)} %bitcast.1030), channel_id=1, source_target_pairs={{0,16},{8,24},{16,0},{24,8},{1,17},{9,25},{17,1},{25,9},{2,18},{10... | collective-permute-start | bytes 884744 | tf_op jit(solution)/shard_map/ppermute | solution.py:527
  116.8 40.8 %collective-permute-start.11 = (bf16[384,768]{1,0:T(8,128)(2,1)S(1)}, bf16[384,768]{1,0:T(8,128)(2,1)S(1)}, u32[]{:S(2)}, u32[]{:S(2)}) collective-permute-start(bf16[384,768]{1,0:T(8,128)(2,1)S(1)} %bitcast.1000), channel_id=1, source_target_pairs={{0,16},{8,24},{16,0},{24,8},{1,17},{9,25},{17,1},{25,9},{2,18},{10... | collective-permute-start | bytes 1769480 | tf_op jit(solution)/shard_map/ppermute | solution.py:527
  125.3 34.4 %collective-permute-start.12 = (bf16[384,768]{1,0:T(8,128)(2,1)S(1)}, bf16[384,768]{1,0:T(8,128)(2,1)S(1)}, u32[]{:S(2)}, u32[]{:S(2)}) collective-permute-start(bf16[384,768]{1,0:T(8,128)(2,1)S(1)} %bitcast.1001), channel_id=1, source_target_pairs={{0,24},{8,0},{16,8},{24,16},{1,25},{9,1},{17,9},{25,17},{2,26},{10... | collective-permute-start | bytes 1769480 | tf_op jit(solution)/shard_map/ppermute | solution.py:527
  128.5 31.4 %collective-permute-start.2 = (bf16[128,1536]{1,0:T(8,128)(2,1)S(1)}, bf16[128,1536]{1,0:T(8,128)(2,1)S(1)}, u32[]{:S(2)}, u32[]{:S(2)}) collective-permute-start(bf16[128,1536]{1,0:T(8,128)(2,1)S(1)} %collective-permute-done.1), channel_id=1, source_target_pairs={{0,1},{1,0},{2,3},{3,2},{4,5},{5,4},{6,7},{7,6},{8,9},{9,8},{10,11... | collective-permute-start | bytes 1179656 | tf_op jit(solution)/shard_map/ppermute | solution.py:473
  129.4 30.4 %collective-permute-start.5 = (bf16[128,1536]{1,0:T(8,128)(2,1)S(1)}, bf16[128,1536]{1,0:T(8,128)(2,1)}, u32[]{:S(2)}, u32[]{:S(2)}) collective-permute-start(bf16[128,1536]{1,0:T(8,128)(2,1)S(1)} %collective-permute-done.1), channel_id=1, source_target_pairs={{0,4},{1,3},{2,6},{3,1},{4,0},{5,7},{6,2},{7,5},{8,12},{9,11},{10,... | collective-permute-start | bytes 1179656 | tf_op jit(solution)/shard_map/ppermute | solution.py:469
  131.5 28.5 %collective-permute-start.4 = (bf16[128,1536]{1,0:T(8,128)(2,1)S(1)}, bf16[128,1536]{1,0:T(8,128)(2,1)S(1)}, u32[]{:S(2)}, u32[]{:S(2)}) collective-permute-start(bf16[128,1536]{1,0:T(8,128)(2,1)S(1)} %collective-permute-done.3), channel_id=1, source_target_pairs={{0,1},{1,0},{2,3},{3,2},{4,5},{5,4},{6,7},{7,6},{8,9},{9,8},{10,11... | collective-permute-start | bytes 1179656 | tf_op jit(solution)/shard_map/ppermute | solution.py:473
  224.0 38.7 %collective-permute-start.47 = (bf16[384,768]{1,0:T(8,128)(2,1)}, bf16[384,768]{1,0:T(8,128)(2,1)S(1)}, u32[]{:S(2)}, u32[]{:S(2)}) collective-permute-start(bf16[384,768]{1,0:T(8,128)(2,1)} %bitcast.1003), channel_id=1, source_target_pairs={{0,16},{8,24},{16,0},{24,8},{1,17},{9,25},{17,1},{25,9},{2,18},{10... | collective-permute-start | bytes 1769480 | tf_op jit(solution)/shard_map/ppermute | solution.py:527
  224.0 39.6 %collective-permute-start.48 = (bf16[384,768]{1,0:T(8,128)(2,1)}, bf16[384,768]{1,0:T(8,128)(2,1)S(1)}, u32[]{:S(2)}, u32[]{:S(2)}) collective-permute-start(bf16[384,768]{1,0:T(8,128)(2,1)} %bitcast.1004), channel_id=1, source_target_pairs={{0,24},{8,0},{16,8},{24,16},{1,25},{9,1},{17,9},{25,17},{2,26},{10... | collective-permute-start | bytes 1769480 | tf_op jit(solution)/shard_map/ppermute | solution.py:527
  702.1 106.8 %collective-permute-start.131 = (bf16[4,128,1536]{2,1,0:T(8,128)(2,1)}, bf16[4,128,1536]{2,1,0:T(8,128)(2,1)}, u32[]{:S(2)}, u32[]{:S(2)}) collective-permute-start(bf16[4,128,1536]{2,1,0:T(8,128)(2,1)} %dynamic-slice_bitcast_fusion.1), channel_id=1, source_target_pairs={{0,1},{1,0},{2,3},{3,2},{4,5},{5,4},{6,7},{7,6},{8,9},{9,8},{10,11... | collective-permute-start | bytes 4718600 | tf_op jit(solution)/shard_map/ppermute | solution.py:473
  709.0 40.2 %collective-permute-start.176 = (bf16[384,384]{1,0:T(8,128)(2,1)}, bf16[384,384]{1,0:T(8,128)(2,1)}, u32[]{:S(2)}, u32[]{:S(2)}) collective-permute-start(bf16[384,384]{1,0:T(8,128)(2,1)} %get-tuple-element.154), channel_id=1, source_target_pairs={{0,8},{8,16},{16,24},{24,0},{1,9},{9,17},{17,25},{25,1},{2,10},{10... | collective-permute-start | bytes 884744 | tf_op jit(solution)/shard_map/ppermute | solution.py:527
  749.2 53.5 %collective-permute-start.165 = (bf16[384,1024]{1,0:T(8,128)(2,1)}, bf16[384,1024]{1,0:T(8,128)(2,1)}, u32[]{:S(2)}, u32[]{:S(2)}) collective-permute-start(bf16[384,1024]{1,0:T(8,128)(2,1)} %get-tuple-element.132), channel_id=1, source_target_pairs={{0,16},{8,24},{16,0},{24,8},{1,17},{9,25},{17,1},{25,9},{2,18},{10... | collective-permute-start | bytes 2359304 | tf_op jit(solution)/shard_map/ppermute | solution.py:527
  749.2 53.5 %collective-permute-start.166 = (bf16[384,1024]{1,0:T(8,128)(2,1)}, bf16[384,1024]{1,0:T(8,128)(2,1)}, u32[]{:S(2)}, u32[]{:S(2)}) collective-permute-start(bf16[384,1024]{1,0:T(8,128)(2,1)} %get-tuple-element.131), channel_id=1, source_target_pairs={{0,24},{8,0},{16,8},{24,16},{1,25},{9,1},{17,9},{25,17},{2,26},{10... | collective-permute-start | bytes 2359304 | tf_op jit(solution)/shard_map/ppermute | solution.py:527
  768.2 43.9 %collective-permute-start.181 = (bf16[96,384]{1,0:T(8,128)(2,1)S(1)}, bf16[96,384]{1,0:T(8,128)(2,1)S(1)}, u32[]{:S(2)}, u32[]{:S(2)}) collective-permute-start(bf16[96,384]{1,0:T(8,128)(2,1)S(1)} %get-tuple-element.195), channel_id=1, source_target_pairs={{0,6},{2,4},{4,2},{6,0},{1,7},{3,5},{5,3},{7,1},{8,14},{10,12},{12... | collective-permute-start | bytes 221192 | tf_op jit(solution)/shard_map/ppermute | solution.py:551
  910.5 46.6 %collective-permute-start.170 = (bf16[384,384]{1,0:T(8,128)(2,1)}, bf16[384,384]{1,0:T(8,128)(2,1)}, u32[]{:S(2)}, u32[]{:S(2)}) collective-permute-start(bf16[384,384]{1,0:T(8,128)(2,1)} %get-tuple-element.151), channel_id=1, source_target_pairs={{0,8},{8,16},{16,24},{24,0},{1,9},{9,17},{17,25},{25,1},{2,10},{10... | collective-permute-start | bytes 884744 | tf_op jit(solution)/shard_map/ppermute | solution.py:527
  956.7 69.3 %collective-permute-start.145 = (bf16[4,128,1536]{2,1,0:T(8,128)(2,1)}, bf16[4,128,1536]{2,1,0:T(8,128)(2,1)}, u32[]{:S(2)}, u32[]{:S(2)}) collective-permute-start(bf16[4,128,1536]{2,1,0:T(8,128)(2,1)} %dynamic-slice_bitcast_fusion), channel_id=1, source_target_pairs={{0,1},{1,0},{2,3},{3,2},{4,5},{5,4},{6,7},{7,6},{8,9},{9,8},{10,11... | collective-permute-start | bytes 4718600 | tf_op jit(solution)/shard_map/ppermute | solution.py:473
  970.8 51.7 %collective-permute-start.158 = (bf16[384,1024]{1,0:T(8,128)(2,1)S(1)}, bf16[384,1024]{1,0:T(8,128)(2,1)S(1)}, u32[]{:S(2)}, u32[]{:S(2)}) collective-permute-start(bf16[384,1024]{1,0:T(8,128)(2,1)S(1)} %get-tuple-element.129), channel_id=1, source_target_pairs={{0,16},{8,24},{16,0},{24,8},{1,17},{9,25},{17,1},{25,9},{2,18},{10... | collective-permute-start | bytes 2359304 | tf_op jit(solution)/shard_map/ppermute | solution.py:527
  970.8 51.7 %collective-permute-start.159 = (bf16[384,1024]{1,0:T(8,128)(2,1)S(1)}, bf16[384,1024]{1,0:T(8,128)(2,1)S(1)}, u32[]{:S(2)}, u32[]{:S(2)}) collective-permute-start(bf16[384,1024]{1,0:T(8,128)(2,1)S(1)} %get-tuple-element.128), channel_id=1, source_target_pairs={{0,24},{8,0},{16,8},{24,16},{1,25},{9,1},{17,9},{25,17},{2,26},{10... | collective-permute-start | bytes 2359304 | tf_op jit(solution)/shard_map/ppermute | solution.py:527
  (319 other events, 3144.8 us)

commit v2 on v1

--- a/solution.py
+++ b/solution.py
@@ -487,60 +487,32 @@
     return lax.dynamic_index_in_dim(array, index, axis, False)
 
 
-def group_gather(block):
-    place, core, near, far, across = places()
-    from_near, from_far = hop(block, 1, 2), hop(block, 2, 1)
-    from_across = hop(from_near, 2, 1)
-    out = jnp.zeros((4, 2) + block.shape, block.dtype)
-    for piece, own, other in (
-        (block, place, place),
-        (from_near, near, far),
-        (from_far, far, near),
-        (from_across, across, across),
-    ):
-        out = put(out, piece, own, core)
-        out = put(out, swap(piece), other, 1 - core)
-    return out
-
-
-def group_scatter(parts):
-    place, core, near, far, across = places()
-    arrived = swap(pick(parts, 1 - core, 1))
-    own = pick(parts, core, 1)
-
-    def both(index):
-        return pick(own, index).astype(F32) + pick(arrived, index).astype(F32)
-
-    side = both(near) + hop(both(across).astype(BF16), 2, 1).astype(F32)
-    here = both(place) + hop(both(far).astype(BF16), 2, 1).astype(F32)
-    return here + hop(side.astype(BF16), 1, 2).astype(F32)
-
-
-def group_sum(value):
-    for first, second in ((1, 2), (2, 1)):
-        value = value + hop(value, first, second)
-    return value + swap(value)
-
-
 def line_shift(value, axis, step):
     count = lax.axis_size(axis)
     return lax.ppermute(value, axis, [(i, (i + step) % count) for i in range(count)])
 
 
-def line_gather(block):
+def line_place(blocks, columns):
+    count, place, rows = lax.axis_size("dp"), lax.axis_index("dp"), blocks[0].shape[0]
+    out = jnp.zeros((count * rows, columns), blocks[0].dtype)
+    for step, block in enumerate(blocks):
+        out = lax.dynamic_update_slice(out, block, ((place - step) % count * rows, 0))
+    return out
+
+
+def line_near(block):
+    count = lax.axis_size("dp")
+    return jnp.stack([block] + [line_shift(block, "dp", step) for step in range(1, count)])
+
+
+def line_sum_steps(part):
     count, place = lax.axis_size("dp"), lax.axis_index("dp")
-    out = put(jnp.zeros((count,) + block.shape, block.dtype), block, place)
-    for step in range(1, count):
-        out = put(out, line_shift(block, "dp", step), (place - step) % count)
-    return out
-
-
-def line_scatter(parts):
-    count, place = lax.axis_size("dp"), lax.axis_index("dp")
-    total = pick(parts, place)
-    for step in range(1, count):
-        sent = pick(parts, (place + step) % count).astype(BF16)
-        total = total + line_shift(sent, "dp", step).astype(F32)
+    sent = [part((place + step) % count).astype(BF16) for step in range(1, count)]
+    got = [line_shift(value, "dp", step + 1) for step, value in enumerate(sent)]
+    token = yield sent
+    total = part(place)
+    for value in gate(got, token):
+        total = total + value.astype(F32)
     return total
 
 
@@ -553,17 +525,29 @@
     return out
 
 
-def mesh_sum(value):
-    for turn in (1, 2):
-        value = value + lax.ppermute(value, "seq", [(i, i ^ turn) for i in range(4)])
+def mesh_sum_steps(value):
     count = lax.axis_size("dp")
-    if count & (count - 1):
-        return lax.psum(value, "dp")
-    turn = 1
-    while turn < count:
-        value = value + lax.ppermute(value, "dp", [(i, i ^ turn) for i in range(count)])
-        turn *= 2
+    turns = [("seq", 4, 1), ("seq", 4, 2)]
+    turns += [("dp", count, 1 << bit) for bit in range(count.bit_length() - 1)]
+    for axis, size, turn in turns:
+        moved = lax.ppermute(value, axis, [(i, i ^ turn) for i in range(size)])
+        token = yield value
+        value = value + gate(moved, token)
     return value
+
+
+def trade_steps(parts):
+    place = lax.axis_index("seq")
+    sent = [pick(parts, place ^ turn) for turn in (1, 2, 3)]
+    got = [
+        lax.ppermute(value, "seq", [(i, i ^ turn) for i in range(4)])
+        for turn, value in zip((1, 2, 3), sent)
+    ]
+    token = yield sent
+    out = put(jnp.zeros_like(parts), pick(parts, place), place)
+    for turn, value in zip((1, 2, 3), gate(got, token)):
+        out = put(out, value, place ^ turn)
+    return out
 
 
 def dot(left, right, left_dim=1, right_dim=0):
@@ -659,6 +643,7 @@
 
 def forward_kernel(
     head_size,
+    order_ref,
     raw_ref,
     taps_ref,
     chans_ref,
@@ -732,6 +717,7 @@
 def backward_kernel(
     head_size,
     inner_count,
+    order_ref,
     grad_ref,
     raw_ref,
     past_ref,
@@ -745,7 +731,6 @@
     upper_ref,
     picker_ref,
     back_ref,
-    normed_ref,
     taps_out,
     chans_out,
     heads_out,
@@ -786,7 +771,6 @@
     gated = mixed * gate_silu
     grad = grad_ref[...]
     scaled_gated = gated * scale
-    normed_ref[...] = (scaled_gated * gain).astype(BF16)
     gain_term = jnp.sum(grad * scaled_gated, axis=0, keepdims=True)
     grad_gated = scale * (grad * gain) - gated * (scale * scale * scale * inner / inner_count)
     grad_mixed = grad_gated * gate_silu
@@ -902,51 +886,54 @@
 
 
 def fixed(shape):
-    return pl.BlockSpec(shape, lambda i: (0,) * len(shape))
-
-
-def mix_forward(raw, small, tabs, head_size, width, state):
+    return pl.BlockSpec(shape, lambda i, order: (0,) * len(shape))
+
+
+def mix_forward(raw, order, small, tabs, head_size, width, state):
     taps, chans, heads = small
     spread, upper, _ = tabs
     tokens, columns = raw.shape
     count = tokens // STRETCH
     return pl.pallas_call(
         lambda *refs: forward_kernel(head_size, *refs),
-        grid=(count,),
-        in_specs=[
-            pl.BlockSpec((STRETCH, columns), lambda i: (i, 0)),
-            fixed(taps.shape),
-            fixed(chans.shape),
-            fixed(heads.shape),
-            fixed(spread.shape),
-            fixed(upper.shape),
-        ],
-        out_specs=[
-            pl.BlockSpec((STRETCH, width), lambda i: (i, 0)),
-            pl.BlockSpec((ROWS, LANES), lambda i: (i, 0)),
-            pl.BlockSpec((STRETCH, width), lambda i: (i, 0)),
-            pl.BlockSpec((None, width, state), lambda i: (i, 0, 0)),
-        ],
+        grid_spec=pltpu.PrefetchScalarGridSpec(
+            num_scalar_prefetch=1,
+            grid=(count,),
+            in_specs=[
+                pl.BlockSpec((STRETCH, columns), lambda i, order: (order[i], 0)),
+                fixed(taps.shape),
+                fixed(chans.shape),
+                fixed(heads.shape),
+                fixed(spread.shape),
+                fixed(upper.shape),
+            ],
+            out_specs=[
+                pl.BlockSpec((STRETCH, width), lambda i, order: (order[i], 0)),
+                pl.BlockSpec((ROWS, LANES), lambda i, order: (i, 0)),
+                pl.BlockSpec((STRETCH, width), lambda i, order: (i, 0)),
+                pl.BlockSpec((None, width, state), lambda i, order: (i, 0, 0)),
+            ],
+            scratch_shapes=[
+                pltpu.VMEM((width, state), F32),
+                pltpu.VMEM((STRETCH + ROWS, width + 2 * state), F32),
+            ],
+        ),
         out_shape=[
             jax.ShapeDtypeStruct((tokens, width), BF16),
             jax.ShapeDtypeStruct((count * ROWS, LANES), F32),
             jax.ShapeDtypeStruct((tokens, width), F32),
             jax.ShapeDtypeStruct((count, width, state), F32),
         ],
-        scratch_shapes=[
-            pltpu.VMEM((width, state), F32),
-            pltpu.VMEM((STRETCH + ROWS, width + 2 * state), F32),
-        ],
         compiler_params=pltpu.CompilerParams(
             dimension_semantics=("arbitrary",), vmem_limit_bytes=40 * 2**20
         ),
         cost_estimate=pl.CostEstimate(
-            flops=15_000_000_000, bytes_accessed=10_000_000, transcendentals=0
+            flops=11_000_000_000, bytes_accessed=10_000_000, transcendentals=0
         ),
-    )(raw, taps, chans, heads, spread, upper)
-
-
-def mix_backward(grad, raw, mixed, states, token_rows, small, tabs, head_size, inner_count):
+    )(order, raw, taps, chans, heads, spread, upper)
+
+
+def mix_backward(grad, raw, mixed, states, token_rows, order, small, tabs, head_size, inner_count):
     taps, chans, heads = small
     spread, upper, picker = tabs
     tokens, columns = raw.shape
@@ -954,56 +941,272 @@
     count = tokens // STRETCH
     per = STRETCH // ROWS
 
-    def back(i):
+    def moved(i, order):
+        return (order[count - 1 - i], 0)
+
+    def back(i, order):
         return (count - 1 - i, 0)
+
+    def past(i, order):
+        return (order[jnp.maximum(count - 2 - i, 0)] * per + per - 1, 0)
 
     return pl.pallas_call(
         lambda *refs: backward_kernel(head_size, inner_count, *refs),
-        grid=(count,),
-        in_specs=[
-            pl.BlockSpec((STRETCH, width), back),
-            pl.BlockSpec((STRETCH, columns), back),
-            pl.BlockSpec((ROWS, columns), lambda i: (jnp.maximum((count - 1 - i) * per - 1, 0), 0)),
-            pl.BlockSpec((STRETCH, width), back),
-            pl.BlockSpec((None, width, state), lambda i: (count - 1 - i, 0, 0)),
-            pl.BlockSpec((ROWS, LANES), back),
-            fixed(taps.shape),
-            fixed(chans.shape),
-            fixed(heads.shape),
-            fixed(spread.shape),
-            fixed(upper.shape),
-            fixed(picker.shape),
-        ],
-        out_specs=[
-            pl.BlockSpec((STRETCH, columns), back),
-            pl.BlockSpec((STRETCH, width), back),
-            fixed(taps.shape),
-            fixed(chans.shape),
-            fixed(heads.shape),
-        ],
+        grid_spec=pltpu.PrefetchScalarGridSpec(
+            num_scalar_prefetch=1,
+            grid=(count,),
+            in_specs=[
+                pl.BlockSpec((STRETCH, width), moved),
+                pl.BlockSpec((STRETCH, columns), moved),
+                pl.BlockSpec((ROWS, columns), past),
+                pl.BlockSpec((STRETCH, width), back),
+                pl.BlockSpec((None, width, state), lambda i, order: (count - 1 - i, 0, 0)),
+                pl.BlockSpec((ROWS, LANES), back),
+                fixed(taps.shape),
+                fixed(chans.shape),
+                fixed(heads.shape),
+                fixed(spread.shape),
+                fixed(upper.shape),
+                fixed(picker.shape),
+            ],
+            out_specs=[
+                pl.BlockSpec((STRETCH, columns), moved),
+                fixed(taps.shape),
+                fixed(chans.shape),
+                fixed(heads.shape),
+            ],
+            scratch_shapes=[
+                pltpu.VMEM((width, state), F32),
+                pltpu.VMEM((STRETCH + ROWS, width + 2 * state), F32),
+                pltpu.VMEM((STRETCH + ROWS, width + 2 * state), F32),
+            ],
+        ),
         out_shape=[
             jax.ShapeDtypeStruct((tokens, columns), BF16),
-            jax.ShapeDtypeStruct((tokens, width), BF16),
             jax.ShapeDtypeStruct(taps.shape, F32),
             jax.ShapeDtypeStruct(chans.shape, F32),
             jax.ShapeDtypeStruct(heads.shape, F32),
-        ],
-        scratch_shapes=[
-            pltpu.VMEM((width, state), F32),
-            pltpu.VMEM((STRETCH + ROWS, width + 2 * state), F32),
-            pltpu.VMEM((STRETCH + ROWS, width + 2 * state), F32),
         ],
         compiler_params=pltpu.CompilerParams(
             dimension_semantics=("arbitrary",), vmem_limit_bytes=40 * 2**20
         ),
         cost_estimate=pl.CostEstimate(
-            flops=30_000_000_000, bytes_accessed=16_000_000, transcendentals=0
+            flops=23_000_000_000, bytes_accessed=16_000_000, transcendentals=0
         ),
-    )(grad, raw, raw, mixed, states, token_rows, taps, chans, heads, spread, upper, picker)
+    )(order, grad, raw, raw, mixed, states, token_rows, taps, chans, heads, spread, upper, picker)
+
+
+def small_kernel(layers, heads_here, head_count, state, spot_ref, place_ref, arrived_ref, out_ref):
+    share = arrived_ref.shape[1]
+    rows = share // layers
+    row = lax.broadcasted_iota(jnp.int32, (LANES, LANES), 0)
+    lane = lax.broadcasted_iota(jnp.int32, (LANES, LANES), 1)
+    chosen = []
+    for layer in range(layers):
+        source = lane + layer * heads_here + place_ref[0] * head_count
+        chosen.append(((row == source) & (lane < head_count)).astype(BF16))
+    for index in range(out_ref.shape[1] // share):
+        pair = [arrived_ref[spot_ref[2 * index + which]] for which in range(2)]
+        own = jnp.where(place_ref[1] == 0, pair[0][:, 2 * state :], pair[1][:, 2 * state :])
+        turned = jnp.concatenate([own.astype(F32), jnp.zeros((LANES - share, LANES), F32)], axis=0)
+        turned = jnp.transpose(turned)[:share].astype(BF16)
+        spot = index * share
+        for layer in range(layers):
+            cut = slice(layer * rows, (layer + 1) * rows)
+            out_ref[layer, spot : spot + rows, : 2 * state] = pair[0][cut, : 2 * state]
+            out_ref[layer, spot + rows : spot + share, : 2 * state] = pair[1][cut, : 2 * state]
+            out_ref[layer, spot : spot + share, 2 * state :] = dot(turned, chosen[layer]).astype(BF16)
+
+
+def small_unpack(arrived, order, layers, heads_here, head_count, state):
+    line, share, columns = arrived.shape[0] // 8, arrived.shape[1], arrived.shape[2]
+    place, core = lax.axis_index("seq"), lax.axis_index("tensor")
+    back = (lax.axis_index("dp") - jnp.arange(line)) % line
+    spots = (order[None, :] * line + back[:, None]).reshape(-1).astype(jnp.int32)
+    scalars = pl.BlockSpec(memory_space=pltpu.SMEM)
+    return pl.pallas_call(
+        lambda *refs: small_kernel(layers, heads_here, head_count, state, *refs),
+        in_specs=[scalars, scalars, pl.BlockSpec(memory_space=pltpu.VMEM)],
+        out_shape=jax.ShapeDtypeStruct((layers, line * 4 * share, columns), BF16),
+        compiler_params=pltpu.CompilerParams(vmem_limit_bytes=40 * 2**20),
+    )(spots, jnp.stack([place, core]).astype(jnp.int32), arrived)
+
+
+def finish_kernel(
+    head_count, state, first_ref, second_ref, first_out, second_out, inner_ref, out_ref, state_ref, rate_ref
+):
+    width = out_ref.shape[2] // 4
+    share = out_ref.shape[1]
+    for layer, (ref, more) in enumerate(((first_ref, first_out), (second_ref, second_out))):
+        states = jnp.zeros((share, 2 * state), F32)
+        rates = []
+        for index in range(4):
+            value = ref[index].astype(F32)
+            spot = slice(index * width, (index + 1) * width)
+            inner_ref[layer, 0, :, spot] = value[:, :width]
+            inner_ref[layer, 1, :, spot] = value[:, width : 2 * width]
+            states = states + value[:, 2 * width : 2 * width + 2 * state]
+            rate = jnp.concatenate(
+                [value[:, 2 * width + 2 * state :], jnp.zeros((LANES - share, LANES), F32)], axis=0
+            )
+            rates.append(jnp.transpose(rate)[:head_count, :share])
+            out_ref[layer, :, spot] = more[index].astype(F32)
+        rate_ref[layer] = jnp.concatenate(rates, axis=0)
+        state_ref[layer] = states
+
+
+def finish(first, second, first_out, second_out, head_count, state, width):
+    share = first.shape[1]
+    return pl.pallas_call(
+        lambda *refs: finish_kernel(head_count, state, *refs),
+        out_shape=[
+            jax.ShapeDtypeStruct((2, 2, share, 4 * width), F32),
+            jax.ShapeDtypeStruct((2, share, 4 * width), F32),
+            jax.ShapeDtypeStruct((2, share, 2 * state), F32),
+            jax.ShapeDtypeStruct((2, 4 * head_count, share), F32),
+        ],
+        compiler_params=pltpu.CompilerParams(vmem_limit_bytes=40 * 2**20),
+    )(first, second, first_out, second_out)
 
 
 def norm_scale(hidden):
     return lax.rsqrt(jnp.mean(hidden * hidden, axis=1, keepdims=True) + EPSILON)
+
+
+PLAN = (
+    "v a l ga",
+    "gb a v a",
+    "b ga gb a",
+    "b a b ga",
+    "gb a b a",
+    "b a b l",
+    "a b a b",
+    "a b a b",
+    "a b a b",
+    "a b a b",
+    "a b a b",
+    "a b oa1 a",
+    "b xo a b",
+    "a ob1 b a",
+    "q ia1 b xo",
+    "a b ib1 r",
+    "a b oa0 a",
+    "b a a b",
+    "ob0 y ia0 b",
+    "ib0 u a b",
+    "a m b y",
+    "q m b q",
+    "m y b xg",
+    "m r m r",
+    "xg m u u",
+)
+
+
+def gate(value, token):
+    return value if token is None else lax.optimization_barrier((value, token))[0]
+
+
+def gather_steps(block):
+    from_near, from_far = hop(block, 1, 2), hop(block, 2, 1)
+    token = yield block
+    from_near = gate(from_near, token)
+    from_across = hop(from_near, 2, 1)
+    token = yield from_near
+    four = jnp.stack([block, from_near, gate(from_far, token), gate(from_across, token)])
+    twin = swap(four)
+    token = yield four
+    return jnp.concatenate([four, gate(twin, token)])
+
+
+def scatter_steps(own, other, tiny=None):
+    got = swap(other)
+    moved = None if tiny is None else hop(tiny, 1, 2)
+    token = yield other
+    got = gate(got, token)
+    to_far = (own[2:].astype(F32) + got[2:].astype(F32)).astype(BF16)
+    from_far = hop(to_far, 2, 1)
+    if tiny is not None:
+        tiny = tiny + gate(moved, token)
+        moved = hop(tiny, 2, 1)
+    token = yield to_far
+    from_far = gate(from_far, token)
+    both = own[:2].astype(F32) + got[:2].astype(F32) + from_far.astype(F32)
+    side = both[1].astype(BF16)
+    from_near = hop(side, 1, 2)
+    if tiny is not None:
+        tiny = tiny + gate(moved, token)
+        moved = swap(tiny)
+    token = yield (side, both[0])
+    total = both[0] + gate(from_near, token).astype(F32)
+    if tiny is not None:
+        tiny = tiny + gate(moved, token)
+    return total, tiny
+
+
+def arrival_order():
+    place, core = lax.axis_index("seq"), lax.axis_index("tensor")
+    block = jnp.arange(8)
+    turn, their = block // 2 ^ place, block % 2
+    first = jnp.where(their == 0, turn, jnp.where(turn == 1, 2, jnp.where(turn == 2, 1, turn)))
+    return (first + jnp.where(their == core, 0, 4)).astype(jnp.int32)
+
+
+class Track:
+    def __init__(self):
+        self.token = None
+        self.chains = {}
+
+    def begin(self, name, chain):
+        next(chain)
+        self.chains[name] = chain
+
+    def run(self, *plan):
+        for name in " ".join(plan).split():
+            name, _, count = name.partition("*")
+            for _ in range(int(count or 1)):
+                try:
+                    self.token = self.chains[name].send(self.token)
+                except StopIteration:
+                    pass
+
+
+def late_gather(store, key, block):
+    token = yield None
+    store[key] = yield from gather_steps(gate(block, token))
+
+
+def kept_result(store, key, chain):
+    yield None
+    store[key] = yield from chain
+
+
+def together(main, side):
+    token = yield (next(main), next(side))
+    result, running = None, [True, True]
+    while any(running):
+        values = []
+        for index, chain in enumerate((main, side)):
+            if running[index]:
+                try:
+                    values.append(chain.send(token))
+                except StopIteration as stop:
+                    running[index] = False
+                    result = stop.value if index == 0 else result
+        if any(running):
+            token = yield tuple(values)
+    return result
+
+
+def sum_steps(value, store, key):
+    moved = hop(value, 1, 2)
+    token = yield value
+    value = value + gate(moved, token)
+    moved = hop(value, 2, 1)
+    token = yield value
+    value = value + gate(moved, token)
+    moved = swap(value)
+    token = yield value
+    store[key] = value + gate(moved, token)
 
 
 def head_body(
@@ -1037,7 +1240,14 @@
     length = own_rows * 8
     conv_width = width + 2 * state
     columns = 2 * width + 2 * state + LANES
+    heads_here = rate_weight.shape[2]
     tabs = tables(width, head_size)
+
+    def own(array):
+        return lax.dynamic_slice_in_dim(array, core * own_rows, own_rows, 0)
+
+    def quarter(array, count):
+        return lax.dynamic_slice_in_dim(array, place * count, count, array.ndim - 1)
 
     def out_share(layer):
         turned = out_weight[layer].T.reshape(share, 4, width)
@@ -1047,214 +1257,361 @@
         cut = inner_weight[layer].reshape(share, 2, 4, width)
         return cut.transpose(2, 0, 1, 3).reshape(4, share, 2 * width)
 
-    def whole(parts):
-        traded = seq_trade(parts)
-        return line_gather(traded.reshape(4 * share, -1)).reshape(line * 4 * share, -1)
-
-    heads_here = rate_weight.shape[2]
-    rate_flat = rate_weight.reshape(layers, state_share, -1)
-    rate_flat = jnp.pad(rate_flat, ((0, 0), (0, 0), (0, LANES - rate_flat.shape[2])))
-    small_share = jnp.concatenate([state_weight, rate_flat], axis=2)
-    small_line = line_gather(small_share.reshape(layers * state_share, -1))
-    small_all = group_gather(small_line.reshape(line * layers * state_share, -1))
-    small_all = small_all.reshape(4, 2, line, layers, state_share, -1)
-    state_full = small_all[..., : 2 * state].transpose(3, 2, 0, 1, 4, 5).reshape(layers, model, -1)
-    rate_half = pick(small_all, core, 1)[..., 2 * state : 2 * state + 2 * heads_here]
-    rate_half = rate_half.reshape(4, line, layers, share, heads_here)
-    rate_own = lax.dynamic_slice_in_dim(rate_half, place * head_count, head_count, 4)
-    rate_own = rate_own.transpose(2, 1, 0, 3, 4).reshape(layers, model, head_count)
-    rate_own = jnp.pad(rate_own, ((0, 0), (0, 0), (0, LANES - head_count)))
-
-    in_weights, out_weights = [], []
-    for layer in range(layers):
-        inner_full = whole(inner_share(layer))
-        in_weights.append(
-            jnp.concatenate([inner_full, state_full[layer], rate_own[layer]], axis=1)
+    def first_for(taker):
+        cut = lax.dynamic_slice(inner_weight[0], (0, 0, taker * width), (share, 2, width))
+        return jnp.concatenate([cut[:, 0], cut[:, 1]], axis=1)
+
+    out_weights, in_weights = {}, {}
+
+    def first_out():
+        token = yield None
+        traded = yield from trade_steps(gate(out_share(0), token))
+        traded = traded.reshape(4 * share, width)
+        got = [line_shift(traded, "dp", step) for step in range(1, line)]
+        token = yield traded
+        out_weights[0] = line_place([traded] + gate(got, token), width)
+
+    def later(layer):
+        token = yield None
+        mixed_share = jnp.concatenate([inner_share(layer), out_share(layer)], axis=2)
+        traded = yield from trade_steps(gate(mixed_share, token))
+        full = lax.all_gather(traded.reshape(4 * share, -1), "dp").reshape(model, -1)
+        token = yield traded
+        full = gate(full, token)
+        out_weights[layer] = full[:, 2 * width :]
+        in_weights[layer] = jnp.concatenate([full[:, : 2 * width], small_full[layer]], axis=1)
+        yield in_weights[layer]
+
+    first = put(jnp.zeros((4, share, 2 * width), BF16), first_for(place), place)
+    first_sent = [first_for(place ^ turn) for turn in (1, 2, 3)]
+    for turn, value in zip((1, 2, 3), first_sent):
+        pairs = [(i, i ^ turn) for i in range(4)]
+        first = put(first, lax.ppermute(value, "seq", pairs), place ^ turn)
+    first = first.reshape(4 * share, 2 * width)
+    rate_rows = rate_weight.transpose(0, 2, 1).reshape(layers * heads_here, share)
+    rate_rows = jnp.pad(rate_rows, ((0, share - layers * heads_here), (0, LANES - share)))
+    small_share = jnp.concatenate([state_weight.reshape(share, 2 * state), rate_rows], axis=1)
+    small_near = line_near(small_share)
+
+    smalls = []
+
+    def prepare():
+        token = yield None
+        given = (conv_inner, conv_state, bias_inner, bias_state, skip_gain, gate_gain, rate_bias, decay_log)
+        (
+            conv_inner_,
+            conv_state_,
+            bias_inner_,
+            bias_state_,
+            skip_gain_,
+            gate_gain_,
+            rate_bias_,
+            decay_log_,
+        ) = gate(given, token)
+        for layer in range(layers):
+            taps = jnp.concatenate([quarter(conv_inner_[layer], width), conv_state_[layer]], axis=1)
+            bias = jnp.concatenate([quarter(bias_inner_[layer], width), bias_state_[layer]])
+            taps = jnp.concatenate([taps, bias[None], jnp.zeros((3, conv_width), F32)], axis=0)
+            skip = jnp.repeat(quarter(skip_gain_[layer], head_count), head_size)
+            chans = jnp.stack([skip, quarter(gate_gain_[layer], width)])
+            chans = jnp.concatenate([chans, jnp.zeros((ROWS - 2, width), F32)], axis=0)
+            heads = jnp.stack(
+                [quarter(rate_bias_[layer], head_count), quarter(decay_log_[layer], head_count)]
+            )
+            heads = jnp.pad(heads, ((0, 0), (0, ROWS - head_count))).reshape(2 * ROWS, 1)
+            smalls.append((taps, chans, jnp.broadcast_to(heads, (2 * ROWS, LANES))))
+        yield smalls
+
+    order = arrival_order()
+    track = Track()
+    track.token = (first_sent, small_share)
+    hiddens = [own(tokens[batch, 0]).astype(F32) for batch in range(batches)]
+    row_scales, normed_all, whole = [], {}, {}
+    for batch in range(batches):
+        row_scales.append(norm_scale(hiddens[batch]))
+        normed = (hiddens[batch] * row_scales[batch] * norm_gain[0][None, :]).astype(BF16)
+        normed = gate(normed, track.token)
+        track.begin(str(batch), kept_result(normed_all, (0, batch), gather_steps(normed)))
+    track.begin("s", kept_result(whole, "small", gather_steps(gate(small_near, first))))
+    track.begin("p", prepare())
+    grads, grad_all = [], {}
+    for batch, name in enumerate(("ga", "gb")):
+        low_part = own(gate(cotangent[batch, 0], first_sent))
+        grads.append(low_part.astype(F32))
+        track.begin(name, late_gather(grad_all, (layers - 1, batch), low_part))
+    track.run("0 1")
+    first_got = [line_shift(first, "dp", step) for step in range(1, line)]
+    track.token = first
+    track.run("s")
+    track.token = first_got[0]
+    track.run("0 1 s p", "0 1 s ga", "gb 0 1 s")
+    track.begin("v", first_out())
+    track.begin("l", later(1))
+    track.run("v l")
+    first_full = line_place(gate([first] + first_got, track.token), columns)
+    small_full = small_unpack(
+        whole["small"].reshape(-1, share, small_share.shape[1]),
+        order,
+        layers,
+        heads_here,
+        head_count,
+        state,
+    )
+    in_weights[0] = lax.dynamic_update_slice(first_full, small_full[0], (0, 2 * width))
+    track.token = first_full
+    gradients, inners, terms, outputs = {}, {}, {}, {}
+
+    def inner_products(grad_low, summed):
+        inner = jnp.sum(grad_low.astype(F32) * summed, axis=1)
+        return put(jnp.zeros((8, own_rows), F32), inner, place * 2 + core)
+
+    moves = order[None, :] == jnp.arange(8)[:, None]
+
+    def halves_of(value, weight):
+        half = length // 2
+        other = dot(value[half:], weight, 1, 1).astype(BF16)
+        return (
+            dot(value[:half], weight, 1, 1).astype(BF16).reshape(4, own_rows, model),
+            other.reshape(4, own_rows, model),
         )
-        out_weights.append(whole(out_share(layer)))
-
-    def quarter(array, count):
-        return lax.dynamic_slice_in_dim(array, place * count, count, array.ndim - 1)
-
-    smalls = []
-    for layer in range(layers):
-        taps = jnp.concatenate([quarter(conv_inner[layer], width), conv_state[layer]], axis=1)
-        bias = jnp.concatenate([quarter(bias_inner[layer], width), bias_state[layer]])
-        taps = jnp.concatenate([taps, bias[None], jnp.zeros((3, conv_width), F32)], axis=0)
-        skip = jnp.repeat(quarter(skip_gain[layer], head_count), head_size)
-        chans = jnp.stack([skip, quarter(gate_gain[layer], width)])
-        chans = jnp.concatenate([chans, jnp.zeros((ROWS - 2, width), F32)], axis=0)
-        heads = jnp.stack([quarter(rate_bias[layer], head_count), quarter(decay_log[layer], head_count)])
-        heads = jnp.pad(heads, ((0, 0), (0, ROWS - head_count))).reshape(2 * ROWS, 1)
-        smalls.append((taps, chans, jnp.broadcast_to(heads, (2 * ROWS, LANES))))
-
-    def own(array):
-        return lax.dynamic_slice_in_dim(array, core * own_rows, own_rows, 0)
-
-    results, kept = [], [[None] * layers for _ in range(batches)]
-    hiddens = [own(tokens[batch, 0]).astype(F32) for batch in range(batches)]
-    for layer in range(layers):
-        for batch in range(batches):
-            hidden = hiddens[batch]
-            row_scale = norm_scale(hidden)
-            normed_own = (hidden * row_scale * norm_gain[layer][None, :]).astype(BF16)
-            normed = group_gather(normed_own).reshape(length, model)
-            raw = dot(normed, in_weights[layer])
+
+    def batch_chain(batch):
+        token = yield None
+        hidden, row_scale = hiddens[batch], row_scales[batch]
+        normed = normed_all[0, batch]
+        kept = {}
+        for layer in range(layers):
+            normed = normed.reshape(length, model)
+            raw = dot(gate(normed, token), in_weights[layer])
+            token = yield raw
             value, squares, mixed, states = mix_forward(
-                raw, smalls[layer], tabs, head_size, width, state
+                gate(raw, token), order, smalls[layer], tabs, head_size, width, state
             )
-            partial = dot(value, out_weights[layer], 1, 1).astype(BF16)
-            summed = group_scatter(partial.reshape(4, 2, own_rows, model))
-            squares = group_sum(squares.reshape(-1, ROWS, LANES)[:, 0])
+            token = yield value
+            halves = halves_of(gate(value, token), out_weights[layer])
+            summed, squares = yield from scatter_steps(
+                *halves, squares.reshape(-1, ROWS, LANES)[:, 0]
+            )
             scales = lax.rsqrt(squares / inner_count + EPSILON)
-            own_scale = pick(scales.reshape(8, own_rows), place * 2 + core)[:, None]
-            kept[batch][layer] = (hidden, row_scale, normed, raw, mixed, states, summed, scales)
-            hiddens[batch] = hidden + own_scale * summed
-    results = hiddens
-
-    grads = [own(cotangent[batch, 0]).astype(F32) for batch in range(batches)]
-    big, small_sums = [None] * layers, [None] * layers
-    for layer in reversed(range(layers)):
-        sums = None
-        for batch in range(batches):
-            hidden, row_scale, normed, raw, mixed, states, summed, scales = kept[batch][layer]
-            grad_hidden = grads[batch]
-            grad_low = grad_hidden.astype(BF16)
-            inner_own = jnp.sum(grad_low.astype(F32) * summed, axis=1)
-            inner = jnp.zeros((8, own_rows), F32)
-            inner = put(inner, inner_own, place * 2 + core)
-            inner = group_sum(inner).reshape(-1, LANES)
-            token_rows = jnp.stack([scales, inner], axis=1)
+            flat_scales = scales.reshape(8, own_rows)
+            own_scale = pick(flat_scales, place * 2 + core)[:, None]
+            arrived = jnp.sum(jnp.where(moves[:, :, None], flat_scales[None], 0.0), axis=1)
+            normed_out = (value.astype(F32) * arrived.reshape(length, 1)).astype(BF16)
+            kept[layer] = (hidden, row_scale, normed, raw, mixed, states, summed, scales, normed_out)
+            hidden = hidden + own_scale * summed
+            if layer + 1 < layers:
+                row_scale = norm_scale(hidden)
+                normed = (hidden * row_scale * norm_gain[layer + 1][None, :]).astype(BF16)
+                normed = yield from gather_steps(normed)
+                token = None
+        outputs[batch] = hidden
+        grad_hidden = grads[batch]
+        top_inner = inner_products(grad_hidden.astype(BF16), kept[layers - 1][6])
+        yield from sum_steps(top_inner, inners, (layers - 1, batch))
+        token = None
+        for layer in reversed(range(layers)):
+            hidden, row_scale, normed, raw, mixed, states, summed, scales, normed_out = kept[layer]
+            whole_grad = grad_all[layer, batch].reshape(length, model)
+            terms[layer, batch] = [whole_grad, normed_out, normed, None]
+            grad_value = dot(gate(whole_grad, token), out_weights[layer])
+            token = yield grad_value
+            token_rows = jnp.stack([scales, inners[layer, batch].reshape(-1, LANES)], axis=1)
             token_rows = jnp.pad(token_rows, ((0, 0), (0, ROWS - 2), (0, 0)))
-            grad_all = group_gather(grad_low).reshape(length, model)
-            grad_value = dot(grad_all, out_weights[layer])
-            back, normed_out, taps_grad, chans_grad, heads_grad = mix_backward(
-                grad_value,
+            back, taps_grad, chans_grad, heads_grad = mix_backward(
+                gate(grad_value, token),
                 raw,
                 mixed,
                 states,
                 token_rows.reshape(-1, LANES),
+                order,
                 smalls[layer],
                 tabs,
                 head_size,
                 inner_count,
             )
-            partial = dot(back, in_weights[layer], 1, 1).astype(BF16)
-            grad_normed = group_scatter(partial.reshape(4, 2, own_rows, model))
-            gain_term = jnp.sum(grad_normed * hidden * row_scale, axis=0)
+            terms[layer, batch][3] = back
+            token = yield back
+            halves = halves_of(gate(back, token), in_weights[layer])
+            gain_term = sum(
+                jnp.sum(part.reshape(-1, model).astype(F32) * cut.astype(F32), axis=0)
+                for part, cut in zip(halves, (normed[: length // 2], normed[length // 2 :]))
+            )
+            gradients[layer, batch] = (
+                taps_grad,
+                chans_grad,
+                heads_grad,
+                gain_term / norm_gain[layer],
+            )
+            grad_normed, _ = yield from scatter_steps(*halves)
             weighted = grad_normed * norm_gain[layer][None, :]
             mean = jnp.mean(weighted * hidden, axis=1, keepdims=True)
-            grads[batch] = (
+            grad_hidden = (
                 grad_hidden
                 + row_scale * weighted
                 - hidden * (row_scale * row_scale * row_scale) * mean
             )
-            out_term = dot(grad_all, normed_out, 0, 0)
-            in_term = dot(normed, back, 0, 0)
-            new = (in_term, out_term, taps_grad, chans_grad, heads_grad, gain_term)
-            sums = new if sums is None else tuple(a + b for a, b in zip(sums, new))
-        big[layer] = sums[:2]
-        small_sums[layer] = sums[2:]
-
-    def traded(total, cut):
-        return seq_trade(total[:, :cut].reshape(4, share, cut).astype(BF16)).astype(F32)
-
-    inner_grads, rate_grads, state_grads, out_grads = [], [], [], []
-    for layer in range(layers):
-        in_sum, out_sum = big[layer]
-        out_total = line_scatter(out_sum.reshape(line, 4 * share, width))
-        out_here = traded(out_total, width)
-        out_grads.append(out_here.transpose(1, 0, 2).reshape(share, half_width).T)
-        states_part = in_sum[:, 2 * width : 2 * width + 2 * state]
-        states_part = states_part.reshape(line * 4, 2, state_share, 2 * state)
-        sent = swap(pick(states_part, 1 - core, 1).astype(BF16))
-        states_part = pick(states_part, core, 1) + sent.astype(F32)
-        states_part = states_part.reshape(line, 4 * share, state)
-        in_part = in_sum.reshape(line, 4 * share, columns)
-        packed = jnp.concatenate(
-            [in_part[..., : 2 * width], states_part, in_part[..., 2 * width + 2 * state :]], axis=2
-        )
-        total = line_scatter(packed)
-        here = traded(total, total.shape[1])
-        inner_here = here[..., : 2 * width].reshape(4, share, 2, width)
-        inner_grads.append(inner_here.transpose(1, 2, 0, 3).reshape(share, 2, half_width))
-        state_grads.append(
-            jnp.sum(here[..., 2 * width : 2 * width + state], axis=0).reshape(state_share, 2 * state)
-        )
-        rate_here = here[..., 2 * width + state : 2 * width + state + head_count]
-        rate_grads.append(rate_here.transpose(1, 0, 2).reshape(share, heads_here))
+            if layer > 0:
+                grad_low = grad_hidden.astype(BF16)
+                inner = inner_products(grad_low, kept[layer - 1][6])
+                grad_all[layer - 1, batch] = yield from together(
+                    gather_steps(grad_low), sum_steps(inner, inners, (layer - 1, batch))
+                )
+                token = None
+        grads[batch] = grad_hidden
+        yield grad_hidden
+
+    totals = {}
+
+    def term(key, layer, batch, left, right):
+        value = dot(left, right, 0, 0)
+        if batch > 0:
+            value = value + totals[key, layer, batch - 1]
+        totals[key, layer, batch] = value.astype(BF16) if batch == batches - 1 else value
+        return totals[key, layer, batch]
+
+    def out_term(layer, batch):
+        token = yield None
+        whole_grad, normed_out, _, _ = terms[layer, batch]
+        yield term("out", layer, batch, gate(whole_grad, token), normed_out)
+
+    def in_term(layer, batch):
+        token = yield None
+        _, _, normed, back = terms[layer, batch]
+        yield term("in", layer, batch, gate(normed, token), back)
+
+    rows = 4 * share
+
+    def line_cut(array, index):
+        return lax.dynamic_slice_in_dim(array, index * rows, rows, 0)
+
+    def out_part(layer):
+        total = totals["out", layer, batches - 1]
+        return lambda index: line_cut(total, index).astype(F32)
+
+    shares = {}
+
+    def line_sum(total):
+        return lax.psum_scatter(total, "dp", scatter_dimension=0, tiled=True)
+
+    def first_sums(key):
+        yield None
+        if key == "out":
+            total = yield from line_sum_steps(out_part(0))
+            total = total.astype(BF16)
+        else:
+            packed = totals["in", 0, batches - 1]
+            total = line_sum(packed)
+            token = yield packed
+            total = gate(total, token)
+        shares[key, 0] = yield from trade_steps(total.reshape(4, share, -1))
+
+    def later_sums(key, layer):
+        token = yield None
+        packed = totals[key, layer, batches - 1]
+        total = line_sum(gate(packed, token))
+        token = yield packed
+        shares[key, layer] = yield from trade_steps(gate(total, token).reshape(4, share, -1))
+        yield shares[key, layer]
+
+    def both_cores(values, store, key):
+        yield None
+        others = [swap(value) for value in values()]
+        token = yield values()
+        both = []
+        for value, other in zip(values(), gate(others, token)):
+            first = jnp.where(core == 0, value, other)
+            second = jnp.where(core == 0, other, value)
+            both.append(jnp.concatenate([first, second], axis=0))
+        store[key] = jnp.stack(both)[:, None]
+        yield store[key]
+
+    def small_sums():
+        yield None
+        flats = []
+        for layer in range(layers):
+            taps_grad, chans_grad, heads_grad, gain_term = (
+                sum(values) for values in zip(*(gradients[layer, batch] for batch in range(batches)))
+            )
+            both = jnp.concatenate([gain_term, taps_grad[:5, width:].reshape(-1)])
+            head_rows = jnp.stack(
+                [
+                    jnp.sum(heads_grad[:ROWS], axis=1)[:head_count],
+                    jnp.sum(heads_grad[ROWS:], axis=1)[:head_count],
+                    jnp.sum(chans_grad[0].reshape(head_count, head_size), axis=1),
+                ]
+            )
+            flat = jnp.concatenate(
+                [
+                    both,
+                    slot(taps_grad[:5, :width], width).reshape(-1),
+                    slot(chans_grad[1], width),
+                    slot(head_rows, head_count).reshape(-1),
+                ]
+            )
+            flats.append(jnp.pad(flat, (0, -flat.shape[0] % LANES)))
+        flat = jnp.stack(flats)
+        shared = model + 10 * state
+        moved = swap(flat[:, :shared])
+        token = yield flat
+        flat = lax.dynamic_update_slice(flat, flat[:, :shared] + gate(moved, token), (0, 0))
+        finished["flat"] = yield from mesh_sum_steps(flat)
 
     def slot(array, count):
         shape = array.shape[:-1] + (4 * count,)
         spots = (0,) * (array.ndim - 1) + (place * count,)
         return lax.dynamic_update_slice(jnp.zeros(shape, F32), array, spots)
 
-    pieces = []
-    for layer in range(layers):
-        taps_grad, chans_grad, heads_grad, gain_term = small_sums[layer]
-        both = jnp.concatenate([gain_term, taps_grad[:5, width:].reshape(-1)])
-        both = both + swap(both)
-        head_rows = jnp.stack(
-            [
-                jnp.sum(heads_grad[:ROWS], axis=1)[:head_count],
-                jnp.sum(heads_grad[ROWS:], axis=1)[:head_count],
-                jnp.sum(chans_grad[0].reshape(head_count, head_size), axis=1),
-            ]
-        )
-        pieces += [
-            both,
-            slot(taps_grad[:5, :width], width).reshape(-1),
-            slot(chans_grad[1], width),
-            slot(head_rows, head_count).reshape(-1),
-        ]
-    flat = jnp.concatenate(pieces)
-    spill = -flat.shape[0] % (ROWS * LANES)
-    flat = mesh_sum(jnp.pad(flat, (0, spill)).reshape(-1, LANES)).reshape(-1)
+    finished = {}
+    for batch, name in enumerate("ab"):
+        track.begin(name, batch_chain(batch))
+        for layer in range(layers):
+            track.begin(f"o{name}{layer}", out_term(layer, batch))
+            track.begin(f"i{name}{layer}", in_term(layer, batch))
+    track.begin("y", first_sums("out"))
+    track.begin("u", first_sums("in"))
+    track.begin("r", later_sums("in", 1))
+    track.begin("q", later_sums("out", 1))
+    track.begin("xo", both_cores(lambda: [outputs[0], outputs[1]], finished, "output"))
+    track.begin("xg", both_cores(lambda: [grads[0], grads[1]], finished, "input_grad"))
+    track.begin("m", small_sums())
+    track.run(*PLAN)
+
+    inner_grad, out_grad, state_terms, rate_grad = finish(
+        shares["in", 0],
+        shares["in", 1],
+        shares["out", 0],
+        shares["out", 1],
+        head_count,
+        state,
+        width,
+    )
+    state_terms = state_terms.reshape(layers, 2, state_share, 2 * state)
+    state_grad = pick(state_terms, core, 1) + swap(pick(state_terms, 1 - core, 1))
+    flat = finished["flat"]
     taken, small_out = 0, []
-    for layer in range(layers):
-        found = []
-        for shape in (
-            (model,),
-            (5, 2 * state),
-            (5, half_width),
-            (half_width,),
-            (3, 4 * head_count),
-        ):
-            size = 1
-            for extent in shape:
-                size *= extent
-            found.append(flat[taken : taken + size].reshape(shape))
-            taken += size
-        small_out.append(found)
-
-    def spread_out(batched):
-        both = []
-        for value in batched:
-            other = swap(value)
-            first = jnp.where(core == 0, value, other)
-            second = jnp.where(core == 0, other, value)
-            both.append(jnp.concatenate([first, second], axis=0))
-        return jnp.stack(both)[:, None]
-
-    def stacked(position, cut=lambda value: value):
-        return jnp.stack([cut(found[position]) for found in small_out])
+    for shape in ((model,), (5, 2 * state), (5, half_width), (half_width,), (3, 4 * head_count)):
+        size = 1
+        for extent in shape:
+            size *= extent
+        small_out.append(flat[:, taken : taken + size].reshape((layers,) + shape))
+        taken += size
 
     return (
-        spread_out(results),
-        spread_out(grads),
-        stacked(0),
-        jnp.stack(inner_grads),
-        jnp.stack(rate_grads),
-        jnp.stack(state_grads),
-        stacked(2, lambda value: value[:4]),
-        stacked(2, lambda value: value[4]),
-        stacked(1, lambda value: value[:4]),
-        stacked(1, lambda value: value[4]),
-        stacked(4, lambda value: value[0]),
-        stacked(4, lambda value: value[1]),
-        stacked(4, lambda value: value[2]),
-        stacked(3),
-        jnp.stack(out_grads),
+        finished["output"],
+        finished["input_grad"],
+        small_out[0],
+        inner_grad.transpose(0, 2, 1, 3),
+        rate_grad.transpose(0, 2, 1),
+        state_grad,
+        small_out[2][:, :4],
+        small_out[2][:, 4],
+        small_out[1][:, :4],
+        small_out[1][:, 4],
+        small_out[4][:, 0],
+        small_out[4][:, 1],
+        small_out[4][:, 2],
+        small_out[3],
+        out_grad.transpose(0, 2, 1),
     )
 
 
@@ -1268,6 +1625,9 @@
         tokens.shape[1] == line
         and tokens.shape[2] % 8 == 0
         and rows == STRETCH
+        and tokens.shape[0] == 2
+        and line >= 2
+        and inner_weight.shape[0] == 2
         and heads % 8 == 0
         and heads // 8 <= ROWS
         and (inner // 8) % LANES == 0

time: 1110 us -> 687 us (0.62)
  waiting for transfers between devices: 360 us -> 88.9 us
  starting transfers between devices: 269 us -> 131 us
  local copies, waits for them, and re-layouts: 158 us -> 117 us
  matrix products: 99.2 us -> 127 us
  other arithmetic: 84.5 us -> 70.7 us
  between operations: 4.93 us -> 17.3 us
    ppermute x27 -> x12, waiting for transfers between devices: 155 us -> 12 us  [line_shift(): lax.ppermute(value, axis, [(i, (i + step) % count) for i in range(count)])]
    ppermute x67 -> x59, waiting for transfers between devices: 145 us -> 54.2 us  [hop(): return lax.ppermute(value, GROUP, pairs)]
    ppermute x27 -> x12, starting transfers between devices: 88.4 us -> 21.4 us  [line_shift(): lax.ppermute(value, axis, [(i, (i + step) % count) for i in range(count)])]
    unnamed x337 -> x353, local copies, waits for them, and re-layouts: 19.8 us -> 60.7 us
    ppermute x60 -> x31, starting transfers between devices: 72.9 us -> 42.2 us  [swap(): return lax.ppermute(value, 'tensor', [(0, 1), (1, 0)])]
    dynamic_update_slice x119 -> x28, local copies, waits for them, and re-layouts: 36.4 us -> 7.59 us  [put(): lax.dynamic_update_slice(buffer, block.reshape((1,) * len(index) + block....]
    dot_general x24 -> x32, matrix products: 99.2 us -> 127 us  [dot(): lax.dot_general(left, right, (((left_dim,), (right_dim,)), ((), ())), pre...]
    ppermute x60 -> x31, waiting for transfers between devices: 25.6 us -> 1.39 us  [swap(): return lax.ppermute(value, 'tensor', [(0, 1), (1, 0)])]
  transfers between devices with their start and end apart: 182 -> 131, of which waited for: 82 -> 26; matrix products, arithmetic and copies ran while one was open for 19% -> 42% of each run, Pallas kernels for 0% -> 18%
where the time goes in v2:
time: 687 us; the launch traced here: 679 us
  starting transfers between devices  131 us (19%)
  Pallas kernels  127 us (18%)
  matrix products  127 us (18%)
  local copies, waits for them, and re-layouts  117 us (17%)
  waiting for transfers between devices  88.9 us (13%)
  other arithmetic  70.7 us (10%)
  between operations  17.3 us (3%)
    dot_general x32, matrix products, dot(): lax.dot_general(left, right, (((left_dim,), (right_dim,)), ((), ())), pre...  127 us
    pallas_call x4, Pallas kernels, mix_backward(): pl.pallas_call(lambda *refs: backward_kernel(head_size, inner_count, *ref...  82.9 us
    unnamed x353, local copies, waits for them, and re-layouts  60.7 us
    ppermute x59, waiting for transfers between devices, hop(): return lax.ppermute(value, GROUP, pairs)  54.2 us
    ppermute x59, starting transfers between devices, hop(): return lax.ppermute(value, GROUP, pairs)  44 us
    ppermute x31, starting transfers between devices, swap(): return lax.ppermute(value, 'tensor', [(0, 1), (1, 0)])  42.2 us
    pallas_call x4, Pallas kernels, mix_forward(): pl.pallas_call(lambda *refs: forward_kernel(head_size, *refs), grid_spec=...  41.3 us
    ppermute x12, starting transfers between devices, line_shift(): lax.ppermute(value, axis, [(i, (i + step) % count) for i in range(count)])  21.4 us
  transfers between devices with their start and end apart: 131, of which 26 were waited for; matrix products, arithmetic and copies ran while one was open for 42% of the time, Pallas kernels for 18%

profile of v2, /device:TPU:1, one launch (start us, length us, event | category | flops | bytes accessed | tf_op | source)
XLA Modules:
  0.0 679.0 jit_solution(12462512535417816941)
XLA Ops:
  52.0 7.7 %collective-permute-done.4 = bf16[384,768]{1,0:T(8,128)(2,1)} collective-permute-done((bf16[384,768]{1,0:T(8,128)(2,1)}, bf16[384,768]{1,0:T(8,128)(2,1)}, u32[]{:S(2)}, u32[]{:S(2)}) %collective-permute-start.4) | collective-permute-done | bytes 589856 | tf_op jit(solution)/shard_map/ppermute | solution.py:492
  87.4 8.3 %collective-permute-start.22 = (bf16[4,4,96,384]{3,2,1,0:T(8,128)(2,1)S(1)}, bf16[4,4,96,384]{3,2,1,0:T(8,128)(2,1)S(1)}, u32[]{:S(2)}, u32[]{:S(2)}) collective-permute-start(bf16[4,4,96,384]{3,2,1,0:T(8,128)(2,1)S(1)} %pad_maximum_fusion.9), channel_id=1, source_target_pairs={{0,1},{1,0},{2,3},{3,2},{4,5},{5,4},{6,7},{7,6},{8,9},{9,8},{10,11... | collective-permute-start | bytes 3538952 | tf_op jit(solution)/shard_map/ppermute | solution.py:473
  119.0 6.1 fusion.135.refs_1_.refs_2_.refs_3_
  135.5 10.3 %shard_map.263 = (bf16[1024,384]{1,0:T(8,128)(2,1)S(1)}, f32[64,128]{1,0:T(8,128)S(1)}, f32[1024,384]{1,0:T(8,128)S(1)}, f32[8,384,128]{2,1,0:T(8,128)S(1)}) custom-call(s32[8]{0:T(128)S(1)} %get-tuple-element.518.refs_0_, f32[1024,1152]{1,0:T(8,128)S(1)} %fusion.135.refs_1_.refs_2_.refs_3_, f32[8,640]{1,0:T(8,128)S(1)} %get-tuple-element.634.refs_2_.refs_7_, ...), custom_call_target="tpu_custom_call" | custom-call | flops 11000000512 | bytes 10000000 | tf_op jit(solution)/shard_map/pallas_call | solution.py:897
  156.6 8.3 %fusion.136.refs_1_.refs_2_.refs_3_ = f32[1024,1152]{1,0:T(8,128)} fusion(bf16[1024,1536]{1,0:T(8,128)(2,1)} %bitcast.81, bf16[1536,1152]{1,0:T(8,128)(2,1)S(1)} %fusion.28), kind=kOutput, calls=%fused_computation.513 | convolution fusion | flops 3623878656 | bytes 11403264 | tf_op jit(solution)/shard_map/dot_general | solution.py:554
  183.2 10.3 %shard_map.264 = (bf16[1024,384]{1,0:T(8,128)(2,1)S(1)}, f32[64,128]{1,0:T(8,128)S(1)}, f32[1024,384]{1,0:T(8,128)S(1)}, f32[8,384,128]{2,1,0:T(8,128)S(1)}) custom-call(s32[8]{0:T(128)S(1)} %get-tuple-element.518.refs_0_, f32[1024,1152]{1,0:T(8,128)S(1)} %bitcast.541, f32[8,640]{1,0:T(8,128)S(1)} %get-tuple-element.634.refs_2_.refs_7_, ...), custom_call_target="tpu_custom_call" | custom-call | flops 11000000512 | bytes 10000000 | tf_op jit(solution)/shard_map/pallas_call | solution.py:897
  212.9 8.2 %collective-permute-done.49 = f32[8,128]{1,0:T(8,128)S(1)} collective-permute-done((f32[8,128]{1,0:T(8,128)S(1)}, f32[8,128]{1,0:T(8,128)S(1)}, u32[]{:S(2)}, u32[]{:S(2)}) %collective-permute-start.49) | collective-permute-done | bytes 4128 | tf_op jit(solution)/shard_map/ppermute | solution.py:469
  225.3 8.3 %collective-permute-done.46 = bf16[128,1536]{1,0:T(8,128)(2,1)S(1)} collective-permute-done((bf16[128,1536]{1,0:T(8,128)(2,1)S(1)}, bf16[128,1536]{1,0:T(8,128)(2,1)S(1)}, u32[]{:S(2)}, u32[]{:S(2)}) %collective-permute-start.46) | collective-permute-done | bytes 393248 | tf_op jit(solution)/shard_map/ppermute | solution.py:469
  249.7 10.4 %shard_map.265 = (bf16[1024,384]{1,0:T(8,128)(2,1)S(1)}, f32[64,128]{1,0:T(8,128)S(1)}, f32[1024,384]{1,0:T(8,128)S(1)}, f32[8,384,128]{2,1,0:T(8,128)S(1)}) custom-call(s32[8]{0:T(128)S(1)} %get-tuple-element.518.refs_0_, f32[1024,1152]{1,0:T(8,128)S(1)} %fusion.111.refs_1_.refs_2_.refs_3_, f32[8,640]{1,0:T(8,128)S(1)} %get-tuple-element.633.refs_2_.refs_7_, ...), custom_call_target="tpu_custom_call" | custom-call | flops 11000000512 | bytes 10000000 | tf_op jit(solution)/shard_map/pallas_call | solution.py:897
  275.9 10.3 %shard_map.266 = (bf16[1024,384]{1,0:T(8,128)(2,1)S(1)}, f32[64,128]{1,0:T(8,128)S(1)}, f32[1024,384]{1,0:T(8,128)S(1)}, f32[8,384,128]{2,1,0:T(8,128)S(1)}) custom-call(s32[8]{0:T(128)S(1)} %get-tuple-element.518.refs_0_, f32[1024,1152]{1,0:T(8,128)S(1)} %fusion.110.refs_1_.refs_2_.refs_3_, f32[8,640]{1,0:T(8,128)S(1)} %get-tuple-element.633.refs_2_.refs_7_, ...), custom_call_target="tpu_custom_call" | custom-call | flops 11000000512 | bytes 10000000 | tf_op jit(solution)/shard_map/pallas_call | solution.py:897
  338.3 20.6 %shard_map.267 = (bf16[1024,1152]{1,0:T(8,128)(2,1)S(1)}, f32[8,640]{1,0:T(8,128)S(1)}, f32[8,384]{1,0:T(8,128)S(1)}, f32[16,128]{1,0:T(8,128)S(1)}) custom-call(s32[8]{0:T(128)S(1)} %get-tuple-element.518.refs_0_, f32[1024,384]{1,0:T(8,128)S(1)} %copy-done.6, f32[1024,1152]{1,0:T(8,128)S(1)} %copy-done.19, f32[1024,1152]{1,0:T(8,128)S(1)} %copy-done.19, ...), custom_call_target="tpu_custom_call" | custom-call | flops 23000000512 | bytes 16000000 | tf_op jit(solution)/shard_map/pallas_call | solution.py:953
  376.2 20.7 %shard_map.268 = (bf16[1024,1152]{1,0:T(8,128)(2,1)S(1)}, f32[8,640]{1,0:T(8,128)S(1)}, f32[8,384]{1,0:T(8,128)S(1)}, f32[16,128]{1,0:T(8,128)S(1)}) custom-call(s32[8]{0:T(128)S(1)} %get-tuple-element.518.refs_0_, f32[1024,384]{1,0:T(8,128)S(1)} %copy-done.5, f32[1024,1152]{1,0:T(8,128)S(1)} %bitcast.545, f32[1024,1152]{1,0:T(8,128)S(1)} %bitcast.545, ...), custom_call_target="tpu_custom_call" | custom-call | flops 23000000512 | bytes 16000000 | tf_op jit(solution)/shard_map/pallas_call | solution.py:953
  402.6 5.3 fusion.2
  416.4 5.6 fusion.10
  425.5 9.1 %fusion.137 = f32[1536,1152]{1,0:T(8,128)} fusion(bf16[1024,1536]{1,0:T(8,128)(2,1)} %bitcast.616, bf16[1024,1152]{1,0:T(8,128)(2,1)S(1)} %copy-done.12), kind=kOutput, calls=%fused_computation.514 | convolution fusion | flops 3623878656 | bytes 12582912 | tf_op jit(solution)/shard_map/dot_general | solution.py:554
  446.2 5.9 collective-permute-start.92
  460.5 9.5 %fusion = bf16[1536,1152]{1,0:T(8,128)(2,1)} fusion(f32[1536,1152]{1,0:T(8,128)} %fusion.137, bf16[1024,1536]{1,0:T(8,128)(2,1)} %bitcast.618, bf16[1024,1152]{1,0:T(8,128)(2,1)S(1)} %copy-done.10), kind=kOutput, calls=%fused_computation.2 | convolution fusion | flops 3627417600 | bytes 16121856 | tf_op jit(solution)/shard_map/dot_general | solution.py:554
  479.8 5.4 fusion.42
  487.6 20.8 %shard_map.269 = (bf16[1024,1152]{1,0:T(8,128)(2,1)S(1)}, f32[8,640]{1,0:T(8,128)S(1)}, f32[8,384]{1,0:T(8,128)S(1)}, f32[16,128]{1,0:T(8,128)S(1)}) custom-call(s32[8]{0:T(128)S(1)} %get-tuple-element.518.refs_0_, f32[1024,384]{1,0:T(8,128)S(1)} %copy-done.7, f32[1024,1152]{1,0:T(8,128)S(1)} %copy-done.16, f32[1024,1152]{1,0:T(8,128)S(1)} %copy-done.16, ...), custom_call_target="tpu_custom_call" | custom-call | flops 23000000512 | bytes 16000000 | tf_op jit(solution)/shard_map/pallas_call | solution.py:953
  534.0 6.4 fusion.140
  540.5 20.8 %shard_map.270 = (bf16[1024,1152]{1,0:T(8,128)(2,1)S(1)}, f32[8,640]{1,0:T(8,128)S(1)}, f32[8,384]{1,0:T(8,128)S(1)}, f32[16,128]{1,0:T(8,128)S(1)}) custom-call(s32[8]{0:T(128)S(1)} %get-tuple-element.518.refs_0_, f32[1024,384]{1,0:T(8,128)S(1)} %fusion.139.refs_1_, f32[1024,1152]{1,0:T(8,128)S(1)} %bitcast.543, f32[1024,1152]{1,0:T(8,128)S(1)} %bitcast.543, ...), custom_call_target="tpu_custom_call" | custom-call | flops 23000000512 | bytes 16000000 | tf_op jit(solution)/shard_map/pallas_call | solution.py:953
  563.7 10.8 %fusion.1 = bf16[1536,1152]{1,0:T(8,128)(2,1)} fusion(f32[1536,1152]{1,0:T(8,128)} %fusion.140, bf16[1024,1536]{1,0:T(8,128)(2,1)} %bitcast.81, bf16[1024,1152]{1,0:T(8,128)(2,1)} %copy-done.13), kind=kOutput, calls=%fused_computation.3 | convolution fusion | flops 3627417600 | bytes 16121856 | tf_op jit(solution)/shard_map/dot_general | solution.py:554
  601.8 6.9 %collective-permute-done.103 = bf16[2,128,1536]{2,1,0:T(8,128)(2,1)} collective-permute-done((bf16[2,128,1536]{2,1,0:T(8,128)(2,1)}, bf16[2,128,1536]{2,1,0:T(8,128)(2,1)}, u32[]{:S(2)}, u32[]{:S(2)}) %collective-permute-start.103) | collective-permute-done | bytes 786464 | tf_op jit(solution)/shard_map/ppermute | solution.py:469
  616.8 5.7 collective-permute-done.108
  (970 shorter events, 419.9 us)
Async XLA Ops:
  7.2 232.2 %all-gather.2.cloned.1.call-start = ((), (), s32[]{:S(2)}) async-start(), calls=%async_computation.3 | async-start | bytes 4423680 | tf_op jit(solution)/shard_map/all_gather | solution.py:1278
  13.2 27.9 %collective-permute-start.2 = (bf16[96,768]{1,0:T(8,128)(2,1)}, bf16[96,768]{1,0:T(8,128)(2,1)}, u32[]{:S(2)}, u32[]{:S(2)}) collective-permute-start(bf16[96,768]{1,0:T(8,128)(2,1)} %pad_maximum_fusion.13), channel_id=1, source_target_pairs={{0,4},{2,6},{4,0},{6,2},{1,5},{3,7},{5,1},{7,3},{8,12},{10,14},{12... | collective-permute-start | bytes 442376 | tf_op jit(solution)/shard_map/ppermute | solution.py:1289
  15.2 28.6 %collective-permute-start.3 = (bf16[96,768]{1,0:T(8,128)(2,1)}, bf16[96,768]{1,0:T(8,128)(2,1)}, u32[]{:S(2)}, u32[]{:S(2)}) collective-permute-start(bf16[96,768]{1,0:T(8,128)(2,1)} %pad_maximum_fusion.14), channel_id=1, source_target_pairs={{0,6},{2,4},{4,2},{6,0},{1,7},{3,5},{5,3},{7,1},{8,14},{10,12},{12... | collective-permute-start | bytes 442376 | tf_op jit(solution)/shard_map/ppermute | solution.py:1289
  15.9 29.9 %collective-permute-start.6 = (bf16[96,384]{1,0:T(8,128)(2,1)}, bf16[96,384]{1,0:T(8,128)(2,1)}, u32[]{:S(2)}, u32[]{:S(2)}) collective-permute-start(bf16[96,384]{1,0:T(8,128)(2,1)} %get-tuple-element.599), channel_id=1, source_target_pairs={{0,8},{8,16},{16,24},{24,0},{1,9},{9,17},{17,25},{25,1},{2,10},{10... | collective-permute-start | bytes 221192 | tf_op jit(solution)/shard_map/ppermute | solution.py:492
  21.7 30.0 %collective-permute-start = (bf16[128,1536]{1,0:T(8,128)(2,1)}, bf16[128,1536]{1,0:T(8,128)(2,1)}, u32[]{:S(2)}, u32[]{:S(2)}) collective-permute-start(bf16[128,1536]{1,0:T(8,128)(2,1)} %get-tuple-element.221), channel_id=1, source_target_pairs={{0,2},{1,5},{2,0},{3,7},{4,6},{5,1},{6,4},{7,3},{8,10},{9,13},{10,... | collective-permute-start | bytes 1179656 | tf_op jit(solution)/shard_map/ppermute | solution.py:469
  51.7 28.8 %collective-permute-start.14 = (bf16[128,1536]{1,0:T(8,128)(2,1)}, bf16[128,1536]{1,0:T(8,128)(2,1)}, u32[]{:S(2)}, u32[]{:S(2)}) collective-permute-start(bf16[128,1536]{1,0:T(8,128)(2,1)} %get-tuple-element.224), channel_id=1, source_target_pairs={{0,4},{1,3},{2,6},{3,1},{4,0},{5,7},{6,2},{7,5},{8,12},{9,11},{10,... | collective-permute-start | bytes 1179656 | tf_op jit(solution)/shard_map/ppermute | solution.py:469
  61.9 36.2 %collective-permute-start.20 = (bf16[384,768]{1,0:T(8,128)(2,1)}, bf16[384,768]{1,0:T(8,128)(2,1)}, u32[]{:S(2)}, u32[]{:S(2)}) collective-permute-start(bf16[384,768]{1,0:T(8,128)(2,1)} %bitcast.22), channel_id=1, source_target_pairs={{0,16},{8,24},{16,0},{24,8},{1,17},{9,25},{17,1},{25,9},{2,18},{10... | collective-permute-start | bytes 1769480 | tf_op jit(solution)/shard_map/ppermute | solution.py:492
  126.6 39.3 %collective-permute-start.30 = (bf16[128,1536]{1,0:T(8,128)(2,1)S(1)}, bf16[128,1536]{1,0:T(8,128)(2,1)S(1)}, u32[]{:S(2)}, u32[]{:S(2)}) collective-permute-start(bf16[128,1536]{1,0:T(8,128)(2,1)S(1)} %copy-done.45), channel_id=1, source_target_pairs={{0,4},{1,3},{2,6},{3,1},{4,0},{5,7},{6,2},{7,5},{8,12},{9,11},{10,... | collective-permute-start | bytes 1179656 | tf_op jit(solution)/shard_map/ppermute | solution.py:469
  145.8 29.4 %collective-permute-start.29 = (bf16[128,1536]{1,0:T(8,128)(2,1)S(1)}, bf16[128,1536]{1,0:T(8,128)(2,1)}, u32[]{:S(2)}, u32[]{:S(2)}) collective-permute-start(bf16[128,1536]{1,0:T(8,128)(2,1)S(1)} %get-tuple-element.244), channel_id=1, source_target_pairs={{0,4},{1,3},{2,6},{3,1},{4,0},{5,7},{6,2},{7,5},{8,12},{9,11},{10,... | collective-permute-start | bytes 1179656 | tf_op jit(solution)/shard_map/ppermute | solution.py:469
  167.2 430.8 %reduce-scatter.4.cloned.1.call-start = ((), (), s32[]{:S(2)}) async-start(), calls=%async_computation.4 | async-start | bytes 1474560 | tf_op jit(solution)/shard_map/reduce_scatter | solution.py:1494
  174.7 32.8 %collective-permute-start.73 = (bf16[4,128,1536]{2,1,0:T(8,128)(2,1)S(1)}, bf16[4,128,1536]{2,1,0:T(8,128)(2,1)S(1)}, u32[]{:S(2)}, u32[]{:S(2)}) collective-permute-start(bf16[4,128,1536]{2,1,0:T(8,128)(2,1)S(1)} %pad_maximum_fusion.3), channel_id=1, source_target_pairs={{0,1},{1,0},{2,3},{3,2},{4,5},{5,4},{6,7},{7,6},{8,9},{9,8},{10,11... | collective-permute-start | bytes 4718600 | tf_op jit(solution)/shard_map/ppermute | solution.py:473
  177.2 31.8 %collective-permute-start.72 = (bf16[4,128,1536]{2,1,0:T(8,128)(2,1)S(1)}, bf16[4,128,1536]{2,1,0:T(8,128)(2,1)S(1)}, u32[]{:S(2)}, u32[]{:S(2)}) collective-permute-start(bf16[4,128,1536]{2,1,0:T(8,128)(2,1)S(1)} %pad_maximum_fusion.4), channel_id=1, source_target_pairs={{0,1},{1,0},{2,3},{3,2},{4,5},{5,4},{6,7},{7,6},{8,9},{9,8},{10,11... | collective-permute-start | bytes 4718600 | tf_op jit(solution)/shard_map/ppermute | solution.py:473
  314.3 126.1 %collective-permute-start.62 = (f32[128,1536]{1,0:T(8,128)}, f32[128,1536]{1,0:T(8,128)}, u32[]{:S(2)}, u32[]{:S(2)}) collective-permute-start(f32[128,1536]{1,0:T(8,128)} %get-tuple-element.522), channel_id=1, source_target_pairs={{0,1},{1,0},{2,3},{3,2},{4,5},{5,4},{6,7},{7,6},{8,9},{9,8},{10,11... | collective-permute-start | bytes 2359304 | tf_op jit(solution)/shard_map/ppermute | solution.py:473
  331.2 27.7 %collective-permute-start.76 = (f32[8,128]{1,0:T(8,128)S(1)}, f32[8,128]{1,0:T(8,128)S(1)}, u32[]{:S(2)}, u32[]{:S(2)}) collective-permute-start(f32[8,128]{1,0:T(8,128)S(1)} %add.706), channel_id=1, source_target_pairs={{0,4},{1,3},{2,6},{3,1},{4,0},{5,7},{6,2},{7,5},{8,12},{9,11},{10,... | collective-permute-start | bytes 12296 | tf_op jit(solution)/shard_map/ppermute | solution.py:469
  370.0 71.2 %collective-permute-start.71 = (f32[128,1536]{1,0:T(8,128)}, f32[128,1536]{1,0:T(8,128)}, u32[]{:S(2)}, u32[]{:S(2)}) collective-permute-start(f32[128,1536]{1,0:T(8,128)} %get-tuple-element.520), channel_id=1, source_target_pairs={{0,1},{1,0},{2,3},{3,2},{4,5},{5,4},{6,7},{7,6},{8,9},{9,8},{10,11... | collective-permute-start | bytes 2359304 | tf_op jit(solution)/shard_map/ppermute | solution.py:473
  436.2 188.3 %reduce-scatter.6.cloned.1.call-start = ((), (), s32[]{:S(2)}) async-start(), calls=%async_computation.5 | async-start | bytes 4423680 | tf_op jit(solution)/shard_map/reduce_scatter | solution.py:1494
  460.2 48.2 %collective-permute-start.93 = (bf16[128,1536]{1,0:T(8,128)(2,1)}, bf16[128,1536]{1,0:T(8,128)(2,1)}, u32[]{:S(2)}, u32[]{:S(2)}) collective-permute-start(bf16[128,1536]{1,0:T(8,128)(2,1)} %copy-done.59), channel_id=1, source_target_pairs={{0,4},{1,3},{2,6},{3,1},{4,0},{5,7},{6,2},{7,5},{8,12},{9,11},{10,... | collective-permute-start | bytes 1179656 | tf_op jit(solution)/shard_map/ppermute | solution.py:469
  470.1 174.4 %reduce-scatter.8.cloned.1.call-start = ((), (), s32[]{:S(2)}) async-start(), calls=%async_computation.6 | async-start | bytes 4423680 | tf_op jit(solution)/shard_map/reduce_scatter | solution.py:1494
  478.2 32.4 %collective-permute-start.95 = (f32[8,128]{1,0:T(8,128)S(1)}, f32[8,128]{1,0:T(8,128)S(1)}, u32[]{:S(2)}, u32[]{:S(2)}) collective-permute-start(f32[8,128]{1,0:T(8,128)S(1)} %add.724), channel_id=1, source_target_pairs={{0,4},{1,3},{2,6},{3,1},{4,0},{5,7},{6,2},{7,5},{8,12},{9,11},{10,... | collective-permute-start | bytes 12296 | tf_op jit(solution)/shard_map/ppermute | solution.py:469
  479.4 33.7 %collective-permute-start.94 = (bf16[128,1536]{1,0:T(8,128)(2,1)}, bf16[128,1536]{1,0:T(8,128)(2,1)S(1)}, u32[]{:S(2)}, u32[]{:S(2)}) collective-permute-start(bf16[128,1536]{1,0:T(8,128)(2,1)} %collective-permute-done.90), channel_id=1, source_target_pairs={{0,4},{1,3},{2,6},{3,1},{4,0},{5,7},{6,2},{7,5},{8,12},{9,11},{10,... | collective-permute-start | bytes 1179656 | tf_op jit(solution)/shard_map/ppermute | solution.py:469
  521.7 52.9 %collective-permute-start.97 = (bf16[2,128,1536]{2,1,0:T(8,128)(2,1)}, bf16[2,128,1536]{2,1,0:T(8,128)(2,1)}, u32[]{:S(2)}, u32[]{:S(2)}) collective-permute-start(bf16[2,128,1536]{2,1,0:T(8,128)(2,1)} %fusion.14), channel_id=1, source_target_pairs={{0,4},{1,3},{2,6},{3,1},{4,0},{5,7},{6,2},{7,5},{8,12},{9,11},{10,... | collective-permute-start | bytes 2359304 | tf_op jit(solution)/shard_map/ppermute | solution.py:469
  527.3 67.9 %collective-permute-start.105 = (bf16[384,384]{1,0:T(8,128)(2,1)}, bf16[384,384]{1,0:T(8,128)(2,1)}, u32[]{:S(2)}, u32[]{:S(2)}) collective-permute-start(bf16[384,384]{1,0:T(8,128)(2,1)} %get-tuple-element.555), channel_id=1, source_target_pairs={{0,8},{8,16},{16,24},{24,0},{1,9},{9,17},{17,25},{25,1},{2,10},{10... | collective-permute-start | bytes 884744 | tf_op jit(solution)/shard_map/ppermute | solution.py:492
  531.7 63.5 %collective-permute-start.106 = (bf16[384,384]{1,0:T(8,128)(2,1)}, bf16[384,384]{1,0:T(8,128)(2,1)}, u32[]{:S(2)}, u32[]{:S(2)}) collective-permute-start(bf16[384,384]{1,0:T(8,128)(2,1)} %get-tuple-element.554), channel_id=1, source_target_pairs={{0,16},{8,24},{16,0},{24,8},{1,17},{9,25},{17,1},{25,9},{2,18},{10... | collective-permute-start | bytes 884744 | tf_op jit(solution)/shard_map/ppermute | solution.py:492
  532.0 63.2 %collective-permute-start.107 = (bf16[384,384]{1,0:T(8,128)(2,1)}, bf16[384,384]{1,0:T(8,128)(2,1)}, u32[]{:S(2)}, u32[]{:S(2)}) collective-permute-start(bf16[384,384]{1,0:T(8,128)(2,1)} %get-tuple-element.553), channel_id=1, source_target_pairs={{0,24},{8,0},{16,8},{24,16},{1,25},{9,1},{17,9},{25,17},{2,26},{10... | collective-permute-start | bytes 884744 | tf_op jit(solution)/shard_map/ppermute | solution.py:492
  (259 other events, 2696.4 us)
Sparse Core Ops, SparseCore 0:
  167.4 72.0 all-gather.1
  436.3 31.4 reduce-scatter.3
  470.2 76.5 reduce-scatter.5
  574.7 69.7 reduce-scatter.7

commit v3 on v2

--- a/solution.py
+++ b/solution.py
@@ -594,10 +594,12 @@
     grown = jnp.exp(running)
     tail = jnp.exp(ending - running)
     rows = [steps, running, grown, tail] + extra
-    rows.append(jnp.zeros((length - ROWS * len(rows), length), F32))
-    columns = jnp.transpose(jnp.concatenate(rows, axis=0))
-    high, low_part = split(columns, 2)
-    wide = dot(high, spread) + dot(low_part, spread)
+    rows.append(jnp.zeros((LANES // 2 - ROWS * len(rows), length), F32))
+    rows = jnp.concatenate(rows, axis=0)
+    high = rows.astype(BF16).astype(F32)
+    halves = jnp.transpose(jnp.concatenate([high, rows - high], axis=0))
+    columns = halves[:, : LANES // 2] + halves[:, LANES // 2 :]
+    wide = dot(halves.astype(BF16), spread)
     whole_decay = jnp.exp(jnp.broadcast_to(ending, (ROWS, LANES)))
     inputs = activated[:, :width]
     return dict(
@@ -644,7 +646,8 @@
 def forward_kernel(
     head_size,
     order_ref,
-    raw_ref,
+    raw_first,
+    raw_second,
     taps_ref,
     chans_ref,
     heads_ref,
@@ -655,73 +658,83 @@
     mixed_ref,
     state_ref,
     carry,
-    window,
+    window_first,
+    window_second,
 ):
-    length, width, state = raw_ref.shape[0], chans_ref.shape[1], carry.shape[1]
+    length, width, state = raw_first.shape[0], chans_ref.shape[1], carry.shape[1]
     conv_width = width + 2 * state
     head_count = width // head_size
     pair = LANES // head_size
-
-    @pl.when(pl.program_id(0) == 0)
+    step = pl.program_id(0)
+
+    @pl.when(step == 0)
     def _():
         carry[...] = jnp.zeros_like(carry)
-        window[0:ROWS, :] = jnp.zeros((ROWS, conv_width), F32)
-
-    raw = raw_ref[...]
-    window[ROWS : ROWS + length, :] = raw[:, width : width + conv_width].astype(BF16).astype(F32)
-    parts = front(
-        raw,
-        window,
-        taps_ref[...],
-        heads_ref[...],
-        spread_ref[...],
-        upper_ref[...],
-        width,
-        state,
-        [],
-    )
-    window[0:ROWS, :] = window[length : length + ROWS, :]
-    inputs, keys, queries = parts["inputs"], parts["keys"], parts["queries"]
-    before = carry[...]
-    state_ref[...] = before
-    stepped = inputs * parts["steps_wide"]
-    stepped_low = stepped.astype(BF16)
-    scores = dot(queries, keys, 1, 1)
+        window_first[0:ROWS, :] = jnp.zeros((ROWS, conv_width), F32)
+
+    raws = [raw_first[...], raw_second[...]]
+    windows = [window_first, window_second]
+    for raw, window in zip(raws, windows):
+        window[ROWS : ROWS + length, :] = raw[:, width : width + conv_width].astype(BF16).astype(F32)
+    window_second[0:ROWS, :] = window_first[length : length + ROWS, :]
+    taps, heads = taps_ref[...], heads_ref[...]
+    fronts = [
+        front(raw, window, taps, heads, spread_ref[...], upper_ref[...], width, state, [])
+        for raw, window in zip(raws, windows)
+    ]
+    window_first[0:ROWS, :] = window_second[length : length + ROWS, :]
     causal = causal_mask(length)
     lane = lax.broadcasted_iota(jnp.int32, (length, LANES), 1) // head_size
-    columns = []
-    for block in range(head_count // pair):
-        source = stepped_low[:, block * LANES : (block + 1) * LANES]
-        joined = None
-        for k in range(pair):
-            mixing = (scores * decay_matrix(parts, block * pair + k, causal)).astype(BF16)
-            got = dot(mixing, source)
-            joined = got if joined is None else jnp.where(lane == k, got, joined)
-        columns.append(joined)
-    carried = dot(queries, before.astype(BF16), 1, 1)
-    mixed = (
-        jnp.concatenate(columns, axis=1)
-        + carried * parts["grown_wide"]
-        + chans_ref[0:1, :] * inputs
-    )
-    update = dot((stepped * parts["tail_wide"]).astype(BF16), keys, 0, 0)
-    carry[...] = per_row(parts["whole_decay"], head_count, head_size) * before + update
-    gate = raw[:, :width]
-    gated = mixed * (gate * jax.nn.sigmoid(gate))
-    mixed_ref[...] = mixed
-    value_ref[...] = (gated * chans_ref[1:2, :]).astype(BF16)
-    squares = jnp.sum(gated * gated, axis=1, keepdims=True)
-    square_ref[...] = jnp.transpose(jnp.broadcast_to(squares, (length, length)))[:ROWS]
+    insides, steppeds = [], []
+    for parts in fronts:
+        stepped = parts["inputs"] * parts["steps_wide"]
+        stepped_low = stepped.astype(BF16)
+        scores = dot(parts["queries"], parts["keys"], 1, 1)
+        columns = []
+        for block in range(head_count // pair):
+            source = stepped_low[:, block * LANES : (block + 1) * LANES]
+            joined = None
+            for k in range(pair):
+                mixing = (scores * decay_matrix(parts, block * pair + k, causal)).astype(BF16)
+                got = dot(mixing, source)
+                joined = got if joined is None else jnp.where(lane == k, got, joined)
+            columns.append(joined)
+        insides.append(jnp.concatenate(columns, axis=1))
+        steppeds.append(stepped)
+    updates = [
+        dot((stepped * parts["tail_wide"]).astype(BF16), parts["keys"], 0, 0)
+        for stepped, parts in zip(steppeds, fronts)
+    ]
+    before = carry[...]
+    for sub, (raw, parts, inside, update) in enumerate(zip(raws, fronts, insides, updates)):
+        inputs = parts["inputs"]
+        state_ref[sub] = before
+        carried = dot(parts["queries"], before.astype(BF16), 1, 1)
+        mixed = inside + carried * parts["grown_wide"] + chans_ref[0:1, :] * inputs
+        before = per_row(parts["whole_decay"], head_count, head_size) * before + update
+        gate_part = raw[:, :width]
+        gated = mixed * (gate_part * jax.nn.sigmoid(gate_part))
+        rows = pl.ds(pl.multiple_of(order_ref[2 * step + sub] * length, length), length)
+        mixed_ref[rows, :] = mixed
+        value_ref[rows, :] = (gated * chans_ref[1:2, :]).astype(BF16)
+        squares = jnp.sum(gated * gated, axis=1, keepdims=True)
+        square_ref[sub * ROWS : (sub + 1) * ROWS, :] = jnp.transpose(
+            jnp.broadcast_to(squares, (length, length))
+        )[:ROWS]
+    carry[...] = before
 
 
 def backward_kernel(
     head_size,
     inner_count,
     order_ref,
-    grad_ref,
-    raw_ref,
+    grad_first,
+    grad_second,
+    raw_first,
+    raw_second,
     past_ref,
-    mixed_ref,
+    mixed_first,
+    mixed_second,
     state_ref,
     token_ref,
     taps_ref,
@@ -735,10 +748,12 @@
     chans_out,
     heads_out,
     carry,
-    window,
-    later,
+    window_first,
+    window_second,
+    later_first,
+    later_second,
 ):
-    length, width, state = raw_ref.shape[0], chans_ref.shape[1], carry.shape[1]
+    length, width, state = raw_first.shape[0], chans_ref.shape[1], carry.shape[1]
     conv_width = width + 2 * state
     head_count = width // head_size
     pair = LANES // head_size
@@ -747,138 +762,157 @@
     @pl.when(step == 0)
     def _():
         carry[...] = jnp.zeros_like(carry)
-        later[length : length + ROWS, :] = jnp.zeros((ROWS, conv_width), F32)
+        later_first[length : length + ROWS, :] = jnp.zeros((ROWS, conv_width), F32)
         taps_out[...] = jnp.zeros_like(taps_out)
         chans_out[...] = jnp.zeros_like(chans_out)
         heads_out[...] = jnp.zeros_like(heads_out)
 
-    raw = raw_ref[...]
-    past = past_ref[:, width : width + conv_width].astype(BF16).astype(F32)
-    window[0:ROWS, :] = jnp.where(step == count - 1, 0.0, past)
-    window[ROWS : ROWS + length, :] = raw[:, width : width + conv_width].astype(BF16).astype(F32)
+    raws = [raw_first[...], raw_second[...]]
+    windows, laters = [window_first, window_second], [later_first, later_second]
+    conv = slice(width, width + conv_width)
+    for raw, window in zip(raws, windows):
+        window[ROWS : ROWS + length, :] = raw[:, conv].astype(BF16).astype(F32)
+    window_first[0:ROWS, :] = window_second[length : length + ROWS, :]
+    past = past_ref[:, conv].astype(BF16).astype(F32)
+    window_second[0:ROWS, :] = jnp.where(step == count - 1, 0.0, past)
     taps, heads, picker = taps_ref[...], heads_ref[...], picker_ref[...]
-    parts = front(
-        raw, window, taps, heads, spread_ref[...], upper_ref[...], width, state, [token_ref[...]]
-    )
-    inputs, keys, queries = parts["inputs"], parts["keys"], parts["queries"]
     skip, gain = chans_ref[0:1, :], chans_ref[1:2, :]
-    scale = parts["columns"][:, 4 * ROWS : 4 * ROWS + 1]
-    inner = parts["columns"][:, 4 * ROWS + 1 : 4 * ROWS + 2]
-
-    gate, mixed = raw[:, :width], mixed_ref[...]
-    gate_sig = jax.nn.sigmoid(gate)
-    gate_silu = gate * gate_sig
-    gated = mixed * gate_silu
-    grad = grad_ref[...]
-    scaled_gated = gated * scale
-    gain_term = jnp.sum(grad * scaled_gated, axis=0, keepdims=True)
-    grad_gated = scale * (grad * gain) - gated * (scale * scale * scale * inner / inner_count)
-    grad_mixed = grad_gated * gate_silu
-    back_ref[:, :width] = (
-        grad_gated * mixed * (gate_sig + gate_silu * (1.0 - gate_sig))
-    ).astype(BF16)
-    skip_term = jnp.sum(grad_mixed * inputs, axis=0, keepdims=True)
-    chans_out[0:1, :] += skip_term
-    chans_out[1:2, :] += gain_term
-
-    stepped = inputs * parts["steps_wide"]
-    stepped_low, grad_low = stepped.astype(BF16), grad_mixed.astype(BF16)
-    scores = dot(queries, keys, 1, 1)
     causal = causal_mask(length)
     lane = lax.broadcasted_iota(jnp.int32, (length, LANES), 1)
     head_lane = lane // head_size
-    grad_scores = jnp.zeros((length, length), F32)
-    row_sums = jnp.zeros((length, length), F32)
-    column_sums, columns = [], []
-    for block in range(head_count // pair):
-        cut = slice(block * LANES, (block + 1) * LANES)
-        source, target = stepped_low[:, cut], grad_low[:, cut]
-        joined = None
-        for k in range(pair):
-            h = block * pair + k
-            spread_h = decay_matrix(parts, h, causal)
-            own_target = jnp.where(head_lane == k, target, jnp.zeros_like(target))
-            pulled = dot(own_target, source, 1, 1) * spread_h
-            grad_scores = grad_scores + pulled
-            moved = pulled * scores
-            row_sums = jnp.where(lane == h, jnp.sum(moved, axis=1, keepdims=True), row_sums)
-            column_sums.append(jnp.sum(moved, axis=0, keepdims=True))
-            got = dot((scores * spread_h).astype(BF16), target, 0, 0)
-            joined = got if joined is None else jnp.where(head_lane == k, got, joined)
-        columns.append(joined)
-    before, after = state_ref[...], carry[...]
-    before_low, after_low = before.astype(BF16), after.astype(BF16)
-    tail_wide, grown_wide = parts["tail_wide"], parts["grown_wide"]
-    through = tail_wide * dot(keys, after_low, 1, 1)
-    grad_stepped = jnp.concatenate(columns, axis=1) + through
-    ended = stepped * through
-    carried = dot(queries, before_low, 1, 1) * grown_wide
-    whole_rows = per_row(parts["whole_decay"], head_count, head_size)
-    kept = whole_rows * after
-    held = jnp.sum(kept * before, axis=1, keepdims=True)
-    spare = jnp.zeros((ROWS - head_count, 1), F32)
-    held_heads = jnp.concatenate(
-        [
-            jnp.sum(held[h * head_size : (h + 1) * head_size], axis=0, keepdims=True)
-            for h in range(head_count)
-        ]
-        + [spare],
-        axis=0,
-    )
-    ended_heads = head_sums(picker, ended)
-    grad_running = (
-        jnp.transpose(row_sums)[:ROWS]
-        - jnp.concatenate(column_sums + [jnp.zeros((ROWS - head_count, length), F32)], axis=0)
-        + head_sums(picker, grad_mixed * carried)
-        - ended_heads
-    )
-    last = jnp.sum(ended_heads, axis=1, keepdims=True) + held_heads
+    places_of = [
+        pl.ds(pl.multiple_of(order_ref[2 * count - 1 - 2 * step - sub] * length, length), length)
+        for sub in range(2)
+    ]
+
+    fronts, held = [], []
+    for sub, (raw, window, grad_ref, mixed_ref) in enumerate(
+        zip(raws, windows, (grad_first, grad_second), (mixed_first, mixed_second))
+    ):
+        token = token_ref[(1 - sub) * ROWS : (2 - sub) * ROWS, :]
+        parts = front(
+            raw, window, taps, heads, spread_ref[...], upper_ref[...], width, state, [token]
+        )
+        fronts.append(parts)
+        inputs = parts["inputs"]
+        scale = parts["columns"][:, 4 * ROWS : 4 * ROWS + 1]
+        inner = parts["columns"][:, 4 * ROWS + 1 : 4 * ROWS + 2]
+        gate_part, mixed = raw[:, :width], mixed_ref[...]
+        gate_sig = jax.nn.sigmoid(gate_part)
+        gate_silu = gate_part * gate_sig
+        gated = mixed * gate_silu
+        grad = grad_ref[...]
+        gain_term = jnp.sum(grad * (gated * scale), axis=0, keepdims=True)
+        grad_gated = scale * (grad * gain) - gated * (scale * scale * scale * inner / inner_count)
+        grad_mixed = grad_gated * gate_silu
+        back_ref[places_of[sub], :width] = (
+            grad_gated * mixed * (gate_sig + gate_silu * (1.0 - gate_sig))
+        ).astype(BF16)
+        chans_out[0:1, :] += jnp.sum(grad_mixed * inputs, axis=0, keepdims=True)
+        chans_out[1:2, :] += gain_term
+        held.append(grad_mixed)
+
+    works = []
+    for parts, grad_mixed in zip(fronts, held):
+        stepped = parts["inputs"] * parts["steps_wide"]
+        stepped_low, grad_low = stepped.astype(BF16), grad_mixed.astype(BF16)
+        scores = dot(parts["queries"], parts["keys"], 1, 1)
+        grad_scores = jnp.zeros((length, length), F32)
+        row_sums = jnp.zeros((length, length), F32)
+        column_sums, columns = [], []
+        for block in range(head_count // pair):
+            cut = slice(block * LANES, (block + 1) * LANES)
+            source, target = stepped_low[:, cut], grad_low[:, cut]
+            joined = None
+            for k in range(pair):
+                h = block * pair + k
+                spread_h = decay_matrix(parts, h, causal)
+                own_target = jnp.where(head_lane == k, target, jnp.zeros_like(target))
+                pulled = dot(own_target, source, 1, 1) * spread_h
+                grad_scores = grad_scores + pulled
+                moved = pulled * scores
+                row_sums = jnp.where(lane == h, jnp.sum(moved, axis=1, keepdims=True), row_sums)
+                column_sums.append(jnp.sum(moved, axis=0, keepdims=True))
+                got = dot((scores * spread_h).astype(BF16), target, 0, 0)
+                joined = got if joined is None else jnp.where(head_lane == k, got, joined)
+            columns.append(joined)
+        column_sums.append(jnp.zeros((ROWS - head_count, length), F32))
+        differences = jnp.transpose(row_sums)[:ROWS] - jnp.concatenate(column_sums, axis=0)
+        works.append((stepped, grad_scores, jnp.concatenate(columns, axis=1), differences))
+
+    after = carry[...]
     row_lane = lax.broadcasted_iota(jnp.int32, (ROWS, length), 1)
-    grad_running = grad_running + jnp.where(row_lane == length - 1, last, 0.0)
-    grad_decays = exact_left(grad_running, upper_ref[...], 3, 1)
-    grad_steps = head_sums(picker, inputs * grad_stepped)
-    grad_rates = (
-        grad_steps - jnp.exp(heads[ROWS : 2 * ROWS, :]) * grad_decays
-    ) * jax.nn.sigmoid(parts["rates"])
     row_head = lax.broadcasted_iota(jnp.int32, (ROWS, length), 0)
-    grad_rates = jnp.where(row_head < head_count, grad_rates, 0.0)
-    heads_out[0:ROWS, :] += grad_rates
-    heads_out[ROWS : 2 * ROWS, :] += grad_decays * parts["decays"]
-    back_ref[:, 2 * width + 2 * state :] = jnp.transpose(
-        jnp.concatenate([grad_rates, jnp.zeros((LANES - ROWS, length), F32)], axis=0)
-    ).astype(BF16)
-
-    grad_inputs = parts["steps_wide"] * grad_stepped + skip * grad_mixed
-    grown_low = (grown_wide * grad_mixed).astype(BF16)
-    scores_low = grad_scores.astype(BF16)
-    grad_queries = dot(scores_low, keys) + dot(grown_low, before_low)
-    grad_keys = dot(scores_low, queries, 0, 0) + dot(
-        (stepped * tail_wide).astype(BF16), after_low
-    )
-    carry[...] = kept + dot(grown_low, queries, 0, 0)
-
-    sig, summed = parts["sig"], parts["summed"]
-    grad_v = jnp.concatenate([grad_inputs, grad_keys, grad_queries], axis=1) * (
-        sig + summed * sig * (1.0 - sig)
-    )
-    later[0:length, :] = grad_v
-    grad_conv = taps[3:4, :] * grad_v
-    taps_out[4:5, :] += jnp.sum(grad_v, axis=0, keepdims=True)
-    for tap in range(4):
-        if tap < 3:
-            grad_conv = grad_conv + taps[tap : tap + 1, :] * later[3 - tap : 3 - tap + length, :]
-        taps_out[tap : tap + 1, :] += jnp.sum(
-            grad_v * window[5 + tap : 5 + tap + length, :], axis=0, keepdims=True
+    for sub, (parts, grad_mixed, work) in enumerate(zip(fronts, held, works)):
+        inputs, keys, queries = parts["inputs"], parts["keys"], parts["queries"]
+        stepped, grad_scores, inside, differences = work
+        window, later = windows[sub], laters[sub]
+        before = state_ref[1 - sub]
+        before_low, after_low = before.astype(BF16), after.astype(BF16)
+        tail_wide, grown_wide = parts["tail_wide"], parts["grown_wide"]
+        through = tail_wide * dot(keys, after_low, 1, 1)
+        grad_stepped = inside + through
+        ended = stepped * through
+        carried = dot(queries, before_low, 1, 1) * grown_wide
+        kept = per_row(parts["whole_decay"], head_count, head_size) * after
+        kept_sum = jnp.sum(kept * before, axis=1, keepdims=True)
+        kept_heads = jnp.concatenate(
+            [
+                jnp.sum(kept_sum[h * head_size : (h + 1) * head_size], axis=0, keepdims=True)
+                for h in range(head_count)
+            ]
+            + [jnp.zeros((ROWS - head_count, 1), F32)],
+            axis=0,
         )
-    later[length : length + ROWS, :] = grad_v[0:ROWS]
-    back_ref[:, width : width + conv_width] = grad_conv.astype(BF16)
+        ended_heads = head_sums(picker, ended)
+        grad_running = differences + head_sums(picker, grad_mixed * carried) - ended_heads
+        last = jnp.sum(ended_heads, axis=1, keepdims=True) + kept_heads
+        grad_running = grad_running + jnp.where(row_lane == length - 1, last, 0.0)
+        grad_decays = exact_left(grad_running, upper_ref[...], 3, 1)
+        grad_steps = head_sums(picker, inputs * grad_stepped)
+        grad_rates = (
+            grad_steps - jnp.exp(heads[ROWS : 2 * ROWS, :]) * grad_decays
+        ) * jax.nn.sigmoid(parts["rates"])
+        grad_rates = jnp.where(row_head < head_count, grad_rates, 0.0)
+        heads_out[0:ROWS, :] += grad_rates
+        heads_out[ROWS : 2 * ROWS, :] += grad_decays * parts["decays"]
+        back_ref[places_of[sub], 2 * width + 2 * state :] = jnp.transpose(
+            jnp.concatenate([grad_rates, jnp.zeros((LANES - ROWS, length), F32)], axis=0)
+        ).astype(BF16)
+
+        grad_inputs = parts["steps_wide"] * grad_stepped + skip * grad_mixed
+        grown_low = (grown_wide * grad_mixed).astype(BF16)
+        scores_low = grad_scores.astype(BF16)
+        grad_queries = dot(scores_low, keys) + dot(grown_low, before_low)
+        grad_keys = dot(scores_low, queries, 0, 0) + dot(
+            (stepped * tail_wide).astype(BF16), after_low
+        )
+        after = kept + dot(grown_low, queries, 0, 0)
+
+        sig, summed = parts["sig"], parts["summed"]
+        grad_v = jnp.concatenate([grad_inputs, grad_keys, grad_queries], axis=1) * (
+            sig + summed * sig * (1.0 - sig)
+        )
+        later[0:length, :] = grad_v
+        grad_conv = taps[3:4, :] * grad_v
+        taps_out[4:5, :] += jnp.sum(grad_v, axis=0, keepdims=True)
+        for tap in range(4):
+            if tap < 3:
+                moved = later[3 - tap : 3 - tap + length, :]
+                grad_conv = grad_conv + taps[tap : tap + 1, :] * moved
+            taps_out[tap : tap + 1, :] += jnp.sum(
+                grad_v * window[5 + tap : 5 + tap + length, :], axis=0, keepdims=True
+            )
+        laters[1 - sub][length : length + ROWS, :] = grad_v[0:ROWS]
+        back_ref[places_of[sub], conv] = grad_conv.astype(BF16)
+    carry[...] = after
 
 
 def tables(width, head_size):
     channel_head = jnp.arange(width)[None, :] // head_size
     rows = jnp.arange(LANES)[:, None]
     spread = jnp.concatenate(
-        [rows == channel_head + ROWS * kind for kind in (0, 2, 3)], axis=1
+        [rows % (LANES // 2) == channel_head + ROWS * kind for kind in (0, 2, 3)], axis=1
     ).astype(BF16)
     upper = (rows <= jnp.arange(LANES)[None, :]).astype(BF16)
     picker = (jnp.arange(ROWS)[:, None] == channel_head).astype(BF16)
@@ -894,13 +928,18 @@
     spread, upper, _ = tabs
     tokens, columns = raw.shape
     count = tokens // STRETCH
+
+    def moved(sub):
+        return pl.BlockSpec((STRETCH, columns), lambda i, order: (order[2 * i + sub], 0))
+
     return pl.pallas_call(
         lambda *refs: forward_kernel(head_size, *refs),
         grid_spec=pltpu.PrefetchScalarGridSpec(
             num_scalar_prefetch=1,
-            grid=(count,),
+            grid=(count // 2,),
             in_specs=[
-                pl.BlockSpec((STRETCH, columns), lambda i, order: (order[i], 0)),
+                moved(0),
+                moved(1),
                 fixed(taps.shape),
                 fixed(chans.shape),
                 fixed(heads.shape),
@@ -908,13 +947,14 @@
                 fixed(upper.shape),
             ],
             out_specs=[
-                pl.BlockSpec((STRETCH, width), lambda i, order: (order[i], 0)),
-                pl.BlockSpec((ROWS, LANES), lambda i, order: (i, 0)),
-                pl.BlockSpec((STRETCH, width), lambda i, order: (i, 0)),
-                pl.BlockSpec((None, width, state), lambda i, order: (i, 0, 0)),
+                fixed((tokens, width)),
+                pl.BlockSpec((2 * ROWS, LANES), lambda i, order: (i, 0)),
+                fixed((tokens, width)),
+                pl.BlockSpec((2, width, state), lambda i, order: (i, 0, 0)),
             ],
             scratch_shapes=[
                 pltpu.VMEM((width, state), F32),
+                pltpu.VMEM((STRETCH + ROWS, width + 2 * state), F32),
                 pltpu.VMEM((STRETCH + ROWS, width + 2 * state), F32),
             ],
         ),
@@ -925,12 +965,12 @@
             jax.ShapeDtypeStruct((count, width, state), F32),
         ],
         compiler_params=pltpu.CompilerParams(
-            dimension_semantics=("arbitrary",), vmem_limit_bytes=40 * 2**20
+            dimension_semantics=("arbitrary",), vmem_limit_bytes=20 * 2**20
         ),
         cost_estimate=pl.CostEstimate(
             flops=11_000_000_000, bytes_accessed=10_000_000, transcendentals=0
         ),
-    )(order, raw, taps, chans, heads, spread, upper)
+    )(order, raw, raw, taps, chans, heads, spread, upper)
 
 
 def mix_backward(grad, raw, mixed, states, token_rows, order, small, tabs, head_size, inner_count):
@@ -941,27 +981,31 @@
     count = tokens // STRETCH
     per = STRETCH // ROWS
 
-    def moved(i, order):
-        return (order[count - 1 - i], 0)
-
-    def back(i, order):
-        return (count - 1 - i, 0)
+    steps = count // 2
+
+    def moved(sub, extent):
+        return pl.BlockSpec(
+            (STRETCH, extent), lambda i, order: (order[count - 1 - 2 * i - sub], 0)
+        )
 
     def past(i, order):
-        return (order[jnp.maximum(count - 2 - i, 0)] * per + per - 1, 0)
+        return (order[jnp.maximum(count - 3 - 2 * i, 0)] * per + per - 1, 0)
 
     return pl.pallas_call(
         lambda *refs: backward_kernel(head_size, inner_count, *refs),
         grid_spec=pltpu.PrefetchScalarGridSpec(
             num_scalar_prefetch=1,
-            grid=(count,),
+            grid=(steps,),
             in_specs=[
-                pl.BlockSpec((STRETCH, width), moved),
-                pl.BlockSpec((STRETCH, columns), moved),
+                moved(0, width),
+                moved(1, width),
+                moved(0, columns),
+                moved(1, columns),
                 pl.BlockSpec((ROWS, columns), past),
-                pl.BlockSpec((STRETCH, width), back),
-                pl.BlockSpec((None, width, state), lambda i, order: (count - 1 - i, 0, 0)),
-                pl.BlockSpec((ROWS, LANES), back),
+                moved(0, width),
+                moved(1, width),
+                pl.BlockSpec((2, width, state), lambda i, order: (steps - 1 - i, 0, 0)),
+                pl.BlockSpec((2 * ROWS, LANES), lambda i, order: (steps - 1 - i, 0)),
                 fixed(taps.shape),
                 fixed(chans.shape),
                 fixed(heads.shape),
@@ -970,16 +1014,13 @@
                 fixed(picker.shape),
             ],
             out_specs=[
-                pl.BlockSpec((STRETCH, columns), moved),
+                fixed((tokens, columns)),
                 fixed(taps.shape),
                 fixed(chans.shape),
                 fixed(heads.shape),
             ],
-            scratch_shapes=[
-                pltpu.VMEM((width, state), F32),
-                pltpu.VMEM((STRETCH + ROWS, width + 2 * state), F32),
-                pltpu.VMEM((STRETCH + ROWS, width + 2 * state), F32),
-            ],
+            scratch_shapes=[pltpu.VMEM((width, state), F32)]
+            + [pltpu.VMEM((STRETCH + ROWS, width + 2 * state), F32) for _ in range(4)],
         ),
         out_shape=[
             jax.ShapeDtypeStruct((tokens, columns), BF16),
@@ -988,12 +1029,29 @@
             jax.ShapeDtypeStruct(heads.shape, F32),
         ],
         compiler_params=pltpu.CompilerParams(
-            dimension_semantics=("arbitrary",), vmem_limit_bytes=40 * 2**20
+            dimension_semantics=("arbitrary",), vmem_limit_bytes=24 * 2**20
         ),
         cost_estimate=pl.CostEstimate(
             flops=23_000_000_000, bytes_accessed=16_000_000, transcendentals=0
         ),
-    )(order, grad, raw, raw, mixed, states, token_rows, taps, chans, heads, spread, upper, picker)
+    )(
+        order,
+        grad,
+        grad,
+        raw,
+        raw,
+        raw,
+        mixed,
+        mixed,
+        states,
+        token_rows,
+        taps,
+        chans,
+        heads,
+        spread,
+        upper,
+        picker,
+    )
 
 
 def small_kernel(layers, heads_here, head_count, state, spot_ref, place_ref, arrived_ref, out_ref):
@@ -1028,7 +1086,7 @@
         lambda *refs: small_kernel(layers, heads_here, head_count, state, *refs),
         in_specs=[scalars, scalars, pl.BlockSpec(memory_space=pltpu.VMEM)],
         out_shape=jax.ShapeDtypeStruct((layers, line * 4 * share, columns), BF16),
-        compiler_params=pltpu.CompilerParams(vmem_limit_bytes=40 * 2**20),
+        compiler_params=pltpu.CompilerParams(vmem_limit_bytes=14 * 2**20),
     )(spots, jnp.stack([place, core]).astype(jnp.int32), arrived)
 
 
@@ -1065,7 +1123,7 @@
             jax.ShapeDtypeStruct((2, share, 2 * state), F32),
             jax.ShapeDtypeStruct((2, 4 * head_count, share), F32),
         ],
-        compiler_params=pltpu.CompilerParams(vmem_limit_bytes=40 * 2**20),
+        compiler_params=pltpu.CompilerParams(vmem_limit_bytes=14 * 2**20),
     )(first, second, first_out, second_out)
 
 

time: 687 us -> 666 us (0.969)
  Pallas kernels: 127 us -> 112 us
  starting transfers between devices: 131 us -> 124 us
    ppermute x59, waiting for transfers between devices: 54.2 us -> 63.7 us  [hop(): return lax.ppermute(value, GROUP, pairs)]
    ppermute x12, starting transfers between devices: 21.4 us -> 13.6 us  [line_shift(): lax.ppermute(value, axis, [(i, (i + step) % count) for i in range(count)])]
    pallas_call x4, Pallas kernels: 41.3 us -> 33.6 us  [mix_forward(): pl.pallas_call(lambda *refs: forward_kernel(head_size, *refs), grid_spec=...]
    unnamed x353 -> x375, local copies, waits for them, and re-layouts: 60.7 us -> 58.6 us
  transfers between devices with their start and end apart: 131 -> 131, of which waited for: 26 -> 29; matrix products, arithmetic and copies ran while one was open for 42% -> 43% of each run, Pallas kernels for 18% -> 17%
where the time goes in v3:
time: 666 us; the launch traced here: 658 us
  starting transfers between devices  124 us (19%)
  matrix products  122 us (18%)
  local copies, waits for them, and re-layouts  118 us (18%)
  Pallas kernels  112 us (17%)
  waiting for transfers between devices  94.5 us (14%)
  other arithmetic  70.8 us (11%)
  between operations  17.3 us (3%)
    dot_general x32, matrix products, dot(): lax.dot_general(left, right, (((left_dim,), (right_dim,)), ((), ())), pre...  122 us
    pallas_call x4, Pallas kernels, mix_backward(): pl.pallas_call(lambda *refs: backward_kernel(head_size, inner_count, *ref...  76.5 us
    ppermute x59, waiting for transfers between devices, hop(): return lax.ppermute(value, GROUP, pairs)  63.7 us
    unnamed x375, local copies, waits for them, and re-layouts  58.6 us
    ppermute x59, starting transfers between devices, hop(): return lax.ppermute(value, GROUP, pairs)  46.2 us
    ppermute x31, starting transfers between devices, swap(): return lax.ppermute(value, 'tensor', [(0, 1), (1, 0)])  39.7 us
    pallas_call x4, Pallas kernels, mix_forward(): pl.pallas_call(lambda *refs: forward_kernel(head_size, *refs), grid_spec=...  33.6 us
    ppermute x18, starting transfers between devices, trade_steps(): lax.ppermute(value, 'seq', [(i, i ^ turn) for i in range(4)])  17.3 us
  transfers between devices with their start and end apart: 131, of which 29 were waited for; matrix products, arithmetic and copies ran while one was open for 43% of the time, Pallas kernels for 17%

profile of v3, /device:TPU:1, one launch (start us, length us, event | category | flops | bytes accessed | tf_op | source)
XLA Modules:
  0.0 658.3 jit_solution(4876276677604686898)
XLA Ops:
  51.7 7.7 %collective-permute-done.4 = bf16[384,768]{1,0:T(8,128)(2,1)} collective-permute-done((bf16[384,768]{1,0:T(8,128)(2,1)}, bf16[384,768]{1,0:T(8,128)(2,1)}, u32[]{:S(2)}, u32[]{:S(2)}) %collective-permute-start.4) | collective-permute-done | bytes 589856 | tf_op jit(solution)/shard_map/ppermute | solution.py:492
  88.5 8.3 %collective-permute-start.22 = (bf16[4,4,96,384]{3,2,1,0:T(8,128)(2,1)S(1)}, bf16[4,4,96,384]{3,2,1,0:T(8,128)(2,1)S(1)}, u32[]{:S(2)}, u32[]{:S(2)}) collective-permute-start(bf16[4,4,96,384]{3,2,1,0:T(8,128)(2,1)S(1)} %pad_maximum_fusion.9), channel_id=1, source_target_pairs={{0,1},{1,0},{2,3},{3,2},{4,5},{5,4},{6,7},{7,6},{8,9},{9,8},{10,11... | collective-permute-start | bytes 3538952 | tf_op jit(solution)/shard_map/ppermute | solution.py:473
  124.9 8.2 %collective-permute-done.23 = bf16[128,1536]{1,0:T(8,128)(2,1)} collective-permute-done((bf16[128,1536]{1,0:T(8,128)(2,1)S(1)}, bf16[128,1536]{1,0:T(8,128)(2,1)}, u32[]{:S(2)}, u32[]{:S(2)}) %collective-permute-start.23) | collective-permute-done | bytes 393248 | tf_op jit(solution)/shard_map/ppermute | solution.py:469
  135.1 8.3 %shard_map.263 = (bf16[1024,384]{1,0:T(8,128)(2,1)S(1)}, f32[64,128]{1,0:T(8,128)S(1)}, f32[1024,384]{1,0:T(8,128)S(1)}, f32[8,384,128]{2,1,0:T(8,128)S(1)}) custom-call(s32[8]{0:T(128)S(1)} %get-tuple-element.518.refs_0_, f32[1024,1152]{1,0:T(8,128)S(1)} %fusion.135.refs_1_.refs_2_.refs_3_.refs_4_.refs_5_, ...), custom_call_target="tpu_custom_call" | custom-call | flops 11000000512 | bytes 10000000 | tf_op jit(solution)/shard_map/pallas_call | solution.py:935
  152.3 5.8 fusion.136.refs_1_.refs_2_.refs_3_.refs_4_.refs_5_
  176.1 8.7 %shard_map.264 = (bf16[1024,384]{1,0:T(8,128)(2,1)S(1)}, f32[64,128]{1,0:T(8,128)S(1)}, f32[1024,384]{1,0:T(8,128)S(1)}, f32[8,384,128]{2,1,0:T(8,128)S(1)}) custom-call(s32[8]{0:T(128)S(1)} %get-tuple-element.518.refs_0_, f32[1024,1152]{1,0:T(8,128)S(1)} %bitcast.541, f32[1024,1152]{1,0:T(8,128)S(1)} %bitcast.541, ...), custom_call_target="tpu_custom_call" | custom-call | flops 11000000512 | bytes 10000000 | tf_op jit(solution)/shard_map/pallas_call | solution.py:935
  203.8 8.4 %collective-permute-done.49 = f32[8,128]{1,0:T(8,128)S(1)} collective-permute-done((f32[8,128]{1,0:T(8,128)S(1)}, f32[8,128]{1,0:T(8,128)S(1)}, u32[]{:S(2)}, u32[]{:S(2)}) %collective-permute-start.49) | collective-permute-done | bytes 4128 | tf_op jit(solution)/shard_map/ppermute | solution.py:469
  216.4 8.3 %collective-permute-done.46 = bf16[128,1536]{1,0:T(8,128)(2,1)S(1)} collective-permute-done((bf16[128,1536]{1,0:T(8,128)(2,1)S(1)}, bf16[128,1536]{1,0:T(8,128)(2,1)S(1)}, u32[]{:S(2)}, u32[]{:S(2)}) %collective-permute-start.46) | collective-permute-done | bytes 393248 | tf_op jit(solution)/shard_map/ppermute | solution.py:469
  241.7 8.4 %shard_map.265 = (bf16[1024,384]{1,0:T(8,128)(2,1)S(1)}, f32[64,128]{1,0:T(8,128)S(1)}, f32[1024,384]{1,0:T(8,128)S(1)}, f32[8,384,128]{2,1,0:T(8,128)S(1)}) custom-call(s32[8]{0:T(128)S(1)} %get-tuple-element.518.refs_0_, f32[1024,1152]{1,0:T(8,128)S(1)} %fusion.111.refs_1_.refs_2_.refs_3_.refs_4_.refs_5_, ...), custom_call_target="tpu_custom_call" | custom-call | flops 11000000512 | bytes 10000000 | tf_op jit(solution)/shard_map/pallas_call | solution.py:935
  266.9 8.3 %shard_map.266 = (bf16[1024,384]{1,0:T(8,128)(2,1)S(1)}, f32[64,128]{1,0:T(8,128)S(1)}, f32[1024,384]{1,0:T(8,128)S(1)}, f32[8,384,128]{2,1,0:T(8,128)S(1)}) custom-call(s32[8]{0:T(128)S(1)} %get-tuple-element.518.refs_0_, f32[1024,1152]{1,0:T(8,128)S(1)} %fusion.110.refs_1_.refs_2_.refs_3_.refs_4_.refs_5_, ...), custom_call_target="tpu_custom_call" | custom-call | flops 11000000512 | bytes 10000000 | tf_op jit(solution)/shard_map/pallas_call | solution.py:935
  291.7 5.3 fusion.61.refs_1_.refs_2_
  328.2 19.0 %shard_map.267 = (bf16[1024,1152]{1,0:T(8,128)(2,1)S(1)}, f32[8,640]{1,0:T(8,128)S(1)}, f32[8,384]{1,0:T(8,128)S(1)}, f32[16,128]{1,0:T(8,128)S(1)}) custom-call(s32[8]{0:T(128)S(1)} %get-tuple-element.518.refs_0_, f32[1024,384]{1,0:T(8,128)S(1)} %copy-done.6, f32[1024,384]{1,0:T(8,128)S(1)} %copy-done.6, f32[1024,1152]{1,0:T(8,128)S(1)} %copy-done.19, ...), custom_call_target="tpu_custom_call" | custom-call | flops 23000000512 | bytes 16000000 | tf_op jit(solution)/shard_map/pallas_call | solution.py:994
  364.6 19.5 %shard_map.268 = (bf16[1024,1152]{1,0:T(8,128)(2,1)S(1)}, f32[8,640]{1,0:T(8,128)S(1)}, f32[8,384]{1,0:T(8,128)S(1)}, f32[16,128]{1,0:T(8,128)S(1)}) custom-call(s32[8]{0:T(128)S(1)} %get-tuple-element.518.refs_0_, f32[1024,384]{1,0:T(8,128)S(1)} %copy-done.5, f32[1024,384]{1,0:T(8,128)S(1)} %copy-done.5, f32[1024,1152]{1,0:T(8,128)S(1)} %bitcast.545, ...), custom_call_target="tpu_custom_call" | custom-call | flops 23000000512 | bytes 16000000 | tf_op jit(solution)/shard_map/pallas_call | solution.py:994
  389.4 5.3 fusion.2
  404.3 5.5 fusion.10
  413.2 9.1 %fusion.137 = f32[1536,1152]{1,0:T(8,128)} fusion(bf16[1024,1536]{1,0:T(8,128)(2,1)} %bitcast.620, bf16[1024,1152]{1,0:T(8,128)(2,1)S(1)} %copy-done.12), kind=kOutput, calls=%fused_computation.515 | convolution fusion | flops 3623878656 | bytes 12582912 | tf_op jit(solution)/shard_map/dot_general | solution.py:554
  434.0 5.9 collective-permute-start.92
  448.3 9.5 %fusion = bf16[1536,1152]{1,0:T(8,128)(2,1)} fusion(f32[1536,1152]{1,0:T(8,128)} %fusion.137, bf16[1024,1536]{1,0:T(8,128)(2,1)} %bitcast.622, bf16[1024,1152]{1,0:T(8,128)(2,1)S(1)} %copy-done.10), kind=kOutput, calls=%fused_computation.2 | convolution fusion | flops 3627417600 | bytes 16121856 | tf_op jit(solution)/shard_map/dot_general | solution.py:554
  473.6 19.1 %shard_map.269 = (bf16[1024,1152]{1,0:T(8,128)(2,1)S(1)}, f32[8,640]{1,0:T(8,128)S(1)}, f32[8,384]{1,0:T(8,128)S(1)}, f32[16,128]{1,0:T(8,128)S(1)}) custom-call(s32[8]{0:T(128)S(1)} %get-tuple-element.518.refs_0_, f32[1024,384]{1,0:T(8,128)S(1)} %copy-done.7, f32[1024,384]{1,0:T(8,128)S(1)} %copy-done.7, f32[1024,1152]{1,0:T(8,128)S(1)} %copy-done.16, ...), custom_call_target="tpu_custom_call" | custom-call | flops 23000000512 | bytes 16000000 | tf_op jit(solution)/shard_map/pallas_call | solution.py:994
  514.8 6.8 %fusion.140 = f32[1536,1152]{1,0:T(8,128)} fusion(bf16[1024,1536]{1,0:T(8,128)(2,1)S(1)} %bitcast.612, bf16[1024,1152]{1,0:T(8,128)(2,1)S(1)} %get-tuple-element.367), kind=kOutput, calls=%fused_computation.518 | convolution fusion | flops 3623878656 | bytes 12582912 | tf_op jit(solution)/shard_map/dot_general | solution.py:554
  521.7 18.9 %shard_map.270 = (bf16[1024,1152]{1,0:T(8,128)(2,1)S(1)}, f32[8,640]{1,0:T(8,128)S(1)}, f32[8,384]{1,0:T(8,128)S(1)}, f32[16,128]{1,0:T(8,128)S(1)}) custom-call(s32[8]{0:T(128)S(1)} %get-tuple-element.518.refs_0_, f32[1024,384]{1,0:T(8,128)S(1)} %fusion.139.refs_1_.refs_2_, f32[1024,384]{1,0:T(8,128)S(1)} %fusion.139.refs_1_.refs_2_, ...), custom_call_target="tpu_custom_call" | custom-call | flops 23000000512 | bytes 16000000 | tf_op jit(solution)/shard_map/pallas_call | solution.py:994
  543.2 10.9 %fusion.1 = bf16[1536,1152]{1,0:T(8,128)(2,1)} fusion(f32[1536,1152]{1,0:T(8,128)} %fusion.140, bf16[1024,1536]{1,0:T(8,128)(2,1)} %bitcast.614, bf16[1024,1152]{1,0:T(8,128)(2,1)} %copy-done.13), kind=kOutput, calls=%fused_computation.3 | convolution fusion | flops 3627417600 | bytes 16121856 | tf_op jit(solution)/shard_map/dot_general | solution.py:554
  583.3 5.6 collective-permute-done.103
  597.1 5.5 collective-permute-done.108
  (991 shorter events, 414.6 us)
Async XLA Ops:
  7.2 224.3 %all-gather.2.cloned.1.call-start = ((), (), s32[]{:S(2)}) async-start(), calls=%async_computation.3 | async-start | bytes 4423680 | tf_op jit(solution)/shard_map/all_gather | solution.py:1336
  10.5 26.4 %collective-permute-start.1 = (bf16[96,768]{1,0:T(8,128)(2,1)}, bf16[96,768]{1,0:T(8,128)(2,1)}, u32[]{:S(2)}, u32[]{:S(2)}) collective-permute-start(bf16[96,768]{1,0:T(8,128)(2,1)} %pad_maximum_fusion.12), channel_id=1, source_target_pairs={{0,2},{2,0},{4,6},{6,4},{1,3},{3,1},{5,7},{7,5},{8,10},{10,8},{12,... | collective-permute-start | bytes 442376 | tf_op jit(solution)/shard_map/ppermute | solution.py:1347
  13.3 27.6 %collective-permute-start.2 = (bf16[96,768]{1,0:T(8,128)(2,1)}, bf16[96,768]{1,0:T(8,128)(2,1)}, u32[]{:S(2)}, u32[]{:S(2)}) collective-permute-start(bf16[96,768]{1,0:T(8,128)(2,1)} %pad_maximum_fusion.13), channel_id=1, source_target_pairs={{0,4},{2,6},{4,0},{6,2},{1,5},{3,7},{5,1},{7,3},{8,12},{10,14},{12... | collective-permute-start | bytes 442376 | tf_op jit(solution)/shard_map/ppermute | solution.py:1347
  15.2 28.2 %collective-permute-start.3 = (bf16[96,768]{1,0:T(8,128)(2,1)}, bf16[96,768]{1,0:T(8,128)(2,1)}, u32[]{:S(2)}, u32[]{:S(2)}) collective-permute-start(bf16[96,768]{1,0:T(8,128)(2,1)} %pad_maximum_fusion.14), channel_id=1, source_target_pairs={{0,6},{2,4},{4,2},{6,0},{1,7},{3,5},{5,3},{7,1},{8,14},{10,12},{12... | collective-permute-start | bytes 442376 | tf_op jit(solution)/shard_map/ppermute | solution.py:1347
  15.9 29.6 %collective-permute-start.6 = (bf16[96,384]{1,0:T(8,128)(2,1)}, bf16[96,384]{1,0:T(8,128)(2,1)}, u32[]{:S(2)}, u32[]{:S(2)}) collective-permute-start(bf16[96,384]{1,0:T(8,128)(2,1)} %get-tuple-element.599), channel_id=1, source_target_pairs={{0,8},{8,16},{16,24},{24,0},{1,9},{9,17},{17,25},{25,1},{2,10},{10... | collective-permute-start | bytes 221192 | tf_op jit(solution)/shard_map/ppermute | solution.py:492
  21.6 29.7 %collective-permute-start = (bf16[128,1536]{1,0:T(8,128)(2,1)}, bf16[128,1536]{1,0:T(8,128)(2,1)}, u32[]{:S(2)}, u32[]{:S(2)}) collective-permute-start(bf16[128,1536]{1,0:T(8,128)(2,1)} %get-tuple-element.221), channel_id=1, source_target_pairs={{0,2},{1,5},{2,0},{3,7},{4,6},{5,1},{6,4},{7,3},{8,10},{9,13},{10,... | collective-permute-start | bytes 1179656 | tf_op jit(solution)/shard_map/ppermute | solution.py:469
  51.4 30.1 %collective-permute-start.14 = (bf16[128,1536]{1,0:T(8,128)(2,1)}, bf16[128,1536]{1,0:T(8,128)(2,1)}, u32[]{:S(2)}, u32[]{:S(2)}) collective-permute-start(bf16[128,1536]{1,0:T(8,128)(2,1)} %get-tuple-element.224), channel_id=1, source_target_pairs={{0,4},{1,3},{2,6},{3,1},{4,0},{5,7},{6,2},{7,5},{8,12},{9,11},{10,... | collective-permute-start | bytes 1179656 | tf_op jit(solution)/shard_map/ppermute | solution.py:469
  61.5 37.6 %collective-permute-start.20 = (bf16[384,768]{1,0:T(8,128)(2,1)}, bf16[384,768]{1,0:T(8,128)(2,1)}, u32[]{:S(2)}, u32[]{:S(2)}) collective-permute-start(bf16[384,768]{1,0:T(8,128)(2,1)} %bitcast.22), channel_id=1, source_target_pairs={{0,16},{8,24},{16,0},{24,8},{1,17},{9,25},{17,1},{25,9},{2,18},{10... | collective-permute-start | bytes 1769480 | tf_op jit(solution)/shard_map/ppermute | solution.py:492
  120.0 29.8 %collective-permute-start.31 = (bf16[4,128,1536]{2,1,0:T(8,128)(2,1)S(1)}, bf16[4,128,1536]{2,1,0:T(8,128)(2,1)S(1)}, u32[]{:S(2)}, u32[]{:S(2)}) collective-permute-start(bf16[4,128,1536]{2,1,0:T(8,128)(2,1)S(1)} %pad_maximum_fusion.2), channel_id=1, source_target_pairs={{0,1},{1,0},{2,3},{3,2},{4,5},{5,4},{6,7},{7,6},{8,9},{9,8},{10,11... | collective-permute-start | bytes 4718600 | tf_op jit(solution)/shard_map/ppermute | solution.py:473
  121.5 37.7 %collective-permute-start.30 = (bf16[128,1536]{1,0:T(8,128)(2,1)S(1)}, bf16[128,1536]{1,0:T(8,128)(2,1)S(1)}, u32[]{:S(2)}, u32[]{:S(2)}) collective-permute-start(bf16[128,1536]{1,0:T(8,128)(2,1)S(1)} %copy-done.45), channel_id=1, source_target_pairs={{0,4},{1,3},{2,6},{3,1},{4,0},{5,7},{6,2},{7,5},{8,12},{9,11},{10,... | collective-permute-start | bytes 1179656 | tf_op jit(solution)/shard_map/ppermute | solution.py:469
  161.4 417.3 %reduce-scatter.4.cloned.1.call-start = ((), (), s32[]{:S(2)}) async-start(), calls=%async_computation.4 | async-start | bytes 1474560 | tf_op jit(solution)/shard_map/reduce_scatter | solution.py:1552
  167.3 32.2 %collective-permute-start.73 = (bf16[4,128,1536]{2,1,0:T(8,128)(2,1)S(1)}, bf16[4,128,1536]{2,1,0:T(8,128)(2,1)S(1)}, u32[]{:S(2)}, u32[]{:S(2)}) collective-permute-start(bf16[4,128,1536]{2,1,0:T(8,128)(2,1)S(1)} %pad_maximum_fusion.3), channel_id=1, source_target_pairs={{0,1},{1,0},{2,3},{3,2},{4,5},{5,4},{6,7},{7,6},{8,9},{9,8},{10,11... | collective-permute-start | bytes 4718600 | tf_op jit(solution)/shard_map/ppermute | solution.py:473
  169.1 31.0 %collective-permute-start.72 = (bf16[4,128,1536]{2,1,0:T(8,128)(2,1)S(1)}, bf16[4,128,1536]{2,1,0:T(8,128)(2,1)S(1)}, u32[]{:S(2)}, u32[]{:S(2)}) collective-permute-start(bf16[4,128,1536]{2,1,0:T(8,128)(2,1)S(1)} %pad_maximum_fusion.4), channel_id=1, source_target_pairs={{0,1},{1,0},{2,3},{3,2},{4,5},{5,4},{6,7},{7,6},{8,9},{9,8},{10,11... | collective-permute-start | bytes 4718600 | tf_op jit(solution)/shard_map/ppermute | solution.py:473
  303.7 124.4 %collective-permute-start.62 = (f32[128,1536]{1,0:T(8,128)}, f32[128,1536]{1,0:T(8,128)}, u32[]{:S(2)}, u32[]{:S(2)}) collective-permute-start(f32[128,1536]{1,0:T(8,128)} %get-tuple-element.522), channel_id=1, source_target_pairs={{0,1},{1,0},{2,3},{3,2},{4,5},{5,4},{6,7},{7,6},{8,9},{9,8},{10,11... | collective-permute-start | bytes 2359304 | tf_op jit(solution)/shard_map/ppermute | solution.py:473
  358.2 70.6 %collective-permute-start.71 = (f32[128,1536]{1,0:T(8,128)}, f32[128,1536]{1,0:T(8,128)}, u32[]{:S(2)}, u32[]{:S(2)}) collective-permute-start(f32[128,1536]{1,0:T(8,128)} %get-tuple-element.520), channel_id=1, source_target_pairs={{0,1},{1,0},{2,3},{3,2},{4,5},{5,4},{6,7},{7,6},{8,9},{9,8},{10,11... | collective-permute-start | bytes 2359304 | tf_op jit(solution)/shard_map/ppermute | solution.py:473
  424.0 180.6 %reduce-scatter.6.cloned.1.call-start = ((), (), s32[]{:S(2)}) async-start(), calls=%async_computation.5 | async-start | bytes 4423680 | tf_op jit(solution)/shard_map/reduce_scatter | solution.py:1552
  448.0 44.7 %collective-permute-start.93 = (bf16[128,1536]{1,0:T(8,128)(2,1)}, bf16[128,1536]{1,0:T(8,128)(2,1)}, u32[]{:S(2)}, u32[]{:S(2)}) collective-permute-start(bf16[128,1536]{1,0:T(8,128)(2,1)} %copy-done.59), channel_id=1, source_target_pairs={{0,4},{1,3},{2,6},{3,1},{4,0},{5,7},{6,2},{7,5},{8,12},{9,11},{10,... | collective-permute-start | bytes 1179656 | tf_op jit(solution)/shard_map/ppermute | solution.py:469
  457.9 166.0 %reduce-scatter.8.cloned.1.call-start = ((), (), s32[]{:S(2)}) async-start(), calls=%async_computation.6 | async-start | bytes 4423680 | tf_op jit(solution)/shard_map/reduce_scatter | solution.py:1552
  465.6 28.3 %collective-permute-start.95 = (f32[8,128]{1,0:T(8,128)S(1)}, f32[8,128]{1,0:T(8,128)S(1)}, u32[]{:S(2)}, u32[]{:S(2)}) collective-permute-start(f32[8,128]{1,0:T(8,128)S(1)} %add.744), channel_id=1, source_target_pairs={{0,4},{1,3},{2,6},{3,1},{4,0},{5,7},{6,2},{7,5},{8,12},{9,11},{10,... | collective-permute-start | bytes 12296 | tf_op jit(solution)/shard_map/ppermute | solution.py:469
  466.8 29.6 %collective-permute-start.94 = (bf16[128,1536]{1,0:T(8,128)(2,1)S(1)}, bf16[128,1536]{1,0:T(8,128)(2,1)S(1)}, u32[]{:S(2)}, u32[]{:S(2)}) collective-permute-start(bf16[128,1536]{1,0:T(8,128)(2,1)S(1)} %collective-permute-done.90), channel_id=1, source_target_pairs={{0,4},{1,3},{2,6},{3,1},{4,0},{5,7},{6,2},{7,5},{8,12},{9,11},{10,... | collective-permute-start | bytes 1179656 | tf_op jit(solution)/shard_map/ppermute | solution.py:469
  505.1 49.0 %collective-permute-start.97 = (bf16[2,128,1536]{2,1,0:T(8,128)(2,1)}, bf16[2,128,1536]{2,1,0:T(8,128)(2,1)}, u32[]{:S(2)}, u32[]{:S(2)}) collective-permute-start(bf16[2,128,1536]{2,1,0:T(8,128)(2,1)} %fusion.14), channel_id=1, source_target_pairs={{0,4},{1,3},{2,6},{3,1},{4,0},{5,7},{6,2},{7,5},{8,12},{9,11},{10,... | collective-permute-start | bytes 2359304 | tf_op jit(solution)/shard_map/ppermute | solution.py:469
  510.5 64.8 %collective-permute-start.105 = (bf16[384,384]{1,0:T(8,128)(2,1)}, bf16[384,384]{1,0:T(8,128)(2,1)}, u32[]{:S(2)}, u32[]{:S(2)}) collective-permute-start(bf16[384,384]{1,0:T(8,128)(2,1)} %get-tuple-element.555), channel_id=1, source_target_pairs={{0,8},{8,16},{16,24},{24,0},{1,9},{9,17},{17,25},{25,1},{2,10},{10... | collective-permute-start | bytes 884744 | tf_op jit(solution)/shard_map/ppermute | solution.py:492
  512.6 62.7 %collective-permute-start.106 = (bf16[384,384]{1,0:T(8,128)(2,1)}, bf16[384,384]{1,0:T(8,128)(2,1)}, u32[]{:S(2)}, u32[]{:S(2)}) collective-permute-start(bf16[384,384]{1,0:T(8,128)(2,1)} %get-tuple-element.554), channel_id=1, source_target_pairs={{0,16},{8,24},{16,0},{24,8},{1,17},{9,25},{17,1},{25,9},{2,18},{10... | collective-permute-start | bytes 884744 | tf_op jit(solution)/shard_map/ppermute | solution.py:492
  512.7 62.7 %collective-permute-start.107 = (bf16[384,384]{1,0:T(8,128)(2,1)}, bf16[384,384]{1,0:T(8,128)(2,1)}, u32[]{:S(2)}, u32[]{:S(2)}) collective-permute-start(bf16[384,384]{1,0:T(8,128)(2,1)} %get-tuple-element.553), channel_id=1, source_target_pairs={{0,24},{8,0},{16,8},{24,16},{1,25},{9,1},{17,9},{25,17},{2,26},{10... | collective-permute-start | bytes 884744 | tf_op jit(solution)/shard_map/ppermute | solution.py:492
  (270 other events, 2635.9 us)
Sparse Core Ops, SparseCore 0:
  161.5 69.8 all-gather.1
  424.1 28.9 reduce-scatter.3
  458.0 76.7 reduce-scatter.5
  554.3 68.8 reduce-scatter.7

commit v4 on v3

--- a/solution.py
+++ b/solution.py
@@ -1101,8 +1101,8 @@
         for index in range(4):
             value = ref[index].astype(F32)
             spot = slice(index * width, (index + 1) * width)
-            inner_ref[layer, 0, :, spot] = value[:, :width]
-            inner_ref[layer, 1, :, spot] = value[:, width : 2 * width]
+            inner_ref[layer, :, 0, spot] = value[:, :width]
+            inner_ref[layer, :, 1, spot] = value[:, width : 2 * width]
             states = states + value[:, 2 * width : 2 * width + 2 * state]
             rate = jnp.concatenate(
                 [value[:, 2 * width + 2 * state :], jnp.zeros((LANES - share, LANES), F32)], axis=0
@@ -1118,7 +1118,7 @@
     return pl.pallas_call(
         lambda *refs: finish_kernel(head_count, state, *refs),
         out_shape=[
-            jax.ShapeDtypeStruct((2, 2, share, 4 * width), F32),
+            jax.ShapeDtypeStruct((2, share, 2, 4 * width), F32),
             jax.ShapeDtypeStruct((2, share, 4 * width), F32),
             jax.ShapeDtypeStruct((2, share, 2 * state), F32),
             jax.ShapeDtypeStruct((2, 4 * head_count, share), F32),
@@ -1523,8 +1523,8 @@
     def term(key, layer, batch, left, right):
         value = dot(left, right, 0, 0)
         if batch > 0:
-            value = value + totals[key, layer, batch - 1]
-        totals[key, layer, batch] = value.astype(BF16) if batch == batches - 1 else value
+            value = value + totals[key, layer, batch - 1].astype(F32)
+        totals[key, layer, batch] = value.astype(BF16)
         return totals[key, layer, batch]
 
     def out_term(layer, batch):
@@ -1658,7 +1658,7 @@
         finished["output"],
         finished["input_grad"],
         small_out[0],
-        inner_grad.transpose(0, 2, 1, 3),
+        inner_grad,
         rate_grad.transpose(0, 2, 1),
         state_grad,
         small_out[2][:, :4],

time: 666 us -> 657 us (0.986)
  local copies, waits for them, and re-layouts: 118 us -> 111 us
    unnamed x375 -> x372, local copies, waits for them, and re-layouts: 58.6 us -> 52.3 us
  transfers between devices with their start and end apart: 131 -> 131, of which waited for: 29 -> 28; matrix products, arithmetic and copies ran while one was open for 43% -> 42% of each run, Pallas kernels for 17% -> 17%
where the time goes in v4:
time: 657 us; the launch traced here: 649 us
  starting transfers between devices  124 us (19%)
  matrix products  118 us (18%)
  Pallas kernels  113 us (17%)
  local copies, waits for them, and re-layouts  111 us (17%)
  waiting for transfers between devices  94.3 us (14%)
  other arithmetic  70.9 us (11%)
  between operations  17.3 us (3%)
    dot_general x32, matrix products, dot(): lax.dot_general(left, right, (((left_dim,), (right_dim,)), ((), ())), pre...  118 us
    pallas_call x4, Pallas kernels, mix_backward(): pl.pallas_call(lambda *refs: backward_kernel(head_size, inner_count, *ref...  76.6 us
    ppermute x59, waiting for transfers between devices, hop(): return lax.ppermute(value, GROUP, pairs)  63.9 us
    unnamed x372, local copies, waits for them, and re-layouts  52.3 us
    ppermute x59, starting transfers between devices, hop(): return lax.ppermute(value, GROUP, pairs)  46.3 us
    ppermute x31, starting transfers between devices, swap(): return lax.ppermute(value, 'tensor', [(0, 1), (1, 0)])  39.9 us
    pallas_call x4, Pallas kernels, mix_forward(): pl.pallas_call(lambda *refs: forward_kernel(head_size, *refs), grid_spec=...  33.6 us
    ppermute x18, starting transfers between devices, trade_steps(): lax.ppermute(value, 'seq', [(i, i ^ turn) for i in range(4)])  17.5 us
  transfers between devices with their start and end apart: 131, of which 28 were waited for; matrix products, arithmetic and copies ran while one was open for 42% of the time, Pallas kernels for 17%

profile of v4, /device:TPU:1, one launch (start us, length us, event | category | flops | bytes accessed | tf_op | source)
XLA Modules:
  0.0 649.3 jit_solution(491289365693808250)
XLA Ops:
  51.7 7.7 %collective-permute-done.4 = bf16[384,768]{1,0:T(8,128)(2,1)} collective-permute-done((bf16[384,768]{1,0:T(8,128)(2,1)}, bf16[384,768]{1,0:T(8,128)(2,1)}, u32[]{:S(2)}, u32[]{:S(2)}) %collective-permute-start.4) | collective-permute-done | bytes 589856 | tf_op jit(solution)/shard_map/ppermute | solution.py:492
  88.6 8.3 %collective-permute-start.22 = (bf16[4,4,96,384]{3,2,1,0:T(8,128)(2,1)S(1)}, bf16[4,4,96,384]{3,2,1,0:T(8,128)(2,1)S(1)}, u32[]{:S(2)}, u32[]{:S(2)}) collective-permute-start(bf16[4,4,96,384]{3,2,1,0:T(8,128)(2,1)S(1)} %pad_maximum_fusion.9), channel_id=1, source_target_pairs={{0,1},{1,0},{2,3},{3,2},{4,5},{5,4},{6,7},{7,6},{8,9},{9,8},{10,11... | collective-permute-start | bytes 3538952 | tf_op jit(solution)/shard_map/ppermute | solution.py:473
  124.9 8.2 %collective-permute-done.23 = bf16[128,1536]{1,0:T(8,128)(2,1)} collective-permute-done((bf16[128,1536]{1,0:T(8,128)(2,1)S(1)}, bf16[128,1536]{1,0:T(8,128)(2,1)}, u32[]{:S(2)}, u32[]{:S(2)}) %collective-permute-start.23) | collective-permute-done | bytes 393248 | tf_op jit(solution)/shard_map/ppermute | solution.py:469
  135.1 8.3 %shard_map.263 = (bf16[1024,384]{1,0:T(8,128)(2,1)S(1)}, f32[64,128]{1,0:T(8,128)S(1)}, f32[1024,384]{1,0:T(8,128)S(1)}, f32[8,384,128]{2,1,0:T(8,128)S(1)}) custom-call(s32[8]{0:T(128)S(1)} %get-tuple-element.458.refs_0_, f32[1024,1152]{1,0:T(8,128)S(1)} %fusion.133.refs_1_.refs_2_.refs_3_.refs_4_.refs_5_, ...), custom_call_target="tpu_custom_call" | custom-call | flops 11000000512 | bytes 10000000 | tf_op jit(solution)/shard_map/pallas_call | solution.py:935
  152.3 5.9 fusion.134.refs_1_.refs_2_.refs_3_.refs_4_.refs_5_
  176.2 8.6 %shard_map.264 = (bf16[1024,384]{1,0:T(8,128)(2,1)S(1)}, f32[64,128]{1,0:T(8,128)S(1)}, f32[1024,384]{1,0:T(8,128)S(1)}, f32[8,384,128]{2,1,0:T(8,128)S(1)}) custom-call(s32[8]{0:T(128)S(1)} %get-tuple-element.458.refs_0_, f32[1024,1152]{1,0:T(8,128)S(1)} %bitcast.539, f32[1024,1152]{1,0:T(8,128)S(1)} %bitcast.539, ...), custom_call_target="tpu_custom_call" | custom-call | flops 11000000512 | bytes 10000000 | tf_op jit(solution)/shard_map/pallas_call | solution.py:935
  204.0 8.3 %collective-permute-done.49 = f32[8,128]{1,0:T(8,128)S(1)} collective-permute-done((f32[8,128]{1,0:T(8,128)S(1)}, f32[8,128]{1,0:T(8,128)S(1)}, u32[]{:S(2)}, u32[]{:S(2)}) %collective-permute-start.49) | collective-permute-done | bytes 4128 | tf_op jit(solution)/shard_map/ppermute | solution.py:469
  216.4 8.3 %collective-permute-done.46 = bf16[128,1536]{1,0:T(8,128)(2,1)S(1)} collective-permute-done((bf16[128,1536]{1,0:T(8,128)(2,1)S(1)}, bf16[128,1536]{1,0:T(8,128)(2,1)S(1)}, u32[]{:S(2)}, u32[]{:S(2)}) %collective-permute-start.46) | collective-permute-done | bytes 393248 | tf_op jit(solution)/shard_map/ppermute | solution.py:469
  241.6 8.4 %shard_map.265 = (bf16[1024,384]{1,0:T(8,128)(2,1)S(1)}, f32[64,128]{1,0:T(8,128)S(1)}, f32[1024,384]{1,0:T(8,128)S(1)}, f32[8,384,128]{2,1,0:T(8,128)S(1)}) custom-call(s32[8]{0:T(128)S(1)} %get-tuple-element.458.refs_0_, f32[1024,1152]{1,0:T(8,128)S(1)} %fusion.109.refs_1_.refs_2_.refs_3_.refs_4_.refs_5_, ...), custom_call_target="tpu_custom_call" | custom-call | flops 11000000512 | bytes 10000000 | tf_op jit(solution)/shard_map/pallas_call | solution.py:935
  266.8 8.3 %shard_map.266 = (bf16[1024,384]{1,0:T(8,128)(2,1)S(1)}, f32[64,128]{1,0:T(8,128)S(1)}, f32[1024,384]{1,0:T(8,128)S(1)}, f32[8,384,128]{2,1,0:T(8,128)S(1)}) custom-call(s32[8]{0:T(128)S(1)} %get-tuple-element.458.refs_0_, f32[1024,1152]{1,0:T(8,128)S(1)} %fusion.108.refs_1_.refs_2_.refs_3_.refs_4_.refs_5_, ...), custom_call_target="tpu_custom_call" | custom-call | flops 11000000512 | bytes 10000000 | tf_op jit(solution)/shard_map/pallas_call | solution.py:935
  291.6 5.3 fusion.59.refs_1_.refs_2_
  328.1 19.0 %shard_map.267 = (bf16[1024,1152]{1,0:T(8,128)(2,1)S(1)}, f32[8,640]{1,0:T(8,128)S(1)}, f32[8,384]{1,0:T(8,128)S(1)}, f32[16,128]{1,0:T(8,128)S(1)}) custom-call(s32[8]{0:T(128)S(1)} %get-tuple-element.458.refs_0_, f32[1024,384]{1,0:T(8,128)S(1)} %copy-done.5, f32[1024,384]{1,0:T(8,128)S(1)} %copy-done.5, f32[1024,1152]{1,0:T(8,128)S(1)} %copy-done.18, ...), custom_call_target="tpu_custom_call" | custom-call | flops 23000000512 | bytes 16000000 | tf_op jit(solution)/shard_map/pallas_call | solution.py:994
  364.1 19.5 %shard_map.268 = (bf16[1024,1152]{1,0:T(8,128)(2,1)S(1)}, f32[8,640]{1,0:T(8,128)S(1)}, f32[8,384]{1,0:T(8,128)S(1)}, f32[16,128]{1,0:T(8,128)S(1)}) custom-call(s32[8]{0:T(128)S(1)} %get-tuple-element.458.refs_0_, f32[1024,384]{1,0:T(8,128)S(1)} %copy-done.4, f32[1024,384]{1,0:T(8,128)S(1)} %copy-done.4, f32[1024,1152]{1,0:T(8,128)S(1)} %bitcast.543, ...), custom_call_target="tpu_custom_call" | custom-call | flops 23000000512 | bytes 16000000 | tf_op jit(solution)/shard_map/pallas_call | solution.py:994
  388.9 5.3 fusion.2
  403.6 5.2 fusion.10
  412.2 8.6 %convolution_convert_fusion.1 = bf16[1536,1152]{1,0:T(8,128)(2,1)} fusion(bf16[1024,1536]{1,0:T(8,128)(2,1)} %bitcast.618, bf16[1024,1152]{1,0:T(8,128)(2,1)S(1)} %copy-done.11), kind=kOutput, calls=%fused_computation.3 | convolution fusion | flops 3625648128 | bytes 9043968 | tf_op jit(solution)/shard_map/dot_general | solution.py:554
  432.5 5.9 collective-permute-start.92
  446.8 8.9 %fusion = bf16[1536,1152]{1,0:T(8,128)(2,1)} fusion(bf16[1024,1536]{1,0:T(8,128)(2,1)} %bitcast.620, bf16[1024,1152]{1,0:T(8,128)(2,1)S(1)} %copy-done.9, bf16[1536,1152]{1,0:T(8,128)(2,1)} %convolution_convert_fusion.1), kind=kOutput, calls=%fused_computation.4 | convolution fusion | flops 3629187072 | bytes 12582912 | tf_op jit(solution)/shard_map/dot_general | solution.py:554
  471.5 19.1 %shard_map.269 = (bf16[1024,1152]{1,0:T(8,128)(2,1)S(1)}, f32[8,640]{1,0:T(8,128)S(1)}, f32[8,384]{1,0:T(8,128)S(1)}, f32[16,128]{1,0:T(8,128)S(1)}) custom-call(s32[8]{0:T(128)S(1)} %get-tuple-element.458.refs_0_, f32[1024,384]{1,0:T(8,128)S(1)} %copy-done.6, f32[1024,384]{1,0:T(8,128)S(1)} %copy-done.6, f32[1024,1152]{1,0:T(8,128)S(1)} %copy-done.15, ...), custom_call_target="tpu_custom_call" | custom-call | flops 23000000512 | bytes 16000000 | tf_op jit(solution)/shard_map/pallas_call | solution.py:994
  512.9 6.2 convolution_convert_fusion
  519.2 19.0 %shard_map.270 = (bf16[1024,1152]{1,0:T(8,128)(2,1)S(1)}, f32[8,640]{1,0:T(8,128)S(1)}, f32[8,384]{1,0:T(8,128)S(1)}, f32[16,128]{1,0:T(8,128)S(1)}) custom-call(s32[8]{0:T(128)S(1)} %get-tuple-element.458.refs_0_, f32[1024,384]{1,0:T(8,128)S(1)} %fusion.136.refs_1_.refs_2_, f32[1024,384]{1,0:T(8,128)S(1)} %fusion.136.refs_1_.refs_2_, ...), custom_call_target="tpu_custom_call" | custom-call | flops 23000000512 | bytes 16000000 | tf_op jit(solution)/shard_map/pallas_call | solution.py:994
  540.8 9.7 %fusion.1 = bf16[1536,1152]{1,0:T(8,128)(2,1)} fusion(bf16[1024,1536]{1,0:T(8,128)(2,1)} %bitcast.612, bf16[1024,1152]{1,0:T(8,128)(2,1)} %copy-done.12, bf16[1536,1152]{1,0:T(8,128)(2,1)} %convolution_convert_fusion), kind=kOutput, calls=%fused_computation.5 | convolution fusion | flops 3629187072 | bytes 12582912 | tf_op jit(solution)/shard_map/dot_general | solution.py:554
  579.7 5.6 collective-permute-done.103
  593.4 5.5 collective-permute-done.108
  (988 shorter events, 409.0 us)
Async XLA Ops:
  7.2 224.2 %all-gather.2.cloned.1.call-start = ((), (), s32[]{:S(2)}) async-start(), calls=%async_computation.3 | async-start | bytes 4423680 | tf_op jit(solution)/shard_map/all_gather | solution.py:1336
  10.5 26.5 %collective-permute-start.1 = (bf16[96,768]{1,0:T(8,128)(2,1)}, bf16[96,768]{1,0:T(8,128)(2,1)}, u32[]{:S(2)}, u32[]{:S(2)}) collective-permute-start(bf16[96,768]{1,0:T(8,128)(2,1)} %pad_maximum_fusion.12), channel_id=1, source_target_pairs={{0,2},{2,0},{4,6},{6,4},{1,3},{3,1},{5,7},{7,5},{8,10},{10,8},{12,... | collective-permute-start | bytes 442376 | tf_op jit(solution)/shard_map/ppermute | solution.py:1347
  13.2 27.6 %collective-permute-start.2 = (bf16[96,768]{1,0:T(8,128)(2,1)}, bf16[96,768]{1,0:T(8,128)(2,1)}, u32[]{:S(2)}, u32[]{:S(2)}) collective-permute-start(bf16[96,768]{1,0:T(8,128)(2,1)} %pad_maximum_fusion.13), channel_id=1, source_target_pairs={{0,4},{2,6},{4,0},{6,2},{1,5},{3,7},{5,1},{7,3},{8,12},{10,14},{12... | collective-permute-start | bytes 442376 | tf_op jit(solution)/shard_map/ppermute | solution.py:1347
  15.2 28.3 %collective-permute-start.3 = (bf16[96,768]{1,0:T(8,128)(2,1)}, bf16[96,768]{1,0:T(8,128)(2,1)}, u32[]{:S(2)}, u32[]{:S(2)}) collective-permute-start(bf16[96,768]{1,0:T(8,128)(2,1)} %pad_maximum_fusion.14), channel_id=1, source_target_pairs={{0,6},{2,4},{4,2},{6,0},{1,7},{3,5},{5,3},{7,1},{8,14},{10,12},{12... | collective-permute-start | bytes 442376 | tf_op jit(solution)/shard_map/ppermute | solution.py:1347
  15.9 29.6 %collective-permute-start.6 = (bf16[96,384]{1,0:T(8,128)(2,1)}, bf16[96,384]{1,0:T(8,128)(2,1)}, u32[]{:S(2)}, u32[]{:S(2)}) collective-permute-start(bf16[96,384]{1,0:T(8,128)(2,1)} %get-tuple-element.539), channel_id=1, source_target_pairs={{0,8},{8,16},{16,24},{24,0},{1,9},{9,17},{17,25},{25,1},{2,10},{10... | collective-permute-start | bytes 221192 | tf_op jit(solution)/shard_map/ppermute | solution.py:492
  21.6 29.8 %collective-permute-start = (bf16[128,1536]{1,0:T(8,128)(2,1)}, bf16[128,1536]{1,0:T(8,128)(2,1)}, u32[]{:S(2)}, u32[]{:S(2)}) collective-permute-start(bf16[128,1536]{1,0:T(8,128)(2,1)} %get-tuple-element.221), channel_id=1, source_target_pairs={{0,2},{1,5},{2,0},{3,7},{4,6},{5,1},{6,4},{7,3},{8,10},{9,13},{10,... | collective-permute-start | bytes 1179656 | tf_op jit(solution)/shard_map/ppermute | solution.py:469
  51.4 30.1 %collective-permute-start.14 = (bf16[128,1536]{1,0:T(8,128)(2,1)}, bf16[128,1536]{1,0:T(8,128)(2,1)}, u32[]{:S(2)}, u32[]{:S(2)}) collective-permute-start(bf16[128,1536]{1,0:T(8,128)(2,1)} %get-tuple-element.224), channel_id=1, source_target_pairs={{0,4},{1,3},{2,6},{3,1},{4,0},{5,7},{6,2},{7,5},{8,12},{9,11},{10,... | collective-permute-start | bytes 1179656 | tf_op jit(solution)/shard_map/ppermute | solution.py:469
  61.6 37.6 %collective-permute-start.20 = (bf16[384,768]{1,0:T(8,128)(2,1)}, bf16[384,768]{1,0:T(8,128)(2,1)}, u32[]{:S(2)}, u32[]{:S(2)}) collective-permute-start(bf16[384,768]{1,0:T(8,128)(2,1)} %bitcast.22), channel_id=1, source_target_pairs={{0,16},{8,24},{16,0},{24,8},{1,17},{9,25},{17,1},{25,9},{2,18},{10... | collective-permute-start | bytes 1769480 | tf_op jit(solution)/shard_map/ppermute | solution.py:492
  119.9 29.9 %collective-permute-start.31 = (bf16[4,128,1536]{2,1,0:T(8,128)(2,1)S(1)}, bf16[4,128,1536]{2,1,0:T(8,128)(2,1)S(1)}, u32[]{:S(2)}, u32[]{:S(2)}) collective-permute-start(bf16[4,128,1536]{2,1,0:T(8,128)(2,1)S(1)} %pad_maximum_fusion.2), channel_id=1, source_target_pairs={{0,1},{1,0},{2,3},{3,2},{4,5},{5,4},{6,7},{7,6},{8,9},{9,8},{10,11... | collective-permute-start | bytes 4718600 | tf_op jit(solution)/shard_map/ppermute | solution.py:473
  121.4 37.8 %collective-permute-start.30 = (bf16[128,1536]{1,0:T(8,128)(2,1)S(1)}, bf16[128,1536]{1,0:T(8,128)(2,1)S(1)}, u32[]{:S(2)}, u32[]{:S(2)}) collective-permute-start(bf16[128,1536]{1,0:T(8,128)(2,1)S(1)} %copy-done.44), channel_id=1, source_target_pairs={{0,4},{1,3},{2,6},{3,1},{4,0},{5,7},{6,2},{7,5},{8,12},{9,11},{10,... | collective-permute-start | bytes 1179656 | tf_op jit(solution)/shard_map/ppermute | solution.py:469
  161.5 413.6 %reduce-scatter.4.cloned.1.call-start = ((), (), s32[]{:S(2)}) async-start(), calls=%async_computation.4 | async-start | bytes 1474560 | tf_op jit(solution)/shard_map/reduce_scatter | solution.py:1552
  167.5 32.2 %collective-permute-start.73 = (bf16[4,128,1536]{2,1,0:T(8,128)(2,1)S(1)}, bf16[4,128,1536]{2,1,0:T(8,128)(2,1)S(1)}, u32[]{:S(2)}, u32[]{:S(2)}) collective-permute-start(bf16[4,128,1536]{2,1,0:T(8,128)(2,1)S(1)} %pad_maximum_fusion.3), channel_id=1, source_target_pairs={{0,1},{1,0},{2,3},{3,2},{4,5},{5,4},{6,7},{7,6},{8,9},{9,8},{10,11... | collective-permute-start | bytes 4718600 | tf_op jit(solution)/shard_map/ppermute | solution.py:473
  169.2 31.0 %collective-permute-start.72 = (bf16[4,128,1536]{2,1,0:T(8,128)(2,1)S(1)}, bf16[4,128,1536]{2,1,0:T(8,128)(2,1)S(1)}, u32[]{:S(2)}, u32[]{:S(2)}) collective-permute-start(bf16[4,128,1536]{2,1,0:T(8,128)(2,1)S(1)} %pad_maximum_fusion.4), channel_id=1, source_target_pairs={{0,1},{1,0},{2,3},{3,2},{4,5},{5,4},{6,7},{7,6},{8,9},{9,8},{10,11... | collective-permute-start | bytes 4718600 | tf_op jit(solution)/shard_map/ppermute | solution.py:473
  303.6 123.1 %collective-permute-start.62 = (f32[128,1536]{1,0:T(8,128)}, f32[128,1536]{1,0:T(8,128)}, u32[]{:S(2)}, u32[]{:S(2)}) collective-permute-start(f32[128,1536]{1,0:T(8,128)} %get-tuple-element.462), channel_id=1, source_target_pairs={{0,1},{1,0},{2,3},{3,2},{4,5},{5,4},{6,7},{7,6},{8,9},{9,8},{10,11... | collective-permute-start | bytes 2359304 | tf_op jit(solution)/shard_map/ppermute | solution.py:473
  357.7 69.7 %collective-permute-start.71 = (f32[128,1536]{1,0:T(8,128)}, f32[128,1536]{1,0:T(8,128)}, u32[]{:S(2)}, u32[]{:S(2)}) collective-permute-start(f32[128,1536]{1,0:T(8,128)} %get-tuple-element.460), channel_id=1, source_target_pairs={{0,1},{1,0},{2,3},{3,2},{4,5},{5,4},{6,7},{7,6},{8,9},{9,8},{10,11... | collective-permute-start | bytes 2359304 | tf_op jit(solution)/shard_map/ppermute | solution.py:473
  422.5 178.5 %reduce-scatter.6.cloned.1.call-start = ((), (), s32[]{:S(2)}) async-start(), calls=%async_computation.5 | async-start | bytes 4423680 | tf_op jit(solution)/shard_map/reduce_scatter | solution.py:1552
  446.4 44.2 %collective-permute-start.93 = (bf16[128,1536]{1,0:T(8,128)(2,1)}, bf16[128,1536]{1,0:T(8,128)(2,1)}, u32[]{:S(2)}, u32[]{:S(2)}) collective-permute-start(bf16[128,1536]{1,0:T(8,128)(2,1)} %copy-done.58), channel_id=1, source_target_pairs={{0,4},{1,3},{2,6},{3,1},{4,0},{5,7},{6,2},{7,5},{8,12},{9,11},{10,... | collective-permute-start | bytes 1179656 | tf_op jit(solution)/shard_map/ppermute | solution.py:469
  455.7 164.6 %reduce-scatter.8.cloned.1.call-start = ((), (), s32[]{:S(2)}) async-start(), calls=%async_computation.6 | async-start | bytes 4423680 | tf_op jit(solution)/shard_map/reduce_scatter | solution.py:1552
  463.5 28.3 %collective-permute-start.95 = (f32[8,128]{1,0:T(8,128)S(1)}, f32[8,128]{1,0:T(8,128)S(1)}, u32[]{:S(2)}, u32[]{:S(2)}) collective-permute-start(f32[8,128]{1,0:T(8,128)S(1)} %add.744), channel_id=1, source_target_pairs={{0,4},{1,3},{2,6},{3,1},{4,0},{5,7},{6,2},{7,5},{8,12},{9,11},{10,... | collective-permute-start | bytes 12296 | tf_op jit(solution)/shard_map/ppermute | solution.py:469
  464.7 29.6 %collective-permute-start.94 = (bf16[128,1536]{1,0:T(8,128)(2,1)S(1)}, bf16[128,1536]{1,0:T(8,128)(2,1)S(1)}, u32[]{:S(2)}, u32[]{:S(2)}) collective-permute-start(bf16[128,1536]{1,0:T(8,128)(2,1)S(1)} %collective-permute-done.90), channel_id=1, source_target_pairs={{0,4},{1,3},{2,6},{3,1},{4,0},{5,7},{6,2},{7,5},{8,12},{9,11},{10,... | collective-permute-start | bytes 1179656 | tf_op jit(solution)/shard_map/ppermute | solution.py:469
  503.1 47.4 %collective-permute-start.97 = (bf16[2,128,1536]{2,1,0:T(8,128)(2,1)}, bf16[2,128,1536]{2,1,0:T(8,128)(2,1)}, u32[]{:S(2)}, u32[]{:S(2)}) collective-permute-start(bf16[2,128,1536]{2,1,0:T(8,128)(2,1)} %fusion.14), channel_id=1, source_target_pairs={{0,4},{1,3},{2,6},{3,1},{4,0},{5,7},{6,2},{7,5},{8,12},{9,11},{10,... | collective-permute-start | bytes 2359304 | tf_op jit(solution)/shard_map/ppermute | solution.py:469
  508.5 63.1 %collective-permute-start.105 = (bf16[384,384]{1,0:T(8,128)(2,1)}, bf16[384,384]{1,0:T(8,128)(2,1)}, u32[]{:S(2)}, u32[]{:S(2)}) collective-permute-start(bf16[384,384]{1,0:T(8,128)(2,1)} %get-tuple-element.495), channel_id=1, source_target_pairs={{0,8},{8,16},{16,24},{24,0},{1,9},{9,17},{17,25},{25,1},{2,10},{10... | collective-permute-start | bytes 884744 | tf_op jit(solution)/shard_map/ppermute | solution.py:492
  510.7 60.9 %collective-permute-start.106 = (bf16[384,384]{1,0:T(8,128)(2,1)}, bf16[384,384]{1,0:T(8,128)(2,1)}, u32[]{:S(2)}, u32[]{:S(2)}) collective-permute-start(bf16[384,384]{1,0:T(8,128)(2,1)} %get-tuple-element.494), channel_id=1, source_target_pairs={{0,16},{8,24},{16,0},{24,8},{1,17},{9,25},{17,1},{25,9},{2,18},{10... | collective-permute-start | bytes 884744 | tf_op jit(solution)/shard_map/ppermute | solution.py:492
  510.7 60.9 %collective-permute-start.107 = (bf16[384,384]{1,0:T(8,128)(2,1)}, bf16[384,384]{1,0:T(8,128)(2,1)}, u32[]{:S(2)}, u32[]{:S(2)}) collective-permute-start(bf16[384,384]{1,0:T(8,128)(2,1)} %get-tuple-element.493), channel_id=1, source_target_pairs={{0,24},{8,0},{16,8},{24,16},{1,25},{9,1},{17,9},{25,17},{2,26},{10... | collective-permute-start | bytes 884744 | tf_op jit(solution)/shard_map/ppermute | solution.py:492
  (269 other events, 2622.2 us)
Sparse Core Ops, SparseCore 0:
  161.6 69.7 all-gather.1
  422.6 29.0 reduce-scatter.3
  455.8 76.7 reduce-scatter.5
  550.6 68.7 reduce-scatter.7

commit v5 on v4

--- a/solution.py
+++ b/solution.py
@@ -1148,8 +1148,8 @@
     "a ob1 b a",
     "q ia1 b xo",
     "a b ib1 r",
-    "a b oa0 a",
-    "b a a b",
+    "a b a b",
+    "a oa0 a b",
     "ob0 y ia0 b",
     "ib0 u a b",
     "a m b y",

time: 657 us -> 656 us (level)
    unnamed x372 -> x374, local copies, waits for them, and re-layouts: 52.3 us -> 55.3 us
  transfers between devices with their start and end apart: 131 -> 131, of which waited for: 28 -> 29; matrix products, arithmetic and copies ran while one was open for 42% -> 41% of each run, Pallas kernels for 17% -> 17%
where the time goes in v5:
time: 656 us; the launch traced here: 648 us
  starting transfers between devices  123 us (19%)
  matrix products  115 us (18%)
  local copies, waits for them, and re-layouts  114 us (17%)
  Pallas kernels  114 us (17%)
  waiting for transfers between devices  94.5 us (14%)
  other arithmetic  70.7 us (11%)
  between operations  17.2 us (3%)
    dot_general x32, matrix products, dot(): lax.dot_general(left, right, (((left_dim,), (right_dim,)), ((), ())), pre...  115 us
    pallas_call x4, Pallas kernels, mix_backward(): pl.pallas_call(lambda *refs: backward_kernel(head_size, inner_count, *ref...  76.7 us
    ppermute x59, waiting for transfers between devices, hop(): return lax.ppermute(value, GROUP, pairs)  63.9 us
    unnamed x374, local copies, waits for them, and re-layouts  55.3 us
    ppermute x59, starting transfers between devices, hop(): return lax.ppermute(value, GROUP, pairs)  46.4 us
    ppermute x31, starting transfers between devices, swap(): return lax.ppermute(value, 'tensor', [(0, 1), (1, 0)])  39.6 us
    pallas_call x4, Pallas kernels, mix_forward(): pl.pallas_call(lambda *refs: forward_kernel(head_size, *refs), grid_spec=...  33.6 us
    ppermute x18, starting transfers between devices, trade_steps(): lax.ppermute(value, 'seq', [(i, i ^ turn) for i in range(4)])  17.2 us
  transfers between devices with their start and end apart: 131, of which 29 were waited for; matrix products, arithmetic and copies ran while one was open for 41% of the time, Pallas kernels for 17%

profile of v5, /device:TPU:1, one launch (start us, length us, event | category | flops | bytes accessed | tf_op | source)
XLA Modules:
  0.0 648.3 jit_solution(5704792043688967401)
XLA Ops:
  51.7 7.7 %collective-permute-done.4 = bf16[384,768]{1,0:T(8,128)(2,1)} collective-permute-done((bf16[384,768]{1,0:T(8,128)(2,1)}, bf16[384,768]{1,0:T(8,128)(2,1)}, u32[]{:S(2)}, u32[]{:S(2)}) %collective-permute-start.4) | collective-permute-done | bytes 589856 | tf_op jit(solution)/shard_map/ppermute | solution.py:492
  88.5 8.3 %collective-permute-start.22 = (bf16[4,4,96,384]{3,2,1,0:T(8,128)(2,1)S(1)}, bf16[4,4,96,384]{3,2,1,0:T(8,128)(2,1)S(1)}, u32[]{:S(2)}, u32[]{:S(2)}) collective-permute-start(bf16[4,4,96,384]{3,2,1,0:T(8,128)(2,1)S(1)} %pad_maximum_fusion.9), channel_id=1, source_target_pairs={{0,1},{1,0},{2,3},{3,2},{4,5},{5,4},{6,7},{7,6},{8,9},{9,8},{10,11... | collective-permute-start | bytes 3538952 | tf_op jit(solution)/shard_map/ppermute | solution.py:473
  124.9 8.2 %collective-permute-done.23 = bf16[128,1536]{1,0:T(8,128)(2,1)} collective-permute-done((bf16[128,1536]{1,0:T(8,128)(2,1)S(1)}, bf16[128,1536]{1,0:T(8,128)(2,1)}, u32[]{:S(2)}, u32[]{:S(2)}) %collective-permute-start.23) | collective-permute-done | bytes 393248 | tf_op jit(solution)/shard_map/ppermute | solution.py:469
  135.1 8.3 %shard_map.263 = (bf16[1024,384]{1,0:T(8,128)(2,1)S(1)}, f32[64,128]{1,0:T(8,128)S(1)}, f32[1024,384]{1,0:T(8,128)S(1)}, f32[8,384,128]{2,1,0:T(8,128)S(1)}) custom-call(s32[8]{0:T(128)S(1)} %get-tuple-element.458.refs_0_, f32[1024,1152]{1,0:T(8,128)S(1)} %fusion.133.refs_1_.refs_2_.refs_3_.refs_4_.refs_5_, ...), custom_call_target="tpu_custom_call" | custom-call | flops 11000000512 | bytes 10000000 | tf_op jit(solution)/shard_map/pallas_call | solution.py:935
  152.3 5.9 fusion.134.refs_1_.refs_2_.refs_3_.refs_4_.refs_5_
  176.2 8.7 %shard_map.264 = (bf16[1024,384]{1,0:T(8,128)(2,1)S(1)}, f32[64,128]{1,0:T(8,128)S(1)}, f32[1024,384]{1,0:T(8,128)S(1)}, f32[8,384,128]{2,1,0:T(8,128)S(1)}) custom-call(s32[8]{0:T(128)S(1)} %get-tuple-element.458.refs_0_, f32[1024,1152]{1,0:T(8,128)S(1)} %bitcast.539, f32[1024,1152]{1,0:T(8,128)S(1)} %bitcast.539, ...), custom_call_target="tpu_custom_call" | custom-call | flops 11000000512 | bytes 10000000 | tf_op jit(solution)/shard_map/pallas_call | solution.py:935
  204.0 8.2 %collective-permute-done.49 = f32[8,128]{1,0:T(8,128)S(1)} collective-permute-done((f32[8,128]{1,0:T(8,128)S(1)}, f32[8,128]{1,0:T(8,128)S(1)}, u32[]{:S(2)}, u32[]{:S(2)}) %collective-permute-start.49) | collective-permute-done | bytes 4128 | tf_op jit(solution)/shard_map/ppermute | solution.py:469
  216.4 8.3 %collective-permute-done.46 = bf16[128,1536]{1,0:T(8,128)(2,1)S(1)} collective-permute-done((bf16[128,1536]{1,0:T(8,128)(2,1)S(1)}, bf16[128,1536]{1,0:T(8,128)(2,1)S(1)}, u32[]{:S(2)}, u32[]{:S(2)}) %collective-permute-start.46) | collective-permute-done | bytes 393248 | tf_op jit(solution)/shard_map/ppermute | solution.py:469
  241.6 8.4 %shard_map.265 = (bf16[1024,384]{1,0:T(8,128)(2,1)S(1)}, f32[64,128]{1,0:T(8,128)S(1)}, f32[1024,384]{1,0:T(8,128)S(1)}, f32[8,384,128]{2,1,0:T(8,128)S(1)}) custom-call(s32[8]{0:T(128)S(1)} %get-tuple-element.458.refs_0_, f32[1024,1152]{1,0:T(8,128)S(1)} %fusion.109.refs_1_.refs_2_.refs_3_.refs_4_.refs_5_, ...), custom_call_target="tpu_custom_call" | custom-call | flops 11000000512 | bytes 10000000 | tf_op jit(solution)/shard_map/pallas_call | solution.py:935
  266.8 8.3 %shard_map.266 = (bf16[1024,384]{1,0:T(8,128)(2,1)S(1)}, f32[64,128]{1,0:T(8,128)S(1)}, f32[1024,384]{1,0:T(8,128)S(1)}, f32[8,384,128]{2,1,0:T(8,128)S(1)}) custom-call(s32[8]{0:T(128)S(1)} %get-tuple-element.458.refs_0_, f32[1024,1152]{1,0:T(8,128)S(1)} %fusion.108.refs_1_.refs_2_.refs_3_.refs_4_.refs_5_, ...), custom_call_target="tpu_custom_call" | custom-call | flops 11000000512 | bytes 10000000 | tf_op jit(solution)/shard_map/pallas_call | solution.py:935
  291.5 5.3 fusion.59.refs_1_.refs_2_
  328.0 19.0 %shard_map.267 = (bf16[1024,1152]{1,0:T(8,128)(2,1)S(1)}, f32[8,640]{1,0:T(8,128)S(1)}, f32[8,384]{1,0:T(8,128)S(1)}, f32[16,128]{1,0:T(8,128)S(1)}) custom-call(s32[8]{0:T(128)S(1)} %get-tuple-element.458.refs_0_, f32[1024,384]{1,0:T(8,128)S(1)} %copy-done.5, f32[1024,384]{1,0:T(8,128)S(1)} %copy-done.5, f32[1024,1152]{1,0:T(8,128)S(1)} %copy-done.17, ...), custom_call_target="tpu_custom_call" | custom-call | flops 23000000512 | bytes 16000000 | tf_op jit(solution)/shard_map/pallas_call | solution.py:994
  363.9 19.5 %shard_map.268 = (bf16[1024,1152]{1,0:T(8,128)(2,1)S(1)}, f32[8,640]{1,0:T(8,128)S(1)}, f32[8,384]{1,0:T(8,128)S(1)}, f32[16,128]{1,0:T(8,128)S(1)}) custom-call(s32[8]{0:T(128)S(1)} %get-tuple-element.458.refs_0_, f32[1024,384]{1,0:T(8,128)S(1)} %copy-done.4, f32[1024,384]{1,0:T(8,128)S(1)} %copy-done.4, f32[1024,1152]{1,0:T(8,128)S(1)} %bitcast.543, ...), custom_call_target="tpu_custom_call" | custom-call | flops 23000000512 | bytes 16000000 | tf_op jit(solution)/shard_map/pallas_call | solution.py:994
  388.7 5.3 fusion.2
  403.5 5.2 fusion.10
  412.1 8.6 %convolution_convert_fusion.1 = bf16[1536,1152]{1,0:T(8,128)(2,1)} fusion(bf16[1024,1536]{1,0:T(8,128)(2,1)} %bitcast.618, bf16[1024,1152]{1,0:T(8,128)(2,1)S(1)} %copy-done.10), kind=kOutput, calls=%fused_computation.3 | convolution fusion | flops 3625648128 | bytes 9043968 | tf_op jit(solution)/shard_map/dot_general | solution.py:554
  432.4 5.8 collective-permute-start.92
  446.7 8.9 %fusion = bf16[1536,1152]{1,0:T(8,128)(2,1)} fusion(bf16[1024,1536]{1,0:T(8,128)(2,1)} %bitcast.620, bf16[1024,1152]{1,0:T(8,128)(2,1)S(1)} %copy-done.8, bf16[1536,1152]{1,0:T(8,128)(2,1)} %convolution_convert_fusion.1), kind=kOutput, calls=%fused_computation.4 | convolution fusion | flops 3629187072 | bytes 12582912 | tf_op jit(solution)/shard_map/dot_general | solution.py:554
  468.9 19.3 %shard_map.269 = (bf16[1024,1152]{1,0:T(8,128)(2,1)S(1)}, f32[8,640]{1,0:T(8,128)S(1)}, f32[8,384]{1,0:T(8,128)S(1)}, f32[16,128]{1,0:T(8,128)S(1)}) custom-call(s32[8]{0:T(128)S(1)} %get-tuple-element.458.refs_0_, f32[1024,384]{1,0:T(8,128)S(1)} %fusion.135.refs_1_.refs_2_, f32[1024,384]{1,0:T(8,128)S(1)} %fusion.135.refs_1_.refs_2_, ...), custom_call_target="tpu_custom_call" | custom-call | flops 23000000512 | bytes 16000000 | tf_op jit(solution)/shard_map/pallas_call | solution.py:994
  512.5 5.8 convolution_convert_fusion
  518.3 19.0 %shard_map.270 = (bf16[1024,1152]{1,0:T(8,128)(2,1)S(1)}, f32[8,640]{1,0:T(8,128)S(1)}, f32[8,384]{1,0:T(8,128)S(1)}, f32[16,128]{1,0:T(8,128)S(1)}) custom-call(s32[8]{0:T(128)S(1)} %get-tuple-element.458.refs_0_, f32[1024,384]{1,0:T(8,128)S(1)} %fusion.136.refs_1_.refs_2_, f32[1024,384]{1,0:T(8,128)S(1)} %fusion.136.refs_1_.refs_2_, ...), custom_call_target="tpu_custom_call" | custom-call | flops 23000000512 | bytes 16000000 | tf_op jit(solution)/shard_map/pallas_call | solution.py:994
  539.8 9.7 %fusion.1 = bf16[1536,1152]{1,0:T(8,128)(2,1)} fusion(bf16[1024,1536]{1,0:T(8,128)(2,1)} %bitcast.612, bf16[1024,1152]{1,0:T(8,128)(2,1)} %copy-done.11, bf16[1536,1152]{1,0:T(8,128)(2,1)} %convolution_convert_fusion), kind=kOutput, calls=%fused_computation.5 | convolution fusion | flops 3629187072 | bytes 12582912 | tf_op jit(solution)/shard_map/dot_general | solution.py:554
  578.7 5.6 collective-permute-done.103
  592.4 5.5 collective-permute-done.108
  (990 shorter events, 408.2 us)
Async XLA Ops:
  7.2 224.3 %all-gather.2.cloned.1.call-start = ((), (), s32[]{:S(2)}) async-start(), calls=%async_computation.3 | async-start | bytes 4423680 | tf_op jit(solution)/shard_map/all_gather | solution.py:1336
  10.5 26.4 %collective-permute-start.1 = (bf16[96,768]{1,0:T(8,128)(2,1)}, bf16[96,768]{1,0:T(8,128)(2,1)}, u32[]{:S(2)}, u32[]{:S(2)}) collective-permute-start(bf16[96,768]{1,0:T(8,128)(2,1)} %pad_maximum_fusion.12), channel_id=1, source_target_pairs={{0,2},{2,0},{4,6},{6,4},{1,3},{3,1},{5,7},{7,5},{8,10},{10,8},{12,... | collective-permute-start | bytes 442376 | tf_op jit(solution)/shard_map/ppermute | solution.py:1347
  13.3 27.6 %collective-permute-start.2 = (bf16[96,768]{1,0:T(8,128)(2,1)}, bf16[96,768]{1,0:T(8,128)(2,1)}, u32[]{:S(2)}, u32[]{:S(2)}) collective-permute-start(bf16[96,768]{1,0:T(8,128)(2,1)} %pad_maximum_fusion.13), channel_id=1, source_target_pairs={{0,4},{2,6},{4,0},{6,2},{1,5},{3,7},{5,1},{7,3},{8,12},{10,14},{12... | collective-permute-start | bytes 442376 | tf_op jit(solution)/shard_map/ppermute | solution.py:1347
  15.2 28.2 %collective-permute-start.3 = (bf16[96,768]{1,0:T(8,128)(2,1)}, bf16[96,768]{1,0:T(8,128)(2,1)}, u32[]{:S(2)}, u32[]{:S(2)}) collective-permute-start(bf16[96,768]{1,0:T(8,128)(2,1)} %pad_maximum_fusion.14), channel_id=1, source_target_pairs={{0,6},{2,4},{4,2},{6,0},{1,7},{3,5},{5,3},{7,1},{8,14},{10,12},{12... | collective-permute-start | bytes 442376 | tf_op jit(solution)/shard_map/ppermute | solution.py:1347
  15.9 29.6 %collective-permute-start.6 = (bf16[96,384]{1,0:T(8,128)(2,1)}, bf16[96,384]{1,0:T(8,128)(2,1)}, u32[]{:S(2)}, u32[]{:S(2)}) collective-permute-start(bf16[96,384]{1,0:T(8,128)(2,1)} %get-tuple-element.539), channel_id=1, source_target_pairs={{0,8},{8,16},{16,24},{24,0},{1,9},{9,17},{17,25},{25,1},{2,10},{10... | collective-permute-start | bytes 221192 | tf_op jit(solution)/shard_map/ppermute | solution.py:492
  21.6 29.7 %collective-permute-start = (bf16[128,1536]{1,0:T(8,128)(2,1)}, bf16[128,1536]{1,0:T(8,128)(2,1)}, u32[]{:S(2)}, u32[]{:S(2)}) collective-permute-start(bf16[128,1536]{1,0:T(8,128)(2,1)} %get-tuple-element.221), channel_id=1, source_target_pairs={{0,2},{1,5},{2,0},{3,7},{4,6},{5,1},{6,4},{7,3},{8,10},{9,13},{10,... | collective-permute-start | bytes 1179656 | tf_op jit(solution)/shard_map/ppermute | solution.py:469
  51.4 30.1 %collective-permute-start.14 = (bf16[128,1536]{1,0:T(8,128)(2,1)}, bf16[128,1536]{1,0:T(8,128)(2,1)}, u32[]{:S(2)}, u32[]{:S(2)}) collective-permute-start(bf16[128,1536]{1,0:T(8,128)(2,1)} %get-tuple-element.224), channel_id=1, source_target_pairs={{0,4},{1,3},{2,6},{3,1},{4,0},{5,7},{6,2},{7,5},{8,12},{9,11},{10,... | collective-permute-start | bytes 1179656 | tf_op jit(solution)/shard_map/ppermute | solution.py:469
  61.6 37.6 %collective-permute-start.20 = (bf16[384,768]{1,0:T(8,128)(2,1)}, bf16[384,768]{1,0:T(8,128)(2,1)}, u32[]{:S(2)}, u32[]{:S(2)}) collective-permute-start(bf16[384,768]{1,0:T(8,128)(2,1)} %bitcast.22), channel_id=1, source_target_pairs={{0,16},{8,24},{16,0},{24,8},{1,17},{9,25},{17,1},{25,9},{2,18},{10... | collective-permute-start | bytes 1769480 | tf_op jit(solution)/shard_map/ppermute | solution.py:492
  119.8 29.9 %collective-permute-start.31 = (bf16[4,128,1536]{2,1,0:T(8,128)(2,1)S(1)}, bf16[4,128,1536]{2,1,0:T(8,128)(2,1)S(1)}, u32[]{:S(2)}, u32[]{:S(2)}) collective-permute-start(bf16[4,128,1536]{2,1,0:T(8,128)(2,1)S(1)} %pad_maximum_fusion.2), channel_id=1, source_target_pairs={{0,1},{1,0},{2,3},{3,2},{4,5},{5,4},{6,7},{7,6},{8,9},{9,8},{10,11... | collective-permute-start | bytes 4718600 | tf_op jit(solution)/shard_map/ppermute | solution.py:473
  121.3 37.9 %collective-permute-start.30 = (bf16[128,1536]{1,0:T(8,128)(2,1)S(1)}, bf16[128,1536]{1,0:T(8,128)(2,1)S(1)}, u32[]{:S(2)}, u32[]{:S(2)}) collective-permute-start(bf16[128,1536]{1,0:T(8,128)(2,1)S(1)} %copy-done.44), channel_id=1, source_target_pairs={{0,4},{1,3},{2,6},{3,1},{4,0},{5,7},{6,2},{7,5},{8,12},{9,11},{10,... | collective-permute-start | bytes 1179656 | tf_op jit(solution)/shard_map/ppermute | solution.py:469
  161.5 412.6 %reduce-scatter.4.cloned.1.call-start = ((), (), s32[]{:S(2)}) async-start(), calls=%async_computation.4 | async-start | bytes 1474560 | tf_op jit(solution)/shard_map/reduce_scatter | solution.py:1552
  167.5 32.2 %collective-permute-start.73 = (bf16[4,128,1536]{2,1,0:T(8,128)(2,1)S(1)}, bf16[4,128,1536]{2,1,0:T(8,128)(2,1)S(1)}, u32[]{:S(2)}, u32[]{:S(2)}) collective-permute-start(bf16[4,128,1536]{2,1,0:T(8,128)(2,1)S(1)} %pad_maximum_fusion.3), channel_id=1, source_target_pairs={{0,1},{1,0},{2,3},{3,2},{4,5},{5,4},{6,7},{7,6},{8,9},{9,8},{10,11... | collective-permute-start | bytes 4718600 | tf_op jit(solution)/shard_map/ppermute | solution.py:473
  169.2 31.0 %collective-permute-start.72 = (bf16[4,128,1536]{2,1,0:T(8,128)(2,1)S(1)}, bf16[4,128,1536]{2,1,0:T(8,128)(2,1)S(1)}, u32[]{:S(2)}, u32[]{:S(2)}) collective-permute-start(bf16[4,128,1536]{2,1,0:T(8,128)(2,1)S(1)} %pad_maximum_fusion.4), channel_id=1, source_target_pairs={{0,1},{1,0},{2,3},{3,2},{4,5},{5,4},{6,7},{7,6},{8,9},{9,8},{10,11... | collective-permute-start | bytes 4718600 | tf_op jit(solution)/shard_map/ppermute | solution.py:473
  303.5 123.0 %collective-permute-start.62 = (f32[128,1536]{1,0:T(8,128)}, f32[128,1536]{1,0:T(8,128)}, u32[]{:S(2)}, u32[]{:S(2)}) collective-permute-start(f32[128,1536]{1,0:T(8,128)} %get-tuple-element.462), channel_id=1, source_target_pairs={{0,1},{1,0},{2,3},{3,2},{4,5},{5,4},{6,7},{7,6},{8,9},{9,8},{10,11... | collective-permute-start | bytes 2359304 | tf_op jit(solution)/shard_map/ppermute | solution.py:473
  357.6 69.6 %collective-permute-start.71 = (f32[128,1536]{1,0:T(8,128)}, f32[128,1536]{1,0:T(8,128)}, u32[]{:S(2)}, u32[]{:S(2)}) collective-permute-start(f32[128,1536]{1,0:T(8,128)} %get-tuple-element.460), channel_id=1, source_target_pairs={{0,1},{1,0},{2,3},{3,2},{4,5},{5,4},{6,7},{7,6},{8,9},{9,8},{10,11... | collective-permute-start | bytes 2359304 | tf_op jit(solution)/shard_map/ppermute | solution.py:473
  422.3 177.6 %reduce-scatter.6.cloned.1.call-start = ((), (), s32[]{:S(2)}) async-start(), calls=%async_computation.5 | async-start | bytes 4423680 | tf_op jit(solution)/shard_map/reduce_scatter | solution.py:1552
  446.3 42.0 %collective-permute-start.93 = (bf16[128,1536]{1,0:T(8,128)(2,1)}, bf16[128,1536]{1,0:T(8,128)(2,1)}, u32[]{:S(2)}, u32[]{:S(2)}) collective-permute-start(bf16[128,1536]{1,0:T(8,128)(2,1)} %copy-done.58), channel_id=1, source_target_pairs={{0,4},{1,3},{2,6},{3,1},{4,0},{5,7},{6,2},{7,5},{8,12},{9,11},{10,... | collective-permute-start | bytes 1179656 | tf_op jit(solution)/shard_map/ppermute | solution.py:469
  455.6 163.7 %reduce-scatter.8.cloned.1.call-start = ((), (), s32[]{:S(2)}) async-start(), calls=%async_computation.6 | async-start | bytes 4423680 | tf_op jit(solution)/shard_map/reduce_scatter | solution.py:1552
  462.2 27.3 %collective-permute-start.95 = (f32[8,128]{1,0:T(8,128)S(1)}, f32[8,128]{1,0:T(8,128)S(1)}, u32[]{:S(2)}, u32[]{:S(2)}) collective-permute-start(f32[8,128]{1,0:T(8,128)S(1)} %add.744), channel_id=1, source_target_pairs={{0,4},{1,3},{2,6},{3,1},{4,0},{5,7},{6,2},{7,5},{8,12},{9,11},{10,... | collective-permute-start | bytes 12296 | tf_op jit(solution)/shard_map/ppermute | solution.py:469
  463.4 28.7 %collective-permute-start.94 = (bf16[128,1536]{1,0:T(8,128)(2,1)S(1)}, bf16[128,1536]{1,0:T(8,128)(2,1)S(1)}, u32[]{:S(2)}, u32[]{:S(2)}) collective-permute-start(bf16[128,1536]{1,0:T(8,128)(2,1)S(1)} %collective-permute-done.90), channel_id=1, source_target_pairs={{0,4},{1,3},{2,6},{3,1},{4,0},{5,7},{6,2},{7,5},{8,12},{9,11},{10,... | collective-permute-start | bytes 1179656 | tf_op jit(solution)/shard_map/ppermute | solution.py:469
  502.7 46.9 %collective-permute-start.97 = (bf16[2,128,1536]{2,1,0:T(8,128)(2,1)}, bf16[2,128,1536]{2,1,0:T(8,128)(2,1)}, u32[]{:S(2)}, u32[]{:S(2)}) collective-permute-start(bf16[2,128,1536]{2,1,0:T(8,128)(2,1)} %fusion.14), channel_id=1, source_target_pairs={{0,4},{1,3},{2,6},{3,1},{4,0},{5,7},{6,2},{7,5},{8,12},{9,11},{10,... | collective-permute-start | bytes 2359304 | tf_op jit(solution)/shard_map/ppermute | solution.py:469
  508.4 62.3 %collective-permute-start.105 = (bf16[384,384]{1,0:T(8,128)(2,1)}, bf16[384,384]{1,0:T(8,128)(2,1)}, u32[]{:S(2)}, u32[]{:S(2)}) collective-permute-start(bf16[384,384]{1,0:T(8,128)(2,1)} %get-tuple-element.495), channel_id=1, source_target_pairs={{0,8},{8,16},{16,24},{24,0},{1,9},{9,17},{17,25},{25,1},{2,10},{10... | collective-permute-start | bytes 884744 | tf_op jit(solution)/shard_map/ppermute | solution.py:492
  510.3 60.5 %collective-permute-start.106 = (bf16[384,384]{1,0:T(8,128)(2,1)}, bf16[384,384]{1,0:T(8,128)(2,1)}, u32[]{:S(2)}, u32[]{:S(2)}) collective-permute-start(bf16[384,384]{1,0:T(8,128)(2,1)} %get-tuple-element.494), channel_id=1, source_target_pairs={{0,16},{8,24},{16,0},{24,8},{1,17},{9,25},{17,1},{25,9},{2,18},{10... | collective-permute-start | bytes 884744 | tf_op jit(solution)/shard_map/ppermute | solution.py:492
  510.3 60.5 %collective-permute-start.107 = (bf16[384,384]{1,0:T(8,128)(2,1)}, bf16[384,384]{1,0:T(8,128)(2,1)}, u32[]{:S(2)}, u32[]{:S(2)}) collective-permute-start(bf16[384,384]{1,0:T(8,128)(2,1)} %get-tuple-element.493), channel_id=1, source_target_pairs={{0,24},{8,0},{16,8},{24,16},{1,25},{9,1},{17,9},{25,17},{2,26},{10... | collective-permute-start | bytes 884744 | tf_op jit(solution)/shard_map/ppermute | solution.py:492
  (270 other events, 2607.7 us)
Sparse Core Ops, SparseCore 0:
  161.6 69.7 all-gather.1
  422.5 29.0 reduce-scatter.3
  455.7 76.6 reduce-scatter.5
  549.7 68.6 reduce-scatter.7
